TPU v7x, 256 devices: a whole 4x4x8 slice. The times are simulated.
256 devices in a mesh: gx: 8 (over x, z_hi), gy: 8 (over y, core), gz: 4 (over z_lo).
Axes of the slice: x: 4, y: 4, z: 8 (z_hi: 2, z_lo: 4; z = z_hi * 4 + z_lo), core: 2. Of those that a mesh axis runs over, the one named last changes fastest.
Arguments:
- adjoint_source: bfloat16 [32, 32, 8, 175, 128], P('gx', 'gy', 'gz'), may hold values from -6 to 6
- warm_start: bfloat16 [32, 32, 8, 175, 128], P('gx', 'gy', 'gz'), may hold values from -6 to 6
- block_inverse: bfloat16 [32, 32, 8, 175, 175], P('gx', 'gy', 'gz'), may hold values from -2 to 2
- face_jacobian: bfloat16 [32, 32, 8, 6, 75, 75], P('gx', 'gy', 'gz'), may hold values from -0.4375 to 0.4375
- trace_basis: bfloat16 [6, 175, 75], replicated, may hold values from -0.4375 to 0.4375
- orientation: int32 [32, 32, 8, 6, 15], P('gx', 'gy', 'gz'), may hold values from 0 to 14, each once within a row
Outputs:
- adjoint: bfloat16 [32, 32, 8, 175, 128], P('gx', 'gy', 'gz')
- shape_gradient: float32 [32, 32, 8, 6, 128], P('gx', 'gy', 'gz')
Inputs may be any that keep to these rules, and one draw needn't show every extreme that they name: `orientation`: every row of 15 entries is a permutation of 0 to 14.
All inputs are finite; a program needn't handle non-finite values.
Results may differ from a plain program's by a relative error of at most 0.011.
Values may be sent and summed in bfloat16 or wider, within the bound.
No kernel may reach another device: no remote copies, remote signals or barrier semaphores. Data moves between devices by JAX's collectives and lax.ppermute only.
A program may use at most 128 MiB of HBM per device.

v0:
```python
import jax
import jax.numpy as jnp
from jax import lax
from jax.experimental import pallas as pl
from jax.experimental.pallas import tpu as pltpu
from jax.sharding import PartitionSpec as P

SWEEPS = 2
PAIR = 76
PAD = 80
LANES = 128
BF = jnp.bfloat16
F32 = jnp.float32
PARAMS = pltpu.CompilerParams(vmem_limit_bytes=40 * 1024 * 1024)
VMEM = pl.BlockSpec(memory_space=pltpu.VMEM)


def mm(a, b):
    return jnp.dot(a, b, preferred_element_type=F32)


def mm_t(a, b):
    return lax.dot_general(a, b, (((1,), (1,)), ((), ())), preferred_element_type=F32)


def call(kernel, out_shape, operands, flops, scratch=()):
    moved = sum(a.size * a.dtype.itemsize for a in operands)
    return pl.pallas_call(
        kernel,
        out_shape=out_shape,
        in_specs=[VMEM] * len(operands),
        out_specs=jax.tree.map(lambda _: VMEM, out_shape),
        scratch_shapes=list(scratch),
        compiler_params=PARAMS,
        cost_estimate=pl.CostEstimate(flops=flops, bytes_accessed=moved, transcendentals=0),
    )(*operands)


class Block:
    def __init__(self, nx, ny, nz, c, r):
        self.nx, self.ny, self.nz, self.c, self.r = nx, ny, nz, c, r
        self.plane = ny * nz

    def send_shapes(self):
        rows = self.nz * PAIR
        x = jax.ShapeDtypeStruct((self.ny, rows, self.r), BF)
        y = jax.ShapeDtypeStruct((self.nx, rows, self.r), BF)
        z = jax.ShapeDtypeStruct((self.nx * self.ny // 2, 2 * PAIR, self.r), BF)
        return [x, x, y, y, z, z]

    def slot(self, face, x, y, z):
        if face < 2:
            return (y, pl.ds(z * PAIR, PAIR))
        if face < 4:
            return (x, pl.ds(z * PAIR, PAIR))
        return (x * (self.ny // 2) + y // 2, pl.ds((y % 2) * PAIR, PAIR))

    def halo_faces(self, x_side, y, z):
        faces = [] if x_side is None else [x_side]
        if y == 0:
            faces.append(2)
        if y == self.ny - 1:
            faces.append(3)
        if z == 0:
            faces.append(4)
        if z == self.nz - 1:
            faces.append(5)
        return faces

    def work(self, x, x_side):
        return [
            (x * self.plane + y * self.nz + z, y, z, self.halo_faces(x_side, y, z))
            for y in range(self.ny)
            for z in range(self.nz)
        ]

    def planes(self, visit):
        def inner(x, carry):
            visit(x, None)
            return carry

        lax.fori_loop(1, self.nx - 1, inner, 0)
        visit(0, 0)
        visit(self.nx - 1, 1)

    def near_local(self, face, x, y, z):
        dx, dy, dz = [(-1, 0, 0), (1, 0, 0), (0, -1, 0), (0, 1, 0), (0, 0, -1), (0, 0, 1)][face]
        return (x + 1 + dx) * self.plane + (y + dy) * self.nz + (z + dz), face ^ 1


def send_traces(block, x, work, values, bt, sends):
    traces = [
        mm(jnp.concatenate([bt[f] for f in faces], axis=0), a).astype(BF)
        for (_, _, _, faces), a in zip(work, values)
    ]
    for (_, y, z, faces), t in zip(work, traces):
        for i, f in enumerate(faces):
            sends[f][block.slot(f, x, y, z)] = t[i * PAD : i * PAD + PAIR]


def first_sends(block, a, bt):
    def kernel(a_ref, bt_ref, *sends):
        def visit(x, x_side):
            work = block.work(x, x_side)
            send_traces(block, x, work, [a_ref[w[0]] for w in work], bt_ref, sends)

        block.planes(visit)

    return call(kernel, block.send_shapes(), [a, bt], 64 * 80 * 175 * 256)


def permuted(jacobian, index):
    count = jacobian.shape[0]
    group = 6

    def kernel(j_ref, i_ref, jp_ref, p_ref):
        rows = lax.broadcasted_iota(jnp.int32, (PAD, PAD), 0)
        cols = lax.broadcasted_iota(jnp.int32, (PAD, PAD), 1)
        eye = (rows == cols).astype(BF)

        def element(e, carry):
            both = []
            for f in range(group):
                transposed = (rows == i_ref[e, f : f + 1, :]).astype(BF)
                both.append(mm_t(jnp.concatenate([j_ref[e, f], eye], axis=0), transposed).astype(BF))
            for f in range(group):
                jp_ref[e, f] = both[f][:PAD]
                p_ref[e, f] = both[f][PAD:]
            return carry

        lax.fori_loop(0, count, element, 0)

    shape = jax.ShapeDtypeStruct((count, group, PAD, PAD), BF)
    return call(kernel, [shape, shape], [jacobian, index], count * 6 * 160 * 80 * 160)


def fill_traces(block, a_ref, bt_ref, t_ref):
    nx, plane = block.nx, block.plane
    t_ref[0:plane, 1] = jnp.zeros((plane, PAD, block.r), BF)
    t_ref[(nx + 1) * plane : (nx + 2) * plane, 0] = jnp.zeros((plane, PAD, block.r), BF)
    every = bt_ref[...].reshape(6 * PAD, block.c)

    def traces(x, carry):
        t = [mm(every, a_ref[x * plane + i]).astype(BF) for i in range(plane)]
        for i in range(plane):
            for f in range(6):
                t_ref[(x + 1) * plane + i, f] = t[i][f * PAD : (f + 1) * PAD]
        return carry

    lax.fori_loop(0, nx, traces, 0)


def local_faces(block, y, z):
    return [f for f in range(6) if f < 2 or f not in block.halo_faces(None, y, z)]


def widened(pieces):
    gap = jnp.zeros((LANES - PAD, pieces[0].shape[1]), BF)
    return jnp.concatenate([part for p in pieces for part in (p, gap)], axis=0)


def coupled(bc_ref, faces, fluxes):
    return mm(jnp.concatenate([bc_ref[f] for f in faces], axis=1), widened(fluxes))


def local_residual(block, a, source, jp, bt, bc):
    def kernel(a_ref, s_ref, j_ref, bt_ref, bc_ref, r_ref, t_ref):
        fill_traces(block, a_ref, bt_ref, t_ref)

        def plane(x, carry):
            work = [(e, y, z, local_faces(block, y, z)) for e, y, z, _ in block.work(x, None)]
            fluxes = [
                [mm(j_ref[e, f], t_ref[block.near_local(f, x, y, z)]).astype(BF) for f in faces]
                for e, y, z, faces in work
            ]
            rest = [
                s_ref[w[0]].astype(F32) - coupled(bc_ref, w[3], flux) for w, flux in zip(work, fluxes)
            ]
            for w, value in zip(work, rest):
                r_ref[w[0]] = value
            return carry

        lax.fori_loop(0, block.nx, plane, 0)

    count = block.nx * block.plane
    return call(
        kernel,
        jax.ShapeDtypeStruct((count, block.c, block.r), F32),
        [a, source, jp, bt, bc],
        count * 175 * 480 * 128 * 4,
        [pltpu.VMEM(((block.nx + 2) * block.plane, 6, PAD, block.r), BF)],
    )


def finish_sweep(block, halos, residual, inverse, jp, bt, bc):
    def kernel(*refs):
        near, (r_ref, v_ref, j_ref, bt_ref, bc_ref, a_ref), sends = refs[:6], refs[6:12], refs[12:]

        def visit(x, x_side):
            work = block.work(x, x_side)
            fluxes = [
                [mm(j_ref[e, f, :, :PAIR], near[f][block.slot(f, x, y, z)]).astype(BF) for f in faces]
                for e, y, z, faces in work
            ]
            rest = [
                (r_ref[w[0]] - coupled(bc_ref, w[3], flux)).astype(BF) for w, flux in zip(work, fluxes)
            ]
            values = [mm(v_ref[w[0]], value).astype(BF) for w, value in zip(work, rest)]
            send_traces(block, x, work, values, bt_ref, sends)
            for w, value in zip(work, values):
                a_ref[w[0]] = value

        block.planes(visit)

    count = block.nx * block.plane
    out = [jax.ShapeDtypeStruct((count, block.c, block.r), BF)] + block.send_shapes()
    result = call(kernel, out, [*halos, residual, inverse, jp, bt, bc], count * 175 * 500 * 256)
    return result[0], result[1:]


def local_gradient(block, a, jp, p, bt):
    def kernel(a_ref, j_ref, p_ref, bt_ref, g_ref, t_ref):
        fill_traces(block, a_ref, bt_ref, t_ref)

        def plane(x, carry):
            grads = []
            for e, y, z, _ in block.work(x, None):
                rows = [jnp.zeros((1, block.r), F32)] * 8
                for f in local_faces(block, y, z):
                    both = jnp.concatenate([j_ref[e, f], p_ref[e, f]], axis=0)
                    both = mm(both, t_ref[block.near_local(f, x, y, z)])
                    own = t_ref[e + block.plane, f].astype(F32)
                    rows[f] = jnp.sum((own - both[PAD:]) * both[:PAD], axis=0, keepdims=True)
                grads.append((e, jnp.concatenate(rows, axis=0)))
            for e, value in grads:
                g_ref[e] = value
            return carry

        lax.fori_loop(0, block.nx, plane, 0)

    count = block.nx * block.plane
    return call(
        kernel,
        jax.ShapeDtypeStruct((count, 8, block.r), F32),
        [a, jp, p, bt],
        count * 480 * 300 * 256,
        [pltpu.VMEM(((block.nx + 2) * block.plane, 6, PAD, block.r), BF)],
    )


def finish_gradient(block, halos, owns, inside, jp, p):
    def kernel(*refs):
        near, own, (g_ref, j_ref, p_ref, out_ref) = refs[:6], refs[6:12], refs[12:]

        def visit(x, x_side):
            for y in range(block.ny):
                grads = []
                for z in range(block.nz):
                    e = x * block.plane + y * block.nz + z
                    faces = block.halo_faces(x_side, y, z)
                    rows = [jnp.zeros((1, block.r), F32)] * 8
                    for f in faces:
                        place = block.slot(f, x, y, z)
                        both = jnp.concatenate([j_ref[e, f, :, :PAIR], p_ref[e, f, :, :PAIR]], axis=0)
                        both = mm(both, near[f][place])
                        gap = own[f][place].astype(F32) - both[PAD : PAD + PAIR]
                        rows[f] = jnp.sum(gap * both[:PAIR], axis=0, keepdims=True)
                    grads.append(jnp.concatenate(rows, axis=0) + g_ref[e])
                for f in range(6):
                    out_ref[x * block.ny + y, f] = jnp.concatenate([g[f : f + 1] for g in grads], axis=0)

        block.planes(visit)

    shape = jax.ShapeDtypeStruct((block.nx * block.ny, 6, block.nz, block.r), F32)
    return call(kernel, shape, [*halos, *owns, inside, jp, p], 64 * 160 * 80 * 256)


def exchange(sends):
    halos = []
    for d, axis in enumerate(("gx", "gy", "gz")):
        count = lax.axis_size(axis)
        up = [(i, (i + 1) % count) for i in range(count)]
        if axis == "gz":
            up = up[:-1]
        down = [(j, i) for i, j in up]
        halos.append(lax.ppermute(sends[2 * d + 1], axis, up))
        halos.append(lax.ppermute(sends[2 * d], axis, down))
    return halos


def on_device(adjoint_source, warm_start, block_inverse, face_jacobian, trace_basis, orientation):
    nx, ny, nz, c, r = warm_start.shape
    count = nx * ny * nz
    width = trace_basis.shape[-1]
    modes = orientation.shape[-1]
    block = Block(nx, ny, nz, c, r)
    gap = PAD - width

    bt = jnp.pad(trace_basis.transpose(0, 2, 1), ((0, 0), (0, gap), (0, 0)))
    bc = jnp.pad(trace_basis, ((0, 0), (0, 0), (0, LANES - width)))
    adjoint = warm_start.reshape(count, c, r)
    sends = first_sends(block, adjoint, bt)

    source = adjoint_source.reshape(count, c, r)
    inverse = block_inverse.reshape(count, c, c)
    base = jnp.arange(width // modes, dtype=jnp.int32)[:, None] * modes
    index = (base + orientation[..., None, :]).reshape(count, 6, width)
    index = jnp.pad(index, ((0, 0), (0, 2), (0, gap)), constant_values=-1)
    jacobian = jnp.pad(face_jacobian.reshape(count, 6, width, width), ((0, 0), (0, 0), (0, gap), (0, gap)))
    jp, p = permuted(jacobian, index)

    for _ in range(SWEEPS):
        halos = exchange(sends)
        residual = local_residual(block, adjoint, source, jp, bt, bc)
        adjoint, sends = finish_sweep(block, halos, residual, inverse, jp, bt, bc)
    halos = exchange(sends)
    inside = local_gradient(block, adjoint, jp, p, bt)
    gradient = finish_gradient(block, halos, sends, inside, jp, p)
    gradient = gradient.reshape(nx, ny, 6, nz, r).transpose(0, 1, 3, 2, 4)
    return (adjoint.reshape(warm_start.shape), gradient)


def solution(mesh):
    return jax.shard_map(
        on_device,
        mesh=mesh,
        in_specs=(
            P("gx", "gy", "gz", None, None),
            P("gx", "gy", "gz", None, None),
            P("gx", "gy", "gz", None, None),
            P("gx", "gy", "gz", None, None, None),
            P(),
            P("gx", "gy", "gz", None, None),
        ),
        out_specs=(P("gx", "gy", "gz", None, None), P("gx", "gy", "gz", None, None)),
        check_vma=False,
    )
```

profile of v0, /device:TPU:44, one launch (start us, length us, event | category | flops | bytes accessed | tf_op | source)
XLA Modules:
  0.0 110.6 jit_solution(2288923039428927025)
XLA Ops:
  0.6 0.0 copy-start.13
  0.7 1.6 %copy.23 = bf16[4,4,2,175,128]{4,3,2,1,0:T(8,128)(2,1)S(1)} copy(bf16[4,4,2,175,128]{4,2,3,1,0:T(2,128)(2,1)} %param.7) | data formatting | bytes 2867200 | tf_op args[1]
  2.3 2.0 %shard_map.77 = (bf16[4,152,128]{2,1,0:T(8,128)(2,1)}, bf16[4,152,128]{2,1,0:T(8,128)(2,1)S(1)}, bf16[4,152,128]{2,1,0:T(8,128)(2,1)}, bf16[4,152,128]{2,1,0:T(8...) custom-call(bf16[32,175,128]{2,1,0:T(8,128)(2,1)S(1)} %bitcast.15, ...), custom_call_target="tpu_custom_call" | custom-call | flops 229376000 | bytes 1601600 | tf_op jit(solution)/shard_map/pallas_call | solution.py:28
  4.3 1.1 %copy-done.2 = bf16[4,4,2,175,128]{4,3,2,1,0:T(8,128)(2,1)} copy-done((bf16[4,4,2,175,128]{4,3,2,1,0:T(8,128)(2,1)}, bf16[4,4,2,175,128]{4,3,2,1,0:T(8,128)(2,1)S(1)}, u32[]{:S(2)}) %copy-start.2) | copy-done | bytes 1433624
  5.5 6.3 %collective-permute-start = (bf16[4,152,128]{2,1,0:T(8,128)(2,1)S(1)}, bf16[4,152,128]{2,1,0:T(8,128)(2,1)S(1)}, u32[]{:S(2)}, u32[]{:S(2)}) collective-permute-start(bf16[4,152,128]{2,1,0:T(8,128)(2,1)S(1)} %get-tuple-element.24), channel_id=1, source_target_pairs={{0,32},{32,64},{64,96},{96,128},{128,160},{160,192},{192,224},{224... | collective-permute-start | bytes 466952 | tf_op jit(solution)/shard_map/ppermute | solution.py:286
  11.8 0.5 collective-permute-start.1
  12.3 0.0 collective-permute-start.2
  12.3 3.8 %collective-permute-start.4 = (bf16[8,152,128]{2,1,0:T(8,128)(2,1)}, bf16[8,152,128]{2,1,0:T(8,128)(2,1)}, u32[]{:S(2)}, u32[]{:S(2)}) collective-permute-start(bf16[8,152,128]{2,1,0:T(8,128)(2,1)} %get-tuple-element.28), channel_id=1, source_target_pairs={{0,1},{1,2},{2,3},{4,5},{5,6},{6,7},{8,9},{9,10},{10,11},{12,13},{... | collective-permute-start | bytes 933896 | tf_op jit(solution)/shard_map/ppermute | solution.py:286
  16.1 2.7 %collective-permute-start.5 = (bf16[8,152,128]{2,1,0:T(8,128)(2,1)}, bf16[8,152,128]{2,1,0:T(8,128)(2,1)}, u32[]{:S(2)}, u32[]{:S(2)}) collective-permute-start(bf16[8,152,128]{2,1,0:T(8,128)(2,1)} %get-tuple-element.29), channel_id=1, source_target_pairs={{1,0},{2,1},{3,2},{5,4},{6,5},{7,6},{9,8},{10,9},{11,10},{13,12},{... | collective-permute-start | bytes 933896 | tf_op jit(solution)/shard_map/ppermute | solution.py:287
  18.9 0.2 copy.29
  19.1 0.1 add.28
  19.2 0.1 add.29
  19.3 0.8 pad.19.bc_ref.refs_10_
  20.1 0.1 add.31
  20.1 0.2 add.32
  20.3 0.0 copy-start.12
  20.3 1.7 %copy.24 = bf16[4,4,2,175,128]{4,3,2,1,0:T(8,128)(2,1)S(1)} copy(bf16[4,4,2,175,128]{4,2,3,1,0:T(2,128)(2,1)} %param.6) | data formatting | bytes 2867200 | tf_op args[0]
  22.0 0.5 copy-done.12
  22.6 0.5 copy.30
  23.1 2.1 %copy-done.11 = bf16[4,4,2,6,75,75]{5,2,4,3,1,0:T(2,128)(2,1)S(1)} copy-done((bf16[4,4,2,6,75,75]{5,2,4,3,1,0:T(2,128)(2,1)S(1)}, bf16[4,4,2,6,75,75]{5,2,4,3,1,0:T(2,128)(2,1)}, u32[]{:S(2)}) %copy-start.11) | copy-done | bytes 2160024
  25.1 0.8 copy.25
  25.9 0.8 pad.17.j_ref
  26.7 0.1 copy_add_fusion
  26.8 0.0 collective-permute-done.refs_0_
  26.9 1.2 %collective-permute-start.3 = (bf16[4,152,128]{2,1,0:T(8,128)(2,1)}, bf16[4,152,128]{2,1,0:T(8,128)(2,1)S(1)}, u32[]{:S(2)}, u32[]{:S(2)}) collective-permute-start(bf16[4,152,128]{2,1,0:T(8,128)(2,1)} %get-tuple-element.27), channel_id=1, source_target_pairs={{4,0},{8,4},{12,8},{16,12},{20,16},{24,20},{28,24},{0,28},{5,1},{9... | collective-permute-start | bytes 466952 | tf_op jit(solution)/shard_map/ppermute | solution.py:287
  28.1 7.0 %shard_map.78 = (bf16[32,6,80,80]{3,2,1,0:T(8,128)(2,1)S(1)}, bf16[32,6,80,80]{3,2,1,0:T(8,128)(2,1)S(1)}) custom-call(bf16[32,6,80,80]{3,2,1,0:T(8,128)(2,1)S(1)} %pad.17.j_ref, s32[32,8,80]{2,1,0:T(8,128)S(1)} %pad.18.i_ref), custom_call_target="tpu_custom_call" | custom-call | flops 393216000 | bytes 2539520 | tf_op jit(solution)/shard_map/pallas_call | solution.py:28
  35.1 6.8 %shard_map.79.refs_6_ = f32[32,175,128]{2,1,0:T(8,128)S(1)} custom-call(bf16[32,175,128]{2,1,0:T(8,128)(2,1)S(1)} %bitcast.16, bf16[32,175,128]{2,1,0:T(8,128)(2,1)S(1)} %bitcast.13, bf16[32,6,80,80]{3,2,1,0:T(8,128)(2,1)S(1)} %get-tuple-element.30.j_ref.refs_8_.refs_13_, bf16[6,80,175]{2,1,0:T(8,128)(2,1)S(1)} %copy-done.5, bf16[6,175,128]{2,1,0:T(8,128)(2,1)S(1)} %copy-done.9), custom_call_target="tpu_custom_call" | custom-call | flops 1376256000 | bytes 5761600 | tf_op jit(solution)/shard_map/pallas_call | solution.py:28
  42.0 1.6 %copy-done.7 = f32[32,175,128]{2,1,0:T(8,128)} copy-done((f32[32,175,128]{2,1,0:T(8,128)}, f32[32,175,128]{2,1,0:T(8,128)S(1)}, u32[]{:S(2)}) %copy-start.7) | copy-done | bytes 2867224
  43.5 0.0 collective-permute-done.1.refs_1_
  43.5 0.0 collective-permute-done.2.refs_2_
  43.5 0.0 collective-permute-done.3.refs_3_
  43.5 0.0 collective-permute-done.4.refs_4_
  43.5 0.0 collective-permute-done.5.refs_5_
  43.6 1.8 %copy-done.8 = f32[32,175,128]{2,1,0:T(8,128)S(1)} copy-done((f32[32,175,128]{2,1,0:T(8,128)S(1)}, f32[32,175,128]{2,1,0:T(8,128)}, u32[]{:S(2)}) %copy-start.8) | copy-done | bytes 2867224
  45.4 5.0 %shard_map.80 = (bf16[32,175,128]{2,1,0:T(8,128)(2,1)S(1)}, bf16[4,152,128]{2,1,0:T(8,128)(2,1)S(1)}, bf16[4,152,128]{2,1,0:T(8,128)(2,1)S(1)}, bf16[4,152,128]{...) custom-call(bf16[4,152,128]{2,1,0:T(8,128)(2,1)S(1)} %collective-per, ...), custom_call_target="tpu_custom_call" | custom-call | flops 716800000 | bytes 8966784 | tf_op jit(solution)/shard_map/pallas_call | solution.py:28
  50.3 5.5 %collective-permute-start.6 = (bf16[4,152,128]{2,1,0:T(8,128)(2,1)S(1)}, bf16[4,152,128]{2,1,0:T(8,128)(2,1)S(1)}, u32[]{:S(2)}, u32[]{:S(2)}) collective-permute-start(bf16[4,152,128]{2,1,0:T(8,128)(2,1)S(1)} %get-tuple-element.31), channel_id=1, source_target_pairs={{0,32},{32,64},{64,96},{96,128},{128,160},{160,192},{192,224},{224... | collective-permute-start | bytes 466952 | tf_op jit(solution)/shard_map/ppermute | solution.py:286
  55.8 2.2 %collective-permute-start.10 = (bf16[8,152,128]{2,1,0:T(8,128)(2,1)S(1)}, bf16[8,152,128]{2,1,0:T(8,128)(2,1)S(1)}, u32[]{:S(2)}, u32[]{:S(2)}) collective-permute-start(bf16[8,152,128]{2,1,0:T(8,128)(2,1)S(1)} %get-tuple-element.35), channel_id=1, source_target_pairs={{0,1},{1,2},{2,3},{4,5},{5,6},{6,7},{8,9},{9,10},{10,11},{12,13},{... | collective-permute-start | bytes 933896 | tf_op jit(solution)/shard_map/ppermute | solution.py:286
  58.1 3.6 %collective-permute-start.11 = (bf16[8,152,128]{2,1,0:T(8,128)(2,1)S(1)}, bf16[8,152,128]{2,1,0:T(8,128)(2,1)S(1)}, u32[]{:S(2)}, u32[]{:S(2)}) collective-permute-start(bf16[8,152,128]{2,1,0:T(8,128)(2,1)S(1)} %get-tuple-element.36), channel_id=1, source_target_pairs={{1,0},{2,1},{3,2},{5,4},{6,5},{7,6},{9,8},{10,9},{11,10},{13,12},{... | collective-permute-start | bytes 933896 | tf_op jit(solution)/shard_map/ppermute | solution.py:287
  61.7 1.7 %collective-permute-start.7 = (bf16[4,152,128]{2,1,0:T(8,128)(2,1)S(1)}, bf16[4,152,128]{2,1,0:T(8,128)(2,1)S(1)}, u32[]{:S(2)}, u32[]{:S(2)}) collective-permute-start(bf16[4,152,128]{2,1,0:T(8,128)(2,1)S(1)} %get-tuple-element.32), channel_id=1, source_target_pairs={{32,0},{64,32},{96,64},{128,96},{160,128},{192,160},{224,192},{0,2... | collective-permute-start | bytes 466952 | tf_op jit(solution)/shard_map/ppermute | solution.py:287
  63.4 0.0 collective-permute-start.8
  63.4 0.0 collective-permute-done.6.refs_0_
  63.4 1.7 %collective-permute-start.9 = (bf16[4,152,128]{2,1,0:T(8,128)(2,1)S(1)}, bf16[4,152,128]{2,1,0:T(8,128)(2,1)S(1)}, u32[]{:S(2)}, u32[]{:S(2)}) collective-permute-start(bf16[4,152,128]{2,1,0:T(8,128)(2,1)S(1)} %get-tuple-element.34), channel_id=1, source_target_pairs={{4,0},{8,4},{12,8},{16,12},{20,16},{24,20},{28,24},{0,28},{5,1},{9... | collective-permute-start | bytes 466952 | tf_op jit(solution)/shard_map/ppermute | solution.py:287
  65.1 6.8 %shard_map.81.refs_6_ = f32[32,175,128]{2,1,0:T(8,128)S(1)} custom-call(bf16[32,175,128]{2,1,0:T(8,128)(2,1)S(1)} %get-tuple-element.37.a_ref, bf16[32,175,128]{2,1,0:T(8,128)(2,1)S(1)} %bitcast.14, bf16[32,6,80,80]{3,2,1,0:T(8,128)(2,1)S(1)} %get-tuple-element.30.j_ref.refs_8_.refs_13_, bf16[6,80,175]{2,1,0:T(8,128)(2,1)S(1)} %copy-done.5, ...), custom_call_target="tpu_custom_call" | custom-call | flops 1376256000 | bytes 5761600 | tf_op jit(solution)/shard_map/pallas_call | solution.py:28
  72.0 4.4 %collective-permute-done.7.refs_1_ = bf16[4,152,128]{2,1,0:T(8,128)(2,1)S(1)} collective-permute-done((bf16[4,152,128]{2,1,0:T(8,128)(2,1)S(1)}, bf16[4,152,128]{2,1,0:T(8,128)(2,1)S(1)}, u32[]{:S(2)}, u32[]{:S(2)}) %collective-permute-start.7) | collective-permute-done | bytes 155680 | tf_op jit(solution)/shard_map/ppermute | solution.py:287
  76.4 0.0 collective-permute-done.8.refs_2_
  76.4 0.0 collective-permute-done.9.refs_3_
  76.4 0.0 collective-permute-done.10.refs_4_
  76.4 0.0 collective-permute-done.11.refs_5_
  76.4 3.7 %shard_map.82 = (bf16[32,175,128]{2,1,0:T(8,128)(2,1)S(1)}, bf16[4,152,128]{2,1,0:T(8,128)(2,1)S(1)}, bf16[4,152,128]{2,1,0:T(8,128)(2,1)S(1)}, bf16[4,152,128]{...) custom-call(bf16[4,152,128]{2,1,0:T(8,128)(2,1)S(1)} %collective-per, ...), custom_call_target="tpu_custom_call" | custom-call | flops 716800000 | bytes 8966784 | tf_op jit(solution)/shard_map/pallas_call | solution.py:28
  80.1 5.0 %collective-permute-start.12 = (bf16[4,152,128]{2,1,0:T(8,128)(2,1)S(1)}, bf16[4,152,128]{2,1,0:T(8,128)(2,1)S(1)}, u32[]{:S(2)}, u32[]{:S(2)}) collective-permute-start(bf16[4,152,128]{2,1,0:T(8,128)(2,1)S(1)} %get-tuple-element.39.refs_7_), channel_id=1, source_target_pairs={{0,32},{32,64},{64,96},{96,128},{128,160},{160,192},{192,224},{224... | collective-permute-start | bytes 466952 | tf_op jit(solution)/shard_map/ppermute | solution.py:286
  85.1 3.8 %collective-permute-start.16 = (bf16[8,152,128]{2,1,0:T(8,128)(2,1)S(1)}, bf16[8,152,128]{2,1,0:T(8,128)(2,1)S(1)}, u32[]{:S(2)}, u32[]{:S(2)}) collective-permute-start(bf16[8,152,128]{2,1,0:T(8,128)(2,1)S(1)} %get-tuple-element.43.refs_11_), channel_id=1, source_target_pairs={{0,1},{1,2},{2,3},{4,5},{5,6},{6,7},{8,9},{9,10},{10,11},{12,13},{... | collective-permute-start | bytes 933896 | tf_op jit(solution)/shard_map/ppermute | solution.py:286
  88.9 2.0 %collective-permute-start.17 = (bf16[8,152,128]{2,1,0:T(8,128)(2,1)S(1)}, bf16[8,152,128]{2,1,0:T(8,128)(2,1)S(1)}, u32[]{:S(2)}, u32[]{:S(2)}) collective-permute-start(bf16[8,152,128]{2,1,0:T(8,128)(2,1)S(1)} %get-tuple-element.44.refs_10_), channel_id=1, source_target_pairs={{1,0},{2,1},{3,2},{5,4},{6,5},{7,6},{9,8},{10,9},{11,10},{13,12},{... | collective-permute-start | bytes 933896 | tf_op jit(solution)/shard_map/ppermute | solution.py:287
  90.9 2.0 %collective-permute-start.13 = (bf16[4,152,128]{2,1,0:T(8,128)(2,1)S(1)}, bf16[4,152,128]{2,1,0:T(8,128)(2,1)S(1)}, u32[]{:S(2)}, u32[]{:S(2)}) collective-permute-start(bf16[4,152,128]{2,1,0:T(8,128)(2,1)S(1)} %get-tuple-element.40.refs_6_), channel_id=1, source_target_pairs={{32,0},{64,32},{96,64},{128,96},{160,128},{192,160},{224,192},{0,2... | collective-permute-start | bytes 466952 | tf_op jit(solution)/shard_map/ppermute | solution.py:287
  92.9 0.0 collective-permute-start.14
  92.9 0.0 collective-permute-done.12.refs_0_
  92.9 1.7 %collective-permute-start.15 = (bf16[4,152,128]{2,1,0:T(8,128)(2,1)S(1)}, bf16[4,152,128]{2,1,0:T(8,128)(2,1)S(1)}, u32[]{:S(2)}, u32[]{:S(2)}) collective-permute-start(bf16[4,152,128]{2,1,0:T(8,128)(2,1)S(1)} %get-tuple-element.42.refs_8_), channel_id=1, source_target_pairs={{4,0},{8,4},{12,8},{16,12},{20,16},{24,20},{28,24},{0,28},{5,1},{9... | collective-permute-start | bytes 466952 | tf_op jit(solution)/shard_map/ppermute | solution.py:287
  94.7 2.2 %copy.31 = bf16[4,4,2,175,128]{4,2,3,1,0:T(2,128)(2,1)} copy(bf16[4,4,2,175,128]{4,3,2,1,0:T(8,128)(2,1)S(1)} %bitcast.17) | data formatting | bytes 2867200
  96.9 5.0 %shard_map.83.refs_12_ = f32[32,8,128]{2,1,0:T(8,128)S(1)} custom-call(bf16[32,175,128]{2,1,0:T(8,128)(2,1)S(1)} %get-tuple-element.38.a_ref, bf16[32,6,80,80]{3,2,1,0:T(8,128)(2,1)S(1)} %get-tuple-element.30.j_ref.refs_8_.refs_13_, bf16[32,6,80,80]{3,2,1,0:T(8,128)(2,1)S(1)} %get-tuple-element.45.p_ref.refs_14_, bf16[6,80,175]{2,1,0:T(8,128)(2,1)S(1)} %copy-done.6), custom_call_target="tpu_custom_call" | custom-call | flops 1179648000 | bytes 6516800 | tf_op jit(solution)/shard_map/pallas_call | solution.py:28
  101.9 6.8 %collective-permute-done.13.refs_1_ = bf16[4,152,128]{2,1,0:T(8,128)(2,1)S(1)} collective-permute-done((bf16[4,152,128]{2,1,0:T(8,128)(2,1)S(1)}, bf16[4,152,128]{2,1,0:T(8,128)(2,1)S(1)}, u32[]{:S(2)}, u32[]{:S(2)}) %collective-permute-start.13) | collective-permute-done | bytes 155680 | tf_op jit(solution)/shard_map/ppermute | solution.py:287
  108.7 0.0 collective-permute-done.14.refs_2_
  108.7 0.0 collective-permute-done.15.refs_3_
  108.7 0.0 collective-permute-done.16.refs_4_
  108.7 0.0 collective-permute-done.17.refs_5_
  108.7 1.9 %shard_map.84 = f32[16,6,2,128]{3,2,1,0:T(2,128)} custom-call(bf16[4,152,128]{2,1,0:T(8,128)(2,1)S(1)} %collective-permute-done.12.refs_0_, bf16[4,152,128]{2,1,0:T(8,128)(2,1)S(1)} %collective-permute-done.13.refs_1_, bf16[4,152,128]{2,1,0:T(8,128)(2,1)S(1)} %collective-permute-done.14.refs_2_, bf16[4,152,128]{2,1,0:T(8,128)(2,1)S(1)} %collective-permute-done.15.refs_3_, ...), custom_call_target="tpu_custom_call" | custom-call | flops 209715200 | bytes 7536640 | tf_op jit(solution)/shard_map/pallas_call | solution.py:28
  (27 shorter events, 0.1 us)
Async XLA Ops:
  0.6 1.6 %copy-start.13 = (bf16[6,175,75]{1,2,0:T(8,128)(2,1)S(1)}, bf16[6,175,75]{1,2,0:T(8,128)(2,1)}, u32[]{:S(2)}) copy-start(bf16[6,175,75]{1,2,0:T(8,128)(2,1)} %param.10) | copy-start | bytes 472504
  0.6 18.6 %copy-start.14 = (s32[4,4,2,6,15]{4,2,3,1,0:T(2,128)S(1)}, s32[4,4,2,6,15]{4,2,3,1,0:T(2,128)}, u32[]{:S(2)}) copy-start(s32[4,4,2,6,15]{4,2,3,1,0:T(2,128)} %param.11) | copy-start | bytes 34564
  2.3 2.0 %copy-start.4 = (bf16[6,80,175]{2,1,0:T(8,128)(2,1)}, bf16[6,80,175]{2,1,0:T(8,128)(2,1)S(1)}, u32[]{:S(2)}) copy-start(bf16[6,80,175]{2,1,0:T(8,128)(2,1)S(1)} %pad.16.bt_ref.refs_9_) | copy-start | bytes 504004
  4.3 1.1 %copy-start.2 = (bf16[4,4,2,175,128]{4,3,2,1,0:T(8,128)(2,1)}, bf16[4,4,2,175,128]{4,3,2,1,0:T(8,128)(2,1)S(1)}, u32[]{:S(2)}) copy-start(bf16[4,4,2,175,128]{4,3,2,1,0:T(8,128)(2,1)S(1)} %copy.23) | copy-start | bytes 4300804
  5.5 21.4 %collective-permute-start = (bf16[4,152,128]{2,1,0:T(8,128)(2,1)S(1)}, bf16[4,152,128]{2,1,0:T(8,128)(2,1)S(1)}, u32[]{:S(2)}, u32[]{:S(2)}) collective-permute-start(bf16[4,152,128]{2,1,0:T(8,128)(2,1)S(1)} %get-tuple-element.24), channel_id=1, source_target_pairs={{0,32},{32,64},{64,96},{96,128},{128,160},{160,192},{192,224},{224... | collective-permute-start | bytes 466952 | tf_op jit(solution)/shard_map/ppermute | solution.py:286
  11.8 31.8 %collective-permute-start.1 = (bf16[4,152,128]{2,1,0:T(8,128)(2,1)}, bf16[4,152,128]{2,1,0:T(8,128)(2,1)}, u32[]{:S(2)}, u32[]{:S(2)}) collective-permute-start(bf16[4,152,128]{2,1,0:T(8,128)(2,1)} %get-tuple-element.25), channel_id=1, source_target_pairs={{32,0},{64,32},{96,64},{128,96},{160,128},{192,160},{224,192},{0,2... | collective-permute-start | bytes 466952 | tf_op jit(solution)/shard_map/ppermute | solution.py:287
  12.3 31.2 %collective-permute-start.2 = (bf16[4,152,128]{2,1,0:T(8,128)(2,1)}, bf16[4,152,128]{2,1,0:T(8,128)(2,1)}, u32[]{:S(2)}, u32[]{:S(2)}) collective-permute-start(bf16[4,152,128]{2,1,0:T(8,128)(2,1)} %get-tuple-element.26), channel_id=1, source_target_pairs={{0,4},{4,8},{8,12},{12,16},{16,20},{20,24},{24,28},{28,0},{1,5},{5... | collective-permute-start | bytes 466952 | tf_op jit(solution)/shard_map/ppermute | solution.py:286
  12.3 31.2 %collective-permute-start.4 = (bf16[8,152,128]{2,1,0:T(8,128)(2,1)}, bf16[8,152,128]{2,1,0:T(8,128)(2,1)}, u32[]{:S(2)}, u32[]{:S(2)}) collective-permute-start(bf16[8,152,128]{2,1,0:T(8,128)(2,1)} %get-tuple-element.28), channel_id=1, source_target_pairs={{0,1},{1,2},{2,3},{4,5},{5,6},{6,7},{8,9},{9,10},{10,11},{12,13},{... | collective-permute-start | bytes 933896 | tf_op jit(solution)/shard_map/ppermute | solution.py:286
  16.1 27.4 %collective-permute-start.5 = (bf16[8,152,128]{2,1,0:T(8,128)(2,1)}, bf16[8,152,128]{2,1,0:T(8,128)(2,1)}, u32[]{:S(2)}, u32[]{:S(2)}) collective-permute-start(bf16[8,152,128]{2,1,0:T(8,128)(2,1)} %get-tuple-element.29), channel_id=1, source_target_pairs={{1,0},{2,1},{3,2},{5,4},{6,5},{7,6},{9,8},{10,9},{11,10},{13,12},{... | collective-permute-start | bytes 933896 | tf_op jit(solution)/shard_map/ppermute | solution.py:287
  20.3 2.2 %copy-start.12 = (bf16[4,4,2,175,175]{4,2,3,1,0:T(2,128)(2,1)S(1)}, bf16[4,4,2,175,175]{4,2,3,1,0:T(2,128)(2,1)}, u32[]{:S(2)}) copy-start(bf16[4,4,2,175,175]{4,2,3,1,0:T(2,128)(2,1)} %param.8) | copy-start | bytes 5880004
  22.6 12.5 %copy-start = (bf16[4,4,2,175,128]{4,3,2,1,0:T(8,128)(2,1)}, bf16[4,4,2,175,128]{4,3,2,1,0:T(8,128)(2,1)S(1)}, u32[]{:S(2)}) copy-start(bf16[4,4,2,175,128]{4,3,2,1,0:T(8,128)(2,1)S(1)} %copy.24) | copy-start | bytes 4300804
  22.6 2.6 %copy-start.11 = (bf16[4,4,2,6,75,75]{5,2,4,3,1,0:T(2,128)(2,1)S(1)}, bf16[4,4,2,6,75,75]{5,2,4,3,1,0:T(2,128)(2,1)}, u32[]{:S(2)}) copy-start(bf16[4,4,2,6,75,75]{5,2,4,3,1,0:T(2,128)(2,1)} %param.9) | copy-start | bytes 6480004
  26.7 8.4 %copy-start.3 = (bf16[4,4,2,175,128]{4,3,2,1,0:T(8,128)(2,1)S(1)}, bf16[4,4,2,175,128]{4,3,2,1,0:T(8,128)(2,1)}, u32[]{:S(2)}) copy-start(bf16[4,4,2,175,128]{4,3,2,1,0:T(8,128)(2,1)} %copy-done.2) | copy-start | bytes 4300804
  26.7 8.4 %copy-start.5 = (bf16[6,80,175]{2,1,0:T(8,128)(2,1)S(1)}, bf16[6,80,175]{2,1,0:T(8,128)(2,1)}, u32[]{:S(2)}) copy-start(bf16[6,80,175]{2,1,0:T(8,128)(2,1)} %copy-done.4) | copy-start | bytes 504004
  26.7 8.4 %copy-start.9 = (bf16[6,175,128]{2,1,0:T(8,128)(2,1)S(1)}, bf16[6,175,128]{2,1,0:T(8,128)(2,1)}, u32[]{:S(2)}) copy-start(bf16[6,175,128]{2,1,0:T(8,128)(2,1)} %pad.19.bc_ref.refs_10_) | copy-start | bytes 806404
  26.9 16.7 %collective-permute-start.3 = (bf16[4,152,128]{2,1,0:T(8,128)(2,1)}, bf16[4,152,128]{2,1,0:T(8,128)(2,1)S(1)}, u32[]{:S(2)}, u32[]{:S(2)}) collective-permute-start(bf16[4,152,128]{2,1,0:T(8,128)(2,1)} %get-tuple-element.27), channel_id=1, source_target_pairs={{4,0},{8,4},{12,8},{16,12},{20,16},{24,20},{28,24},{0,28},{5,1},{9... | collective-permute-start | bytes 466952 | tf_op jit(solution)/shard_map/ppermute | solution.py:287
  41.9 1.6 %copy-start.7 = (f32[32,175,128]{2,1,0:T(8,128)}, f32[32,175,128]{2,1,0:T(8,128)S(1)}, u32[]{:S(2)}) copy-start(f32[32,175,128]{2,1,0:T(8,128)S(1)} %shard_map.79.refs_6_) | copy-start | bytes 8601604
  43.6 1.8 %copy-start.8 = (f32[32,175,128]{2,1,0:T(8,128)S(1)}, f32[32,175,128]{2,1,0:T(8,128)}, u32[]{:S(2)}) copy-start(f32[32,175,128]{2,1,0:T(8,128)} %copy-done.7) | copy-start | bytes 8601604
  45.4 19.7 %copy-start.1 = (bf16[4,4,2,175,128]{4,3,2,1,0:T(8,128)(2,1)S(1)}, bf16[4,4,2,175,128]{4,3,2,1,0:T(8,128)(2,1)}, u32[]{:S(2)}) copy-start(bf16[4,4,2,175,128]{4,3,2,1,0:T(8,128)(2,1)} %copy-done) | copy-start | bytes 4300804
  50.3 13.0 %collective-permute-start.6 = (bf16[4,152,128]{2,1,0:T(8,128)(2,1)S(1)}, bf16[4,152,128]{2,1,0:T(8,128)(2,1)S(1)}, u32[]{:S(2)}, u32[]{:S(2)}) collective-permute-start(bf16[4,152,128]{2,1,0:T(8,128)(2,1)S(1)} %get-tuple-element.31), channel_id=1, source_target_pairs={{0,32},{32,64},{64,96},{96,128},{128,160},{160,192},{192,224},{224... | collective-permute-start | bytes 466952 | tf_op jit(solution)/shard_map/ppermute | solution.py:286
  55.8 20.5 %collective-permute-start.10 = (bf16[8,152,128]{2,1,0:T(8,128)(2,1)S(1)}, bf16[8,152,128]{2,1,0:T(8,128)(2,1)S(1)}, u32[]{:S(2)}, u32[]{:S(2)}) collective-permute-start(bf16[8,152,128]{2,1,0:T(8,128)(2,1)S(1)} %get-tuple-element.35), channel_id=1, source_target_pairs={{0,1},{1,2},{2,3},{4,5},{5,6},{6,7},{8,9},{9,10},{10,11},{12,13},{... | collective-permute-start | bytes 933896 | tf_op jit(solution)/shard_map/ppermute | solution.py:286
  58.1 18.3 %collective-permute-start.11 = (bf16[8,152,128]{2,1,0:T(8,128)(2,1)S(1)}, bf16[8,152,128]{2,1,0:T(8,128)(2,1)S(1)}, u32[]{:S(2)}, u32[]{:S(2)}) collective-permute-start(bf16[8,152,128]{2,1,0:T(8,128)(2,1)S(1)} %get-tuple-element.36), channel_id=1, source_target_pairs={{1,0},{2,1},{3,2},{5,4},{6,5},{7,6},{9,8},{10,9},{11,10},{13,12},{... | collective-permute-start | bytes 933896 | tf_op jit(solution)/shard_map/ppermute | solution.py:287
  61.7 14.7 %collective-permute-start.7 = (bf16[4,152,128]{2,1,0:T(8,128)(2,1)S(1)}, bf16[4,152,128]{2,1,0:T(8,128)(2,1)S(1)}, u32[]{:S(2)}, u32[]{:S(2)}) collective-permute-start(bf16[4,152,128]{2,1,0:T(8,128)(2,1)S(1)} %get-tuple-element.32), channel_id=1, source_target_pairs={{32,0},{64,32},{96,64},{128,96},{160,128},{192,160},{224,192},{0,2... | collective-permute-start | bytes 466952 | tf_op jit(solution)/shard_map/ppermute | solution.py:287
  63.4 13.0 %collective-permute-start.8 = (bf16[4,152,128]{2,1,0:T(8,128)(2,1)S(1)}, bf16[4,152,128]{2,1,0:T(8,128)(2,1)S(1)}, u32[]{:S(2)}, u32[]{:S(2)}) collective-permute-start(bf16[4,152,128]{2,1,0:T(8,128)(2,1)S(1)} %get-tuple-element.33), channel_id=1, source_target_pairs={{0,4},{4,8},{8,12},{12,16},{16,20},{20,24},{24,28},{28,0},{1,5},{5... | collective-permute-start | bytes 466952 | tf_op jit(solution)/shard_map/ppermute | solution.py:286
  63.4 13.0 %collective-permute-start.9 = (bf16[4,152,128]{2,1,0:T(8,128)(2,1)S(1)}, bf16[4,152,128]{2,1,0:T(8,128)(2,1)S(1)}, u32[]{:S(2)}, u32[]{:S(2)}) collective-permute-start(bf16[4,152,128]{2,1,0:T(8,128)(2,1)S(1)} %get-tuple-element.34), channel_id=1, source_target_pairs={{4,0},{8,4},{12,8},{16,12},{20,16},{24,20},{28,24},{0,28},{5,1},{9... | collective-permute-start | bytes 466952 | tf_op jit(solution)/shard_map/ppermute | solution.py:287
  65.1 11.3 %copy-start.6 = (bf16[6,80,175]{2,1,0:T(8,128)(2,1)S(1)}, bf16[6,80,175]{2,1,0:T(8,128)(2,1)}, u32[]{:S(2)}) copy-start(bf16[6,80,175]{2,1,0:T(8,128)(2,1)} %copy-done.4) | copy-start | bytes 504004
  65.1 11.3 %copy-start.10 = (bf16[6,175,128]{2,1,0:T(8,128)(2,1)S(1)}, bf16[6,175,128]{2,1,0:T(8,128)(2,1)}, u32[]{:S(2)}) copy-start(bf16[6,175,128]{2,1,0:T(8,128)(2,1)} %pad.19.bc_ref.refs_10_) | copy-start | bytes 806404
  80.1 12.9 %collective-permute-start.12 = (bf16[4,152,128]{2,1,0:T(8,128)(2,1)S(1)}, bf16[4,152,128]{2,1,0:T(8,128)(2,1)S(1)}, u32[]{:S(2)}, u32[]{:S(2)}) collective-permute-start(bf16[4,152,128]{2,1,0:T(8,128)(2,1)S(1)} %get-tuple-element.39.refs_7_), channel_id=1, source_target_pairs={{0,32},{32,64},{64,96},{96,128},{128,160},{160,192},{192,224},{224... | collective-permute-start | bytes 466952 | tf_op jit(solution)/shard_map/ppermute | solution.py:286
  85.1 23.6 %collective-permute-start.16 = (bf16[8,152,128]{2,1,0:T(8,128)(2,1)S(1)}, bf16[8,152,128]{2,1,0:T(8,128)(2,1)S(1)}, u32[]{:S(2)}, u32[]{:S(2)}) collective-permute-start(bf16[8,152,128]{2,1,0:T(8,128)(2,1)S(1)} %get-tuple-element.43.refs_11_), channel_id=1, source_target_pairs={{0,1},{1,2},{2,3},{4,5},{5,6},{6,7},{8,9},{9,10},{10,11},{12,13},{... | collective-permute-start | bytes 933896 | tf_op jit(solution)/shard_map/ppermute | solution.py:286
  88.9 19.7 %collective-permute-start.17 = (bf16[8,152,128]{2,1,0:T(8,128)(2,1)S(1)}, bf16[8,152,128]{2,1,0:T(8,128)(2,1)S(1)}, u32[]{:S(2)}, u32[]{:S(2)}) collective-permute-start(bf16[8,152,128]{2,1,0:T(8,128)(2,1)S(1)} %get-tuple-element.44.refs_10_), channel_id=1, source_target_pairs={{1,0},{2,1},{3,2},{5,4},{6,5},{7,6},{9,8},{10,9},{11,10},{13,12},{... | collective-permute-start | bytes 933896 | tf_op jit(solution)/shard_map/ppermute | solution.py:287
  90.9 17.7 %collective-permute-start.13 = (bf16[4,152,128]{2,1,0:T(8,128)(2,1)S(1)}, bf16[4,152,128]{2,1,0:T(8,128)(2,1)S(1)}, u32[]{:S(2)}, u32[]{:S(2)}) collective-permute-start(bf16[4,152,128]{2,1,0:T(8,128)(2,1)S(1)} %get-tuple-element.40.refs_6_), channel_id=1, source_target_pairs={{32,0},{64,32},{96,64},{128,96},{160,128},{192,160},{224,192},{0,2... | collective-permute-start | bytes 466952 | tf_op jit(solution)/shard_map/ppermute | solution.py:287
  92.9 15.7 %collective-permute-start.14 = (bf16[4,152,128]{2,1,0:T(8,128)(2,1)S(1)}, bf16[4,152,128]{2,1,0:T(8,128)(2,1)S(1)}, u32[]{:S(2)}, u32[]{:S(2)}) collective-permute-start(bf16[4,152,128]{2,1,0:T(8,128)(2,1)S(1)} %get-tuple-element.41.refs_9_), channel_id=1, source_target_pairs={{0,4},{4,8},{8,12},{12,16},{16,20},{20,24},{24,28},{28,0},{1,5},{5... | collective-permute-start | bytes 466952 | tf_op jit(solution)/shard_map/ppermute | solution.py:286
  92.9 15.7 %collective-permute-start.15 = (bf16[4,152,128]{2,1,0:T(8,128)(2,1)S(1)}, bf16[4,152,128]{2,1,0:T(8,128)(2,1)S(1)}, u32[]{:S(2)}, u32[]{:S(2)}) collective-permute-start(bf16[4,152,128]{2,1,0:T(8,128)(2,1)S(1)} %get-tuple-element.42.refs_8_), channel_id=1, source_target_pairs={{4,0},{8,4},{12,8},{16,12},{20,16},{24,20},{28,24},{0,28},{5,1},{9... | collective-permute-start | bytes 466952 | tf_op jit(solution)/shard_map/ppermute | solution.py:287
where the time goes:
time: 111 us
  starting transfers between devices  43.9 us (40%)
  Pallas kernels  38.2 us (34%)
  local copies, waits for them, and re-layouts  16.2 us (15%)
  waiting for transfers between devices  11.2 us (10%)
    pallas_call x8, Pallas kernels, call(): pl.pallas_call(kernel, out_shape=out_shape, in_specs=[VMEM] * len(operand...  38.2 us
    ppermute x9, starting transfers between devices, exchange(): halos.append(lax.ppermute(sends[2 * d + 1], axis, up))  26.7 us
    ppermute x9, starting transfers between devices, exchange(): halos.append(lax.ppermute(sends[2 * d], axis, down))  17.2 us
    unnamed x37, local copies, waits for them, and re-layouts  14.2 us
    ppermute x9, waiting for transfers between devices, exchange(): halos.append(lax.ppermute(sends[2 * d], axis, down))  11.2 us
  transfers between devices with their start and end apart: 18, of which 2 were waited for; matrix products, arithmetic and copies ran while one was open for 7% of the time, Pallas kernels for 23%

commit v1 on v0

v1 whole, which is shorter than its diff:
```python
import jax
import jax.numpy as jnp
from jax import lax
from jax.experimental import pallas as pl
from jax.experimental.pallas import tpu as pltpu
from jax.sharding import PartitionSpec as P

SWEEPS = 2
VARS = 5
FIRST = 1000
SECOND = 1000
LOCAL = 1000
PREP = 1000
WAIT = 2500000000
PAIR = 76
PAD = 80
LANES = 128
BF = jnp.bfloat16
F32 = jnp.float32
PARAMS = pltpu.CompilerParams(vmem_limit_bytes=20 * 1024 * 1024)
VMEM = pl.BlockSpec(memory_space=pltpu.VMEM)


def mm(a, b):
    return jnp.dot(a, b, preferred_element_type=F32)


def mm_t(a, b):
    return lax.dot_general(a, b, (((1,), (1,)), ((), ())), preferred_element_type=F32)


def call(kernel, out_shape, operands, flops, scratch=()):
    return pl.pallas_call(
        kernel,
        out_shape=out_shape,
        in_specs=[VMEM] * len(operands),
        out_specs=jax.tree.map(lambda _: VMEM, out_shape),
        scratch_shapes=list(scratch),
        compiler_params=PARAMS,
        cost_estimate=pl.CostEstimate(flops=flops, bytes_accessed=0, transcendentals=0),
    )(*operands)


class Block:
    def __init__(self, nx, ny, nz, c, r):
        self.nx, self.ny, self.nz, self.c, self.r = nx, ny, nz, c, r
        self.plane = ny * nz

    def send_shapes(self):
        rows = self.nz * PAIR
        x = jax.ShapeDtypeStruct((self.ny, rows, self.r), BF)
        y = jax.ShapeDtypeStruct((self.nx, rows, self.r), BF)
        z = jax.ShapeDtypeStruct((self.nx * self.ny // 2, 2 * PAIR, self.r), BF)
        return [x, x, y, y, z, z]

    def slot(self, face, x, y, z):
        if face < 2:
            return (y, pl.ds(z * PAIR, PAIR))
        if face < 4:
            return (x, pl.ds(z * PAIR, PAIR))
        return (x * (self.ny // 2) + y // 2, pl.ds((y % 2) * PAIR, PAIR))

    def halo_faces(self, x_side, y, z):
        faces = [] if x_side is None else [x_side]
        if y == 0:
            faces.append(2)
        if y == self.ny - 1:
            faces.append(3)
        if z == 0:
            faces.append(4)
        if z == self.nz - 1:
            faces.append(5)
        return faces

    def work(self, x, x_side):
        return [
            (x * self.plane + y * self.nz + z, y, z, self.halo_faces(x_side, y, z))
            for y in range(self.ny)
            for z in range(self.nz)
        ]

    def every_plane(self, visit):
        lax.fori_loop(0, self.nx, lambda x, carry: (visit(x), carry)[1], 0)

    def inner_planes(self, visit):
        lax.fori_loop(1, self.nx - 1, lambda x, carry: (visit(x, None), carry)[1], 0)

    def end_planes(self, visit):
        visit(0, 0)
        visit(self.nx - 1, 1)

    def near_local(self, face, x, y, z):
        dx, dy, dz = [(-1, 0, 0), (1, 0, 0), (0, -1, 0), (0, 1, 0), (0, 0, -1), (0, 0, 1)][face]
        return (x + 1 + dx) * self.plane + (y + dy) * self.nz + (z + dz), face ^ 1


def even_in_z():
    return lax.rem(lax.axis_index("gz"), 2) == 0


def pick(near, f, place):
    if f < 4:
        return near[f][place]
    first, second = near[4][place], near[5][place]
    return jnp.where(even_in_z(), *((second, first) if f == 4 else (first, second)))


def send_traces(block, x, work, values, bt, sends):
    traces = [
        mm(jnp.concatenate([bt[f] for f in faces], axis=0), a).astype(BF)
        for (_, _, _, faces), a in zip(work, values)
    ]
    sides = {}
    for (_, y, z, faces), t in zip(work, traces):
        for i, f in enumerate(faces):
            piece = t[i * PAD : i * PAD + PAIR]
            if f < 4:
                sends[f][block.slot(f, x, y, z)] = piece
            else:
                sides[f, y] = piece
    for y in sorted({y for _, y in sides}):
        place, low, high = block.slot(4, x, y, 0), sides[4, y], sides[5, y]
        sends[4][place] = jnp.where(even_in_z(), high, low)
        sends[5][place] = jnp.where(even_in_z(), low, high)


def first_sends(block, a, bt):
    def along_x(a_ref, bt_ref, *sends):
        def visit(x, side):
            work = [(e, y, z, [side]) for e, y, z, _ in block.work(x, None)]
            send_traces(block, x, work, [a_ref[w[0]] for w in work], bt_ref, sends)

        block.end_planes(visit)

    def others(a_ref, bt_ref, *sends):
        def visit(x):
            work = block.work(x, None)
            send_traces(block, x, work, [a_ref[w[0]] for w in work], bt_ref, (None, None) + sends)

        block.every_plane(visit)

    shapes = block.send_shapes()
    first = call(along_x, shapes[:2], [a, bt], FIRST)
    return [*first, *call(others, shapes[2:], [a, bt], SECOND)]


def one_hots(o_ref, e):
    own = o_ref[e]
    group, modes = own.shape
    index = jnp.concatenate([own + v * modes for v in range(VARS)], axis=1)
    rows = lax.broadcasted_iota(jnp.int32, (PAD, VARS * modes), 0)
    return [(rows == index[f : f + 1]).astype(BF) for f in range(group)]


def prepared(block, jacobian, orientation, bt):
    count, group, width, _ = jacobian.shape
    many = 4

    def kernel(j_ref, o_ref, bt_ref, jp_ref, bc_ref, ball_ref):
        for f in range(group):
            basis = bt_ref[f].astype(F32).T.astype(BF)
            ball_ref[:, f * PAD : (f + 1) * PAD] = basis
            bc_ref[f] = jnp.concatenate([basis, jnp.zeros((block.c, LANES - PAD), BF)], axis=1)
        none = jnp.zeros((PAD - width, PAD), BF)

        def elements(step, carry):
            places = [many * step + i for i in range(many)]
            turned = [one_hots(o_ref, e) for e in places]
            moved = [
                [mm_t(j_ref[e, f], turn[f]).astype(BF) for f in range(group)]
                for e, turn in zip(places, turned)
            ]
            for e, values in zip(places, moved):
                for f in range(group):
                    jp_ref[e, f, :width] = values[f]
                    jp_ref[e, f, width:] = none
            return carry

        lax.fori_loop(0, count // many, elements, 0)

    shape = jax.ShapeDtypeStruct((count, group, PAD, PAD), BF)
    bc = jax.ShapeDtypeStruct((group, block.c, LANES), BF)
    ball = jax.ShapeDtypeStruct((block.c, group * PAD), BF)
    return call(kernel, [shape, bc, ball], [jacobian, orientation, bt], PREP)


def write_permutations(block, o_ref, p_ref):
    group, modes = o_ref.shape[1:]
    rows = lax.broadcasted_iota(jnp.int32, (PAD, VARS * modes), 0)
    eye = (rows == lax.broadcasted_iota(jnp.int32, (PAD, VARS * modes), 1)).astype(BF)

    def elements(step, carry):
        places = [4 * step + i for i in range(4)]
        values = [[mm_t(eye, turn).astype(BF) for turn in one_hots(o_ref, e)] for e in places]
        for e, value in zip(places, values):
            for f in range(group):
                p_ref[e, f] = value[f]
        return carry

    lax.fori_loop(0, block.nx * block.plane // 4, elements, 0)


def fill_traces(block, a_ref, bt_ref, t_ref):
    nx, plane = block.nx, block.plane
    t_ref[0:plane, 1] = jnp.zeros((plane, PAD, block.r), BF)
    t_ref[(nx + 1) * plane : (nx + 2) * plane, 0] = jnp.zeros((plane, PAD, block.r), BF)
    every = bt_ref[...].reshape(6 * PAD, block.c)

    def traces(x):
        t = []
        for i in range(0, plane, 2):
            pair = jnp.concatenate([a_ref[x * plane + i], a_ref[x * plane + i + 1]], axis=1)
            both = mm(every, pair).astype(BF)
            t += [both[:, : block.r], both[:, block.r :]]
        for i in range(plane):
            for f in range(6):
                t_ref[(x + 1) * plane + i, f] = t[i][f * PAD : (f + 1) * PAD]

    block.every_plane(traces)


def local_faces(block, y, z):
    return [f for f in range(6) if f < 2 or f not in block.halo_faces(None, y, z)]


def widened(pieces):
    gap = jnp.zeros((LANES - PAD, pieces[0].shape[1]), BF)
    return jnp.concatenate([part for p in pieces for part in (p, gap)], axis=0)


def coupled(bc_ref, faces, fluxes):
    return mm(jnp.concatenate([bc_ref[f] for f in faces], axis=1), widened(fluxes))


def local_residual(block, a, source, jp, bt, ball, orientation=None):
    def kernel(a_ref, s_ref, j_ref, bt_ref, ball_ref, *refs):
        if orientation is not None:
            o_ref, r_ref, p_ref, t_ref = refs
            write_permutations(block, o_ref, p_ref)
        else:
            r_ref, t_ref = refs
        fill_traces(block, a_ref, bt_ref, t_ref)
        none = jnp.zeros((PAD, block.r), BF)

        def plane(x):
            work = [(e, y, z, local_faces(block, y, z)) for e, y, z, _ in block.work(x, None)]
            fluxes = [
                [mm(j_ref[e, f], t_ref[block.near_local(f, x, y, z)]).astype(BF) for f in faces]
                for e, y, z, faces in work
            ]
            full = [
                jnp.concatenate([dict(zip(w[3], flux)).get(f, none) for f in range(6)], axis=0)
                for w, flux in zip(work, fluxes)
            ]
            rest = []
            for i in range(0, len(work), 2):
                both = mm(ball_ref[...], jnp.concatenate(full[i : i + 2], axis=1))
                rest += [both[:, : block.r], both[:, block.r :]]
            for w, value in zip(work, rest):
                r_ref[w[0]] = s_ref[w[0]].astype(F32) - value

        block.every_plane(plane)

    count = block.nx * block.plane
    out = [jax.ShapeDtypeStruct((count, block.c, block.r), F32)]
    operands = [a, source, jp, bt, ball]
    if orientation is not None:
        out.append(jax.ShapeDtypeStruct(jp.shape, BF))
        operands.append(orientation)
    traces = pltpu.VMEM(((block.nx + 2) * block.plane, 6, PAD, block.r), BF)
    return call(kernel, out, operands, LOCAL, [traces])


def z_then_y(parts):
    return [*parts[4:], *parts[2:4]]


def by_face(refs):
    return (None, None) + tuple(refs[2:4]) + tuple(refs[:2])


def x_fluxes(block, halos, jp):
    def kernel(low_ref, high_ref, j_ref, out_ref):
        near = (low_ref, high_ref)

        def visit(x, side):
            work = block.work(x, None)
            fluxes = [
                mm(j_ref[e, side, :, :PAIR], near[side][block.slot(side, x, y, z)]).astype(BF)
                for e, y, z, _ in work
            ]
            for i, flux in enumerate(fluxes):
                out_ref[side * block.plane + i] = flux

        block.end_planes(visit)

    shape = jax.ShapeDtypeStruct((2 * block.plane, PAD, block.r), BF)
    return call(kernel, shape, [*halos, jp], WAIT)


def finish_sweep(block, halos, residual, inverse, jp, bt, bc):
    def plane(x, x_side, ready, near, sends, r_ref, v_ref, j_ref, bt_ref, bc_ref, a_ref):
        work = block.work(x, x_side)
        fluxes = [
            [
                ready[x_side * block.plane + i]
                if f < 2
                else mm(j_ref[e, f, :, :PAIR], pick(near, f, block.slot(f, x, y, z))).astype(BF)
                for f in faces
            ]
            for i, (e, y, z, faces) in enumerate(work)
        ]
        rest = [(r_ref[w[0]] - coupled(bc_ref, w[3], flux)).astype(BF) for w, flux in zip(work, fluxes)]
        values = [mm(v_ref[w[0]], value).astype(BF) for w, value in zip(work, rest)]
        send_traces(block, x, work, values, bt_ref, sends)
        for w, value in zip(work, values):
            a_ref[w[0]] = value

    def ends(*refs):
        ready, near, fixed, (a_ref, *sends) = refs[0], by_face(refs[1:5]), refs[5:10], refs[10:]
        block.end_planes(lambda x, side: plane(x, side, ready, near, sends, *fixed, a_ref))

    def inner(*refs):
        done, near, fixed, (a_ref, *sends) = refs[:5], by_face(refs[5:9]), refs[9:14], refs[14:]
        sends = [None, None, *sends]
        block.inner_planes(lambda x, side: plane(x, side, None, near, sends, *fixed, a_ref))
        for have, want in zip(done, [a_ref, *sends[2:]]):
            step = want.shape[0] // block.nx
            for x in (0, block.nx - 1):
                want[x * step : (x + 1) * step] = have[x * step : (x + 1) * step]

    fixed = [residual, inverse, jp, bt, bc]
    shapes = block.send_shapes()
    whole = jax.ShapeDtypeStruct((block.nx * block.plane, block.c, block.r), BF)
    ready = x_fluxes(block, halos[:2], jp)
    part, *sends = call(ends, [whole] + shapes, [ready, *z_then_y(halos), *fixed], FIRST)
    a, *rest = call(inner, [whole] + shapes[2:], [part, *sends[2:], *z_then_y(halos), *fixed], SECOND)
    return a, [*sends[:2], *rest]


def local_gradient(block, a, jp, p, bt):
    def kernel(a_ref, j_ref, p_ref, bt_ref, g_ref, t_ref):
        fill_traces(block, a_ref, bt_ref, t_ref)

        def plane(x, carry):
            grads = []
            for e, y, z, _ in block.work(x, None):
                rows = [jnp.zeros((1, block.r), F32)] * 8
                for f in local_faces(block, y, z):
                    both = jnp.concatenate([j_ref[e, f], p_ref[e, f]], axis=0)
                    both = mm(both, t_ref[block.near_local(f, x, y, z)])
                    own = t_ref[e + block.plane, f].astype(F32)
                    rows[f] = jnp.sum((own - both[PAD:]) * both[:PAD], axis=0, keepdims=True)
                grads.append((e, jnp.concatenate(rows, axis=0)))
            for e, value in grads:
                g_ref[e] = value
            return carry

        lax.fori_loop(0, block.nx, plane, 0)

    count = block.nx * block.plane
    return call(
        kernel,
        jax.ShapeDtypeStruct((count, 8, block.r), F32),
        [a, jp, p, bt],
        LOCAL,
        [pltpu.VMEM(((block.nx + 2) * block.plane, 6, PAD, block.r), BF)],
    )


def finish_gradient(block, halos, owns, inside, jp, p):
    def add(x, work, near, own, j_ref, p_ref, g_ref):
        total = []
        for e, y, z, faces in work:
            rows = [jnp.zeros((1, block.r), F32)] * 8
            for f in faces:
                place = block.slot(f, x, y, z)
                both = jnp.concatenate([j_ref[e, f, :, :PAIR], p_ref[e, f, :, :PAIR]], axis=0)
                both = mm(both, pick(near, f, place))
                gap = pick(own, f, place).astype(F32) - both[PAD : PAD + PAIR]
                rows[f] = jnp.sum(gap * both[:PAIR], axis=0, keepdims=True)
            total.append(g_ref[e] + jnp.concatenate(rows, axis=0))
        return total

    def along_x(*refs):
        near, own, (j_ref, p_ref, g_ref, out_ref) = refs[:2], refs[2:4], refs[4:]

        def visit(x, side):
            work = [(e, y, z, [side]) for e, y, z, _ in block.work(x, None)]
            for w, value in zip(work, add(x, work, near, own, j_ref, p_ref, g_ref)):
                out_ref[w[0]] = value

        block.end_planes(visit)
        kept = slice(block.plane, (block.nx - 1) * block.plane)
        out_ref[kept] = g_ref[kept]

    def others(*refs):
        near, own, (j_ref, p_ref, g_ref, out_ref) = by_face(refs[:4]), by_face(refs[4:8]), refs[8:]

        def visit(x):
            work = block.work(x, None)
            total = add(x, work, near, own, j_ref, p_ref, g_ref)
            for y in range(block.ny):
                for f in range(6):
                    rows = [g[f : f + 1] for g in total[y * block.nz : (y + 1) * block.nz]]
                    out_ref[x * block.ny + y, f] = jnp.concatenate(rows, axis=0)

        block.every_plane(visit)

    inside = call(along_x, inside, [*halos[:2], *owns[:2], jp, p, inside], WAIT)
    shape = jax.ShapeDtypeStruct((block.nx * block.ny, 6, block.nz, block.r), F32)
    return call(others, shape, [*z_then_y(halos), *z_then_y(owns), jp, p, inside], LOCAL)


def exchange(sends):
    halos = []
    for d, axis in enumerate(("gx", "gy")):
        count = lax.axis_size(axis)
        up = [(i, (i + 1) % count) for i in range(count)]
        down = [(j, i) for i, j in up]
        halos.append(lax.ppermute(sends[2 * d + 1], axis, up))
        halos.append(lax.ppermute(sends[2 * d], axis, down))
    for part, start in enumerate((0, 1)):
        pairs = [(i, i + 1) for i in range(start, lax.axis_size("gz") - 1, 2)]
        halos.append(lax.ppermute(sends[4 + part], "gz", pairs + [(j, i) for i, j in pairs]))
    return halos


def on_device(adjoint_source, warm_start, block_inverse, face_jacobian, trace_basis, orientation):
    nx, ny, nz, c, r = warm_start.shape
    count = nx * ny * nz
    width = trace_basis.shape[-1]
    modes = orientation.shape[-1]
    block = Block(nx, ny, nz, c, r)
    gap = PAD - width

    bt = jnp.pad(trace_basis.transpose(0, 2, 1), ((0, 0), (0, gap), (0, 0)))
    adjoint = warm_start.reshape(count, c, r)
    sends = first_sends(block, adjoint, bt)

    source = adjoint_source.reshape(count, c, r)
    inverse = block_inverse.reshape(count, c, c)
    turns = orientation.reshape(count, 6, modes)
    jacobian = face_jacobian.reshape(count, 6, width, width)
    jp, bc, ball = prepared(block, jacobian, turns, bt)

    for sweep in range(SWEEPS):
        halos = exchange(sends)
        last = [turns] if sweep == SWEEPS - 1 else []
        residual, *rest = local_residual(block, adjoint, source, jp, bt, ball, *last)
        adjoint, sends = finish_sweep(block, halos, residual, inverse, jp, bt, bc)
    (p,) = rest
    halos = exchange(sends)
    inside = local_gradient(block, adjoint, jp, p, bt)
    gradient = finish_gradient(block, halos, sends, inside, jp, p)
    gradient = gradient.reshape(nx, ny, 6, nz, r).transpose(0, 1, 3, 2, 4)
    return (adjoint.reshape(warm_start.shape), gradient)


def solution(mesh):
    return jax.shard_map(
        on_device,
        mesh=mesh,
        in_specs=(
            P("gx", "gy", "gz", None, None),
            P("gx", "gy", "gz", None, None),
            P("gx", "gy", "gz", None, None),
            P("gx", "gy", "gz", None, None, None),
            P(),
            P("gx", "gy", "gz", None, None),
        ),
        out_specs=(P("gx", "gy", "gz", None, None), P("gx", "gy", "gz", None, None)),
        check_vma=False,
    )
```

time: 111 us -> 92.9 us (0.84)
  the two profiles are of different devices: /device:TPU:44 before, /device:TPU:57 now
where the time goes in v1:
time: 92.9 us; the launch traced here: 92.7 us
  starting transfers between devices  37 us (40%)
  Pallas kernels  33.2 us (36%)
  waiting for transfers between devices  16.3 us (18%)
  local copies, waits for them, and re-layouts  5.3 us (6%)
    pallas_call x14, Pallas kernels, call(): pl.pallas_call(kernel, out_shape=out_shape, in_specs=[VMEM] * len(operand...  33.2 us
    ppermute x6, starting transfers between devices, exchange(): halos.append(lax.ppermute(sends[2 * d], axis, down))  14.5 us
    ppermute x6, waiting for transfers between devices, exchange(): halos.append(lax.ppermute(sends[2 * d], axis, down))  14.5 us
    ppermute x6, starting transfers between devices, exchange(): halos.append(lax.ppermute(sends[2 * d + 1], axis, up))  12.2 us
    ppermute x6, starting transfers between devices, exchange(): lax.ppermute(sends[4 + part], 'gz', pairs + [(j, i) for i, j in pairs])  10.3 us
    unnamed x16, local copies, waits for them, and re-layouts  5.26 us
  transfers between devices with their start and end apart: 18, of which 4 were waited for; matrix products, arithmetic and copies ran while one was open for 4% of the time, Pallas kernels for 30%

profile of v1, /device:TPU:57, one launch (start us, length us, event | category | flops | bytes accessed | tf_op | source)
XLA Modules:
  0.0 92.7 jit_solution(793260143787418713)
XLA Ops:
  0.6 0.0 copy-start.3
  0.6 1.6 %copy.8 = bf16[4,4,2,175,128]{4,3,2,1,0:T(8,128)(2,1)S(1)} copy(bf16[4,4,2,175,128]{4,2,3,1,0:T(2,128)(2,1)} %param.7) | data formatting | bytes 2867200 | tf_op args[1]
  2.2 0.0 copy-done.3
  2.2 0.0 copy-start
  2.3 0.0 copy-start.4
  2.3 0.3 shard_map.77
  2.7 6.1 %collective-permute-start = (bf16[4,152,128]{2,1,0:T(8,128)(2,1)S(1)}, bf16[4,152,128]{2,1,0:T(8,128)(2,1)S(1)}, u32[]{:S(2)}, u32[]{:S(2)}) collective-permute-start(bf16[4,152,128]{2,1,0:T(8,128)(2,1)S(1)} %get-tuple-element.37), channel_id=1, source_target_pairs={{0,32},{32,64},{64,96},{96,128},{128,160},{160,192},{192,224},{224... | collective-permute-start | bytes 466952 | tf_op jit(solution)/shard_map/ppermute | solution.py:421
  8.8 2.3 %collective-permute-start.1 = (bf16[4,152,128]{2,1,0:T(8,128)(2,1)S(1)}, bf16[4,152,128]{2,1,0:T(8,128)(2,1)S(1)}, u32[]{:S(2)}, u32[]{:S(2)}) collective-permute-start(bf16[4,152,128]{2,1,0:T(8,128)(2,1)S(1)} %get-tuple-element.38), channel_id=1, source_target_pairs={{32,0},{64,32},{96,64},{128,96},{160,128},{192,160},{224,192},{0,2... | collective-permute-start | bytes 466952 | tf_op jit(solution)/shard_map/ppermute | solution.py:422
  11.1 1.1 %shard_map.80 = (bf16[4,152,128]{2,1,0:T(8,128)(2,1)S(1)}, bf16[4,152,128]{2,1,0:T(8,128)(2,1)S(1)}, bf16[8,152,128]{2,1,0:T(8,128)(2,1)S(1)}, bf16[8,152,128]{2,1,0:T(8,128)(2,1)S(1)}) custom-call(bf16[32,175,128]{2,1,0:T(8,128)(2,1)S(1)} %bitcast.15, bf16[6,80,175]{2,1,0:T(8,128)(2,1)S(1)} %pad.4.bt_ref.refs_8_.refs_12_), custom_call_target="tpu_custom_call" | custom-call | flops 1000 | tf_op jit(solution)/shard_map/pallas_call | solution.py:33
  12.2 0.8 collective-permute-start.2
  13.0 3.6 %collective-permute-start.3 = (bf16[8,152,128]{2,1,0:T(8,128)(2,1)S(1)}, bf16[8,152,128]{2,1,0:T(8,128)(2,1)S(1)}, u32[]{:S(2)}, u32[]{:S(2)}) collective-permute-start(bf16[8,152,128]{2,1,0:T(8,128)(2,1)S(1)} %get-tuple-element.41), channel_id=1, source_target_pairs={{1,2},{2,1},{5,6},{6,5},{9,10},{10,9},{13,14},{14,13},{17,18},{18,... | collective-permute-start | bytes 933896 | tf_op jit(solution)/shard_map/ppermute | solution.py:425
  16.6 1.6 %collective-permute-start.4 = (bf16[4,152,128]{2,1,0:T(8,128)(2,1)S(1)}, bf16[4,152,128]{2,1,0:T(8,128)(2,1)S(1)}, u32[]{:S(2)}, u32[]{:S(2)}) collective-permute-start(bf16[4,152,128]{2,1,0:T(8,128)(2,1)S(1)} %get-tuple-element.42), channel_id=1, source_target_pairs={{0,4},{4,8},{8,12},{12,16},{16,20},{20,24},{24,28},{28,0},{1,5},{5... | collective-permute-start | bytes 466952 | tf_op jit(solution)/shard_map/ppermute | solution.py:421
  18.3 0.0 copy-done.4
  18.3 0.0 copy-done
  18.3 0.8 copy.9
  19.1 0.0 copy-start.2
  19.1 4.3 %shard_map.78 = (bf16[32,6,80,80]{3,2,1,0:T(8,128)(2,1)S(1)}, bf16[6,175,128]{2,1,0:T(8,128)(2,1)S(1)}, bf16[175,480]{1,0:T(8,128)(2,1)S(1)}) custom-call(bf16[32,6,75,75]{3,2,1,0:T(8,128)(2,1)S(1)} %bitcast.17, s32[32,6,15]{2,1,0:T(8,128)S(1)} %bitcast.21, bf16[6,80,175]{2,1,0:T(8,128)(2,1)S(1)} %pad.4.bt_ref.refs_8_.refs_12_), custom_call_target="tpu_custom_call" | custom-call | flops 1000 | tf_op jit(solution)/shard_map/pallas_call | solution.py:33
  23.4 0.0 copy-done.2
  23.4 0.2 copy.11
  23.6 0.0 copy-start.1
  23.6 4.7 %shard_map.81.refs_5_.refs_9_ = f32[32,175,128]{2,1,0:T(8,128)S(1)} custom-call(bf16[32,175,128]{2,1,0:T(8,128)(2,1)S(1)} %bitcast.16, bf16[32,175,128]{2,1,0:T(8,128)(2,1)S(1)} %bitcast.18, bf16[32,6,80,80]{3,2,1,0:T(8,128)(2,1)S(1)} %get-tuple-element.39.j_ref.refs_7_.refs_11_.refs_4_.refs_8_, bf16[6,80,175]{2,1,0:T(8,128)(2,1)S(1)} %pad.4.bt_ref.refs_8_.refs_12_, ...), custom_call_target="tpu_custom_call" | custom-call | flops 1000 | tf_op jit(solution)/shard_map/pallas_call | solution.py:33
  28.4 0.4 copy.12
  28.9 0.0 collective-permute-done.low_ref
  28.9 0.2 collective-permute-start.5
  29.1 0.0 collective-permute-done.1.high_ref
  29.1 0.3 shard_map.79.refs_0_
  29.4 0.0 collective-permute-done.4.refs_3_.refs_7_
  29.4 5.3 %collective-permute-done.5.refs_4_.refs_8_ = bf16[4,152,128]{2,1,0:T(8,128)(2,1)S(1)} collective-permute-done((bf16[4,152,128]{2,1,0:T(8,128)(2,1)S(1)}, bf16[4,152,128]{2,1,0:T(8,128)(2,1)S(1)}, u32[]{:S(2)}, u32[]{:S(2)}) %collective-permute-start.5) | collective-permute-done | bytes 155680 | tf_op jit(solution)/shard_map/ppermute | solution.py:422
  34.8 0.0 collective-permute-done.2.refs_1_.refs_5_
  34.8 0.0 collective-permute-done.3.refs_2_.refs_6_
  34.8 1.8 %shard_map.82 = (bf16[32,175,128]{2,1,0:T(8,128)(2,1)S(1)}, bf16[4,152,128]{2,1,0:T(8,128)(2,1)S(1)}, bf16[4,152,128]{2,1,0:T(8,128)(2,1)S(1)}, bf16[4,152,128]{...) custom-call(bf16[16,80,128]{2,1,0:T(8,128)(2,1)S(1)} %shard_map.79.r, ...), custom_call_target="tpu_custom_call" | custom-call | flops 1000 | tf_op jit(solution)/shard_map/pallas_call | solution.py:33
  36.6 2.2 %collective-permute-start.6 = (bf16[4,152,128]{2,1,0:T(8,128)(2,1)S(1)}, bf16[4,152,128]{2,1,0:T(8,128)(2,1)S(1)}, u32[]{:S(2)}, u32[]{:S(2)}) collective-permute-start(bf16[4,152,128]{2,1,0:T(8,128)(2,1)S(1)} %get-tuple-element.46), channel_id=1, source_target_pairs={{0,32},{32,64},{64,96},{96,128},{128,160},{160,192},{192,224},{224... | collective-permute-start | bytes 466952 | tf_op jit(solution)/shard_map/ppermute | solution.py:421
  38.8 5.3 %collective-permute-start.7 = (bf16[4,152,128]{2,1,0:T(8,128)(2,1)S(1)}, bf16[4,152,128]{2,1,0:T(8,128)(2,1)S(1)}, u32[]{:S(2)}, u32[]{:S(2)}) collective-permute-start(bf16[4,152,128]{2,1,0:T(8,128)(2,1)S(1)} %get-tuple-element.47), channel_id=1, source_target_pairs={{32,0},{64,32},{96,64},{128,96},{160,128},{192,160},{224,192},{0,2... | collective-permute-start | bytes 466952 | tf_op jit(solution)/shard_map/ppermute | solution.py:422
  44.1 1.8 %shard_map.84 = (bf16[32,175,128]{2,1,0:T(8,128)(2,1)S(1)}, bf16[4,152,128]{2,1,0:T(8,128)(2,1)S(1)}, bf16[4,152,128]{2,1,0:T(8,128)(2,1)S(1)}, bf16[8,152,128]{2,1,0:T(8,128)(2,1)S(1)}, bf16[8,152,128]{2,1,0:T(8,128)(2,1)S(1)}) custom-call(bf16[32,175,128]{2,1,0:T(8,128)(2,1)S(1)} %get-tuple-element.48.refs_0_, ...), custom_call_target="tpu_custom_call" | custom-call | flops 1000 | tf_op jit(solution)/shard_map/pallas_call | solution.py:33
  45.9 0.1 collective-permute-start.8
  46.0 2.1 %collective-permute-start.9 = (bf16[8,152,128]{2,1,0:T(8,128)(2,1)S(1)}, bf16[8,152,128]{2,1,0:T(8,128)(2,1)S(1)}, u32[]{:S(2)}, u32[]{:S(2)}) collective-permute-start(bf16[8,152,128]{2,1,0:T(8,128)(2,1)S(1)} %get-tuple-element.54), channel_id=1, source_target_pairs={{1,2},{2,1},{5,6},{6,5},{9,10},{10,9},{13,14},{14,13},{17,18},{18,... | collective-permute-start | bytes 933896 | tf_op jit(solution)/shard_map/ppermute | solution.py:425
  48.1 0.4 collective-permute-start.10
  48.6 8.7 %shard_map.85 = (f32[32,175,128]{2,1,0:T(8,128)S(1)}, bf16[32,6,80,80]{3,2,1,0:T(8,128)(2,1)S(1)}) custom-call(bf16[32,175,128]{2,1,0:T(8,128)(2,1)S(1)} %get-tuple-element.57.a_ref, bf16[32,175,128]{2,1,0:T(8,128)(2,1)S(1)} %bitcast.19, bf16[32,6,80,80]{3,2,1,0:T(8,128)(2,1)S(1)} %get-tuple-element.39.j_ref.refs_7_.refs_11_.refs_4_.refs_8_, ...), custom_call_target="tpu_custom_call" | custom-call | flops 1000 | tf_op jit(solution)/shard_map/pallas_call | solution.py:33
  57.3 0.0 collective-permute-done.6.low_ref
  57.3 0.1 collective-permute-start.11
  57.4 0.0 collective-permute-done.7.high_ref
  57.4 0.3 shard_map.83.refs_0_
  57.7 0.0 collective-permute-done.10.refs_3_.refs_7_
  57.7 5.4 %collective-permute-done.11.refs_4_.refs_8_ = bf16[4,152,128]{2,1,0:T(8,128)(2,1)S(1)} collective-permute-done((bf16[4,152,128]{2,1,0:T(8,128)(2,1)S(1)}, bf16[4,152,128]{2,1,0:T(8,128)(2,1)S(1)}, u32[]{:S(2)}, u32[]{:S(2)}) %collective-permute-start.11) | collective-permute-done | bytes 155680 | tf_op jit(solution)/shard_map/ppermute | solution.py:422
  63.1 0.0 collective-permute-done.8.refs_1_.refs_5_
  63.1 0.0 collective-permute-done.9.refs_2_.refs_6_
  63.1 1.8 %shard_map.86 = (bf16[32,175,128]{2,1,0:T(8,128)(2,1)S(1)}, bf16[4,152,128]{2,1,0:T(8,128)(2,1)S(1)}, bf16[4,152,128]{2,1,0:T(8,128)(2,1)S(1)}, bf16[4,152,128]{...) custom-call(bf16[16,80,128]{2,1,0:T(8,128)(2,1)S(1)} %shard_map.83.r, ...), custom_call_target="tpu_custom_call" | custom-call | flops 1000 | tf_op jit(solution)/shard_map/pallas_call | solution.py:33
  65.0 1.1 %collective-permute-start.16 = (bf16[4,152,128]{2,1,0:T(8,128)(2,1)S(1)}, bf16[4,152,128]{2,1,0:T(8,128)(2,1)S(1)}, u32[]{:S(2)}, u32[]{:S(2)}) collective-permute-start(bf16[4,152,128]{2,1,0:T(8,128)(2,1)S(1)} %get-tuple-element.70.refs_3_), channel_id=1, source_target_pairs={{0,32},{32,64},{64,96},{96,128},{128,160},{160,192},{192,224},{224... | collective-permute-start | bytes 466952 | tf_op jit(solution)/shard_map/ppermute | solution.py:421
  66.1 6.5 %collective-permute-start.17 = (bf16[4,152,128]{2,1,0:T(8,128)(2,1)S(1)}, bf16[4,152,128]{2,1,0:T(8,128)(2,1)S(1)}, u32[]{:S(2)}, u32[]{:S(2)}) collective-permute-start(bf16[4,152,128]{2,1,0:T(8,128)(2,1)S(1)} %get-tuple-element.71.refs_2_), channel_id=1, source_target_pairs={{32,0},{64,32},{96,64},{128,96},{160,128},{192,160},{224,192},{0,2... | collective-permute-start | bytes 466952 | tf_op jit(solution)/shard_map/ppermute | solution.py:422
  72.5 1.8 %shard_map.87 = (bf16[32,175,128]{2,1,0:T(8,128)(2,1)S(1)}, bf16[4,152,128]{2,1,0:T(8,128)(2,1)S(1)}, bf16[4,152,128]{2,1,0:T(8,128)(2,1)S(1)}, bf16[8,152,128]{2,1,0:T(8,128)(2,1)S(1)}, bf16[8,152,128]{2,1,0:T(8,128)(2,1)S(1)}) custom-call(bf16[32,175,128]{2,1,0:T(8,128)(2,1)S(1)} %get-tuple-element.59.refs_0_, ...), custom_call_target="tpu_custom_call" | custom-call | flops 1000 | tf_op jit(solution)/shard_map/pallas_call | solution.py:33
  74.4 0.6 collective-permute-start.12
  74.9 3.2 %collective-permute-start.13 = (bf16[8,152,128]{2,1,0:T(8,128)(2,1)S(1)}, bf16[8,152,128]{2,1,0:T(8,128)(2,1)S(1)}, u32[]{:S(2)}, u32[]{:S(2)}) collective-permute-start(bf16[8,152,128]{2,1,0:T(8,128)(2,1)S(1)} %get-tuple-element.66.refs_5_), channel_id=1, source_target_pairs={{1,2},{2,1},{5,6},{6,5},{9,10},{10,9},{13,14},{14,13},{17,18},{18,... | collective-permute-start | bytes 933896 | tf_op jit(solution)/shard_map/ppermute | solution.py:425
  78.1 4.0 %shard_map.88.refs_6_ = f32[32,8,128]{2,1,0:T(8,128)S(1)} custom-call(bf16[32,175,128]{2,1,0:T(8,128)(2,1)S(1)} %get-tuple-element.64.a_ref, bf16[32,6,80,80]{3,2,1,0:T(8,128)(2,1)S(1)} %get-tuple-element.39.j_ref.refs_7_.refs_11_.refs_4_.refs_8_, bf16[32,6,80,80]{3,2,1,0:T(8,128)(2,1)S(1)} %get-tuple-element.69.p_ref.refs_5_.refs_9_, ...), custom_call_target="tpu_custom_call" | custom-call | flops 1000 | tf_op jit(solution)/shard_map/pallas_call | solution.py:33
  82.1 2.2 %copy.13 = bf16[4,4,2,175,128]{4,2,3,1,0:T(2,128)(2,1)} copy(bf16[4,4,2,175,128]{4,3,2,1,0:T(8,128)(2,1)S(1)} %bitcast.20) | data formatting | bytes 2867200
  84.3 0.7 collective-permute-start.14
  85.0 0.0 collective-permute-done.16.refs_0_
  85.0 0.0 collective-permute-start.15
  85.0 0.0 collective-permute-done.17.refs_1_
  85.0 0.4 shard_map.89.refs_10_
  85.3 1.8 %collective-permute-done.14.refs_2_ = bf16[4,152,128]{2,1,0:T(8,128)(2,1)S(1)} collective-permute-done((bf16[4,152,128]{2,1,0:T(8,128)(2,1)S(1)}, bf16[4,152,128]{2,1,0:T(8,128)(2,1)S(1)}, u32[]{:S(2)}, u32[]{:S(2)}) %collective-permute-start.14) | collective-permute-done | bytes 155680 | tf_op jit(solution)/shard_map/ppermute | solution.py:421
  87.1 3.7 %collective-permute-done.15.refs_3_ = bf16[4,152,128]{2,1,0:T(8,128)(2,1)S(1)} collective-permute-done((bf16[4,152,128]{2,1,0:T(8,128)(2,1)S(1)}, bf16[4,152,128]{2,1,0:T(8,128)(2,1)S(1)}, u32[]{:S(2)}, u32[]{:S(2)}) %collective-permute-start.15) | collective-permute-done | bytes 155680 | tf_op jit(solution)/shard_map/ppermute | solution.py:422
  90.8 0.0 collective-permute-done.12.refs_0_
  90.8 0.0 collective-permute-done.13.refs_1_
  90.8 1.9 %shard_map.90 = f32[16,6,2,128]{3,2,1,0:T(2,128)} custom-call(bf16[8,152,128]{2,1,0:T(8,128)(2,1)S(1)} %collective-permute-done.12.refs_0_, bf16[8,152,128]{2,1,0:T(8,128)(2,1)S(1)} %collective-permute-done.13.refs_1_, bf16[4,152,128]{2,1,0:T(8,128)(2,1)S(1)} %collective-permute-done.14.refs_2_, bf16[4,152,128]{2,1,0:T(8,128)(2,1)S(1)} %collective-permute-done.15.refs_3_, ...), custom_call_target="tpu_custom_call" | custom-call | flops 1000 | tf_op jit(solution)/shard_map/pallas_call | solution.py:33
  (3 shorter events, 0.1 us)
Async XLA Ops:
  0.6 1.6 %copy-start.3 = (bf16[6,175,75]{1,2,0:T(8,128)(2,1)S(1)}, bf16[6,175,75]{1,2,0:T(8,128)(2,1)}, u32[]{:S(2)}) copy-start(bf16[6,175,75]{1,2,0:T(8,128)(2,1)} %param.10) | copy-start | bytes 472504
  2.2 16.1 %copy-start = (bf16[4,4,2,6,75,75]{5,2,4,3,1,0:T(2,128)(2,1)S(1)}, bf16[4,4,2,6,75,75]{5,2,4,3,1,0:T(2,128)(2,1)}, u32[]{:S(2)}) copy-start(bf16[4,4,2,6,75,75]{5,2,4,3,1,0:T(2,128)(2,1)} %param.9) | copy-start | bytes 6480004
  2.3 16.0 %copy-start.4 = (s32[4,4,2,6,15]{4,2,3,1,0:T(2,128)S(1)}, s32[4,4,2,6,15]{4,2,3,1,0:T(2,128)}, u32[]{:S(2)}) copy-start(s32[4,4,2,6,15]{4,2,3,1,0:T(2,128)} %param.11) | copy-start | bytes 34564
  2.7 26.2 %collective-permute-start = (bf16[4,152,128]{2,1,0:T(8,128)(2,1)S(1)}, bf16[4,152,128]{2,1,0:T(8,128)(2,1)S(1)}, u32[]{:S(2)}, u32[]{:S(2)}) collective-permute-start(bf16[4,152,128]{2,1,0:T(8,128)(2,1)S(1)} %get-tuple-element.37), channel_id=1, source_target_pairs={{0,32},{32,64},{64,96},{96,128},{128,160},{160,192},{192,224},{224... | collective-permute-start | bytes 466952 | tf_op jit(solution)/shard_map/ppermute | solution.py:421
  8.8 20.4 %collective-permute-start.1 = (bf16[4,152,128]{2,1,0:T(8,128)(2,1)S(1)}, bf16[4,152,128]{2,1,0:T(8,128)(2,1)S(1)}, u32[]{:S(2)}, u32[]{:S(2)}) collective-permute-start(bf16[4,152,128]{2,1,0:T(8,128)(2,1)S(1)} %get-tuple-element.38), channel_id=1, source_target_pairs={{32,0},{64,32},{96,64},{128,96},{160,128},{192,160},{224,192},{0,2... | collective-permute-start | bytes 466952 | tf_op jit(solution)/shard_map/ppermute | solution.py:422
  12.2 22.5 %collective-permute-start.2 = (bf16[8,152,128]{2,1,0:T(8,128)(2,1)S(1)}, bf16[8,152,128]{2,1,0:T(8,128)(2,1)S(1)}, u32[]{:S(2)}, u32[]{:S(2)}) collective-permute-start(bf16[8,152,128]{2,1,0:T(8,128)(2,1)S(1)} %get-tuple-element.40), channel_id=1, source_target_pairs={{0,1},{2,3},{1,0},{3,2},{4,5},{6,7},{5,4},{7,6},{8,9},{10,11},{9,8... | collective-permute-start | bytes 933896 | tf_op jit(solution)/shard_map/ppermute | solution.py:425
  13.0 21.8 %collective-permute-start.3 = (bf16[8,152,128]{2,1,0:T(8,128)(2,1)S(1)}, bf16[8,152,128]{2,1,0:T(8,128)(2,1)S(1)}, u32[]{:S(2)}, u32[]{:S(2)}) collective-permute-start(bf16[8,152,128]{2,1,0:T(8,128)(2,1)S(1)} %get-tuple-element.41), channel_id=1, source_target_pairs={{1,2},{2,1},{5,6},{6,5},{9,10},{10,9},{13,14},{14,13},{17,18},{18,... | collective-permute-start | bytes 933896 | tf_op jit(solution)/shard_map/ppermute | solution.py:425
  16.6 12.8 %collective-permute-start.4 = (bf16[4,152,128]{2,1,0:T(8,128)(2,1)S(1)}, bf16[4,152,128]{2,1,0:T(8,128)(2,1)S(1)}, u32[]{:S(2)}, u32[]{:S(2)}) collective-permute-start(bf16[4,152,128]{2,1,0:T(8,128)(2,1)S(1)} %get-tuple-element.42), channel_id=1, source_target_pairs={{0,4},{4,8},{8,12},{12,16},{16,20},{20,24},{24,28},{28,0},{1,5},{5... | collective-permute-start | bytes 466952 | tf_op jit(solution)/shard_map/ppermute | solution.py:421
  19.1 4.3 %copy-start.2 = (bf16[4,4,2,175,128]{4,2,3,1,0:T(2,128)(2,1)S(1)}, bf16[4,4,2,175,128]{4,2,3,1,0:T(2,128)(2,1)}, u32[]{:S(2)}) copy-start(bf16[4,4,2,175,128]{4,2,3,1,0:T(2,128)(2,1)} %param.6) | copy-start | bytes 4300804
  23.6 4.8 %copy-start.1 = (bf16[4,4,2,175,175]{4,2,3,1,0:T(2,128)(2,1)S(1)}, bf16[4,4,2,175,175]{4,2,3,1,0:T(2,128)(2,1)}, u32[]{:S(2)}) copy-start(bf16[4,4,2,175,175]{4,2,3,1,0:T(2,128)(2,1)} %param.8) | copy-start | bytes 5880004
  28.9 5.9 %collective-permute-start.5 = (bf16[4,152,128]{2,1,0:T(8,128)(2,1)S(1)}, bf16[4,152,128]{2,1,0:T(8,128)(2,1)S(1)}, u32[]{:S(2)}, u32[]{:S(2)}) collective-permute-start(bf16[4,152,128]{2,1,0:T(8,128)(2,1)S(1)} %get-tuple-element.43), channel_id=1, source_target_pairs={{4,0},{8,4},{12,8},{16,12},{20,16},{24,20},{28,24},{0,28},{5,1},{9... | collective-permute-start | bytes 466952 | tf_op jit(solution)/shard_map/ppermute | solution.py:422
  36.6 20.7 %collective-permute-start.6 = (bf16[4,152,128]{2,1,0:T(8,128)(2,1)S(1)}, bf16[4,152,128]{2,1,0:T(8,128)(2,1)S(1)}, u32[]{:S(2)}, u32[]{:S(2)}) collective-permute-start(bf16[4,152,128]{2,1,0:T(8,128)(2,1)S(1)} %get-tuple-element.46), channel_id=1, source_target_pairs={{0,32},{32,64},{64,96},{96,128},{128,160},{160,192},{192,224},{224... | collective-permute-start | bytes 466952 | tf_op jit(solution)/shard_map/ppermute | solution.py:421
  38.8 18.6 %collective-permute-start.7 = (bf16[4,152,128]{2,1,0:T(8,128)(2,1)S(1)}, bf16[4,152,128]{2,1,0:T(8,128)(2,1)S(1)}, u32[]{:S(2)}, u32[]{:S(2)}) collective-permute-start(bf16[4,152,128]{2,1,0:T(8,128)(2,1)S(1)} %get-tuple-element.47), channel_id=1, source_target_pairs={{32,0},{64,32},{96,64},{128,96},{160,128},{192,160},{224,192},{0,2... | collective-permute-start | bytes 466952 | tf_op jit(solution)/shard_map/ppermute | solution.py:422
  45.9 17.2 %collective-permute-start.8 = (bf16[8,152,128]{2,1,0:T(8,128)(2,1)S(1)}, bf16[8,152,128]{2,1,0:T(8,128)(2,1)S(1)}, u32[]{:S(2)}, u32[]{:S(2)}) collective-permute-start(bf16[8,152,128]{2,1,0:T(8,128)(2,1)S(1)} %get-tuple-element.53), channel_id=1, source_target_pairs={{0,1},{2,3},{1,0},{3,2},{4,5},{6,7},{5,4},{7,6},{8,9},{10,11},{9,8... | collective-permute-start | bytes 933896 | tf_op jit(solution)/shard_map/ppermute | solution.py:425
  46.0 17.1 %collective-permute-start.9 = (bf16[8,152,128]{2,1,0:T(8,128)(2,1)S(1)}, bf16[8,152,128]{2,1,0:T(8,128)(2,1)S(1)}, u32[]{:S(2)}, u32[]{:S(2)}) collective-permute-start(bf16[8,152,128]{2,1,0:T(8,128)(2,1)S(1)} %get-tuple-element.54), channel_id=1, source_target_pairs={{1,2},{2,1},{5,6},{6,5},{9,10},{10,9},{13,14},{14,13},{17,18},{18,... | collective-permute-start | bytes 933896 | tf_op jit(solution)/shard_map/ppermute | solution.py:425
  48.1 9.5 %collective-permute-start.10 = (bf16[4,152,128]{2,1,0:T(8,128)(2,1)S(1)}, bf16[4,152,128]{2,1,0:T(8,128)(2,1)S(1)}, u32[]{:S(2)}, u32[]{:S(2)}) collective-permute-start(bf16[4,152,128]{2,1,0:T(8,128)(2,1)S(1)} %get-tuple-element.55), channel_id=1, source_target_pairs={{0,4},{4,8},{8,12},{12,16},{16,20},{20,24},{24,28},{28,0},{1,5},{5... | collective-permute-start | bytes 466952 | tf_op jit(solution)/shard_map/ppermute | solution.py:421
  57.3 5.9 %collective-permute-start.11 = (bf16[4,152,128]{2,1,0:T(8,128)(2,1)S(1)}, bf16[4,152,128]{2,1,0:T(8,128)(2,1)S(1)}, u32[]{:S(2)}, u32[]{:S(2)}) collective-permute-start(bf16[4,152,128]{2,1,0:T(8,128)(2,1)S(1)} %get-tuple-element.56), channel_id=1, source_target_pairs={{4,0},{8,4},{12,8},{16,12},{20,16},{24,20},{28,24},{0,28},{5,1},{9... | collective-permute-start | bytes 466952 | tf_op jit(solution)/shard_map/ppermute | solution.py:422
  65.0 20.0 %collective-permute-start.16 = (bf16[4,152,128]{2,1,0:T(8,128)(2,1)S(1)}, bf16[4,152,128]{2,1,0:T(8,128)(2,1)S(1)}, u32[]{:S(2)}, u32[]{:S(2)}) collective-permute-start(bf16[4,152,128]{2,1,0:T(8,128)(2,1)S(1)} %get-tuple-element.70.refs_3_), channel_id=1, source_target_pairs={{0,32},{32,64},{64,96},{96,128},{128,160},{160,192},{192,224},{224... | collective-permute-start | bytes 466952 | tf_op jit(solution)/shard_map/ppermute | solution.py:421
  66.1 18.9 %collective-permute-start.17 = (bf16[4,152,128]{2,1,0:T(8,128)(2,1)S(1)}, bf16[4,152,128]{2,1,0:T(8,128)(2,1)S(1)}, u32[]{:S(2)}, u32[]{:S(2)}) collective-permute-start(bf16[4,152,128]{2,1,0:T(8,128)(2,1)S(1)} %get-tuple-element.71.refs_2_), channel_id=1, source_target_pairs={{32,0},{64,32},{96,64},{128,96},{160,128},{192,160},{224,192},{0,2... | collective-permute-start | bytes 466952 | tf_op jit(solution)/shard_map/ppermute | solution.py:422
  74.4 16.5 %collective-permute-start.12 = (bf16[8,152,128]{2,1,0:T(8,128)(2,1)S(1)}, bf16[8,152,128]{2,1,0:T(8,128)(2,1)S(1)}, u32[]{:S(2)}, u32[]{:S(2)}) collective-permute-start(bf16[8,152,128]{2,1,0:T(8,128)(2,1)S(1)} %get-tuple-element.65.refs_4_), channel_id=1, source_target_pairs={{0,1},{2,3},{1,0},{3,2},{4,5},{6,7},{5,4},{7,6},{8,9},{10,11},{9,8... | collective-permute-start | bytes 933896 | tf_op jit(solution)/shard_map/ppermute | solution.py:425
  74.9 15.9 %collective-permute-start.13 = (bf16[8,152,128]{2,1,0:T(8,128)(2,1)S(1)}, bf16[8,152,128]{2,1,0:T(8,128)(2,1)S(1)}, u32[]{:S(2)}, u32[]{:S(2)}) collective-permute-start(bf16[8,152,128]{2,1,0:T(8,128)(2,1)S(1)} %get-tuple-element.66.refs_5_), channel_id=1, source_target_pairs={{1,2},{2,1},{5,6},{6,5},{9,10},{10,9},{13,14},{14,13},{17,18},{18,... | collective-permute-start | bytes 933896 | tf_op jit(solution)/shard_map/ppermute | solution.py:425
  84.3 2.9 %collective-permute-start.14 = (bf16[4,152,128]{2,1,0:T(8,128)(2,1)S(1)}, bf16[4,152,128]{2,1,0:T(8,128)(2,1)S(1)}, u32[]{:S(2)}, u32[]{:S(2)}) collective-permute-start(bf16[4,152,128]{2,1,0:T(8,128)(2,1)S(1)} %get-tuple-element.67.refs_7_), channel_id=1, source_target_pairs={{0,4},{4,8},{8,12},{12,16},{16,20},{20,24},{24,28},{28,0},{1,5},{5... | collective-permute-start | bytes 466952 | tf_op jit(solution)/shard_map/ppermute | solution.py:421
  85.0 5.9 %collective-permute-start.15 = (bf16[4,152,128]{2,1,0:T(8,128)(2,1)S(1)}, bf16[4,152,128]{2,1,0:T(8,128)(2,1)S(1)}, u32[]{:S(2)}, u32[]{:S(2)}) collective-permute-start(bf16[4,152,128]{2,1,0:T(8,128)(2,1)S(1)} %get-tuple-element.68.refs_6_), channel_id=1, source_target_pairs={{4,0},{8,4},{12,8},{16,12},{20,16},{24,20},{28,24},{0,28},{5,1},{9... | collective-permute-start | bytes 466952 | tf_op jit(solution)/shard_map/ppermute | solution.py:422

commit v2 on v1

--- a/solution.py
+++ b/solution.py
@@ -19,6 +19,7 @@
 F32 = jnp.float32
 PARAMS = pltpu.CompilerParams(vmem_limit_bytes=20 * 1024 * 1024)
 VMEM = pl.BlockSpec(memory_space=pltpu.VMEM)
+ANY = pl.BlockSpec(memory_space=pl.ANY)
 
 
 def mm(a, b):
@@ -29,11 +30,11 @@
     return lax.dot_general(a, b, (((1,), (1,)), ((), ())), preferred_element_type=F32)
 
 
-def call(kernel, out_shape, operands, flops, scratch=()):
+def call(kernel, out_shape, operands, flops, scratch=(), specs=None):
     return pl.pallas_call(
         kernel,
         out_shape=out_shape,
-        in_specs=[VMEM] * len(operands),
+        in_specs=specs or [VMEM] * len(operands),
         out_specs=jax.tree.map(lambda _: VMEM, out_shape),
         scratch_shapes=list(scratch),
         compiler_params=PARAMS,
@@ -154,7 +155,7 @@
 
 def prepared(block, jacobian, orientation, bt):
     count, group, width, _ = jacobian.shape
-    many = 4
+    many = 8
 
     def kernel(j_ref, o_ref, bt_ref, jp_ref, bc_ref, ball_ref):
         for f in range(group):
@@ -184,20 +185,25 @@
     return call(kernel, [shape, bc, ball], [jacobian, orientation, bt], PREP)
 
 
-def write_permutations(block, o_ref, p_ref):
-    group, modes = o_ref.shape[1:]
-    rows = lax.broadcasted_iota(jnp.int32, (PAD, VARS * modes), 0)
-    eye = (rows == lax.broadcasted_iota(jnp.int32, (PAD, VARS * modes), 1)).astype(BF)
-
-    def elements(step, carry):
-        places = [4 * step + i for i in range(4)]
-        values = [[mm_t(eye, turn).astype(BF) for turn in one_hots(o_ref, e)] for e in places]
-        for e, value in zip(places, values):
-            for f in range(group):
-                p_ref[e, f] = value[f]
-        return carry
-
-    lax.fori_loop(0, block.nx * block.plane // 4, elements, 0)
+def permutations(block, orientation, after):
+    count, group, modes = orientation.shape
+
+    def kernel(o_ref, _, p_ref):
+        rows = lax.broadcasted_iota(jnp.int32, (PAD, VARS * modes), 0)
+        eye = (rows == lax.broadcasted_iota(jnp.int32, (PAD, VARS * modes), 1)).astype(BF)
+
+        def elements(step, carry):
+            places = [4 * step + i for i in range(4)]
+            values = [[mm_t(eye, turn).astype(BF) for turn in one_hots(o_ref, e)] for e in places]
+            for e, value in zip(places, values):
+                for f in range(group):
+                    p_ref[e, f] = value[f]
+            return carry
+
+        lax.fori_loop(0, count // 4, elements, 0)
+
+    shape = jax.ShapeDtypeStruct((count, group, PAD, PAD), BF)
+    return call(kernel, shape, [orientation, after], PREP, specs=[VMEM, ANY])
 
 
 def fill_traces(block, a_ref, bt_ref, t_ref):
@@ -232,13 +238,9 @@
     return mm(jnp.concatenate([bc_ref[f] for f in faces], axis=1), widened(fluxes))
 
 
-def local_residual(block, a, source, jp, bt, ball, orientation=None):
+def local_residual(block, a, source, jp, bt, ball, after):
     def kernel(a_ref, s_ref, j_ref, bt_ref, ball_ref, *refs):
-        if orientation is not None:
-            o_ref, r_ref, p_ref, t_ref = refs
-            write_permutations(block, o_ref, p_ref)
-        else:
-            r_ref, t_ref = refs
+        r_ref, t_ref = refs[len(after) :]
         fill_traces(block, a_ref, bt_ref, t_ref)
         none = jnp.zeros((PAD, block.r), BF)
 
@@ -262,13 +264,10 @@
         block.every_plane(plane)
 
     count = block.nx * block.plane
-    out = [jax.ShapeDtypeStruct((count, block.c, block.r), F32)]
-    operands = [a, source, jp, bt, ball]
-    if orientation is not None:
-        out.append(jax.ShapeDtypeStruct(jp.shape, BF))
-        operands.append(orientation)
     traces = pltpu.VMEM(((block.nx + 2) * block.plane, 6, PAD, block.r), BF)
-    return call(kernel, out, operands, LOCAL, [traces])
+    shape = jax.ShapeDtypeStruct((count, block.c, block.r), F32)
+    operands = [a, source, jp, bt, ball, *after]
+    return call(kernel, shape, operands, LOCAL, [traces], [VMEM] * 5 + [ANY] * len(after))
 
 
 def z_then_y(parts):
@@ -338,8 +337,8 @@
     return a, [*sends[:2], *rest]
 
 
-def local_gradient(block, a, jp, p, bt):
-    def kernel(a_ref, j_ref, p_ref, bt_ref, g_ref, t_ref):
+def local_gradient(block, a, jp, p, bt, after):
+    def kernel(a_ref, j_ref, p_ref, bt_ref, _, g_ref, t_ref):
         fill_traces(block, a_ref, bt_ref, t_ref)
 
         def plane(x, carry):
@@ -362,9 +361,10 @@
     return call(
         kernel,
         jax.ShapeDtypeStruct((count, 8, block.r), F32),
-        [a, jp, p, bt],
+        [a, jp, p, bt, after],
         LOCAL,
         [pltpu.VMEM(((block.nx + 2) * block.plane, 6, PAD, block.r), BF)],
+        [VMEM] * 4 + [ANY],
     )
 
 
@@ -446,12 +446,14 @@
 
     for sweep in range(SWEEPS):
         halos = exchange(sends)
-        last = [turns] if sweep == SWEEPS - 1 else []
-        residual, *rest = local_residual(block, adjoint, source, jp, bt, ball, *last)
+        after = [halos[0]]
+        if sweep == SWEEPS - 1:
+            p = permutations(block, turns, adjoint)
+            after.append(p)
+        residual = local_residual(block, adjoint, source, jp, bt, ball, after)
         adjoint, sends = finish_sweep(block, halos, residual, inverse, jp, bt, bc)
-    (p,) = rest
     halos = exchange(sends)
-    inside = local_gradient(block, adjoint, jp, p, bt)
+    inside = local_gradient(block, adjoint, jp, p, bt, halos[0])
     gradient = finish_gradient(block, halos, sends, inside, jp, p)
     gradient = gradient.reshape(nx, ny, 6, nz, r).transpose(0, 1, 3, 2, 4)
     return (adjoint.reshape(warm_start.shape), gradient)

time: 92.9 us -> 87.2 us (0.939)
  waiting for transfers between devices: 16.3 us -> 5.49 us
  starting transfers between devices: 37 us -> 41.2 us
  local copies, waits for them, and re-layouts: 5.3 us -> 6.94 us
    ppermute x6, waiting for transfers between devices: 14.5 us -> 2.72 us  [exchange(): halos.append(lax.ppermute(sends[2 * d], axis, down))]
    ppermute x6, starting transfers between devices: 12.2 us -> 17.8 us  [exchange(): halos.append(lax.ppermute(sends[2 * d + 1], axis, up))]
    ppermute x6, waiting for transfers between devices: 0.02 us -> 2.76 us  [exchange(): lax.ppermute(sends[4 + part], 'gz', pairs + [(j, i) for i, j in pairs])]
    ppermute x6, starting transfers between devices: 14.5 us -> 12.4 us  [exchange(): halos.append(lax.ppermute(sends[2 * d], axis, down))]
    ppermute x6, waiting for transfers between devices: 1.82 us -> 0.02 us  [exchange(): halos.append(lax.ppermute(sends[2 * d + 1], axis, up))]
    unnamed x16, local copies, waits for them, and re-layouts: 5.26 us -> 6.9 us
    pallas_call x14 -> x15, Pallas kernels: 33.2 us -> 32.3 us  [call(): pl.pallas_call(kernel, out_shape=out_shape, in_specs=specs or [VMEM] * le...]
  transfers between devices with their start and end apart: 18 -> 18, of which waited for: 4 -> 6; matrix products, arithmetic and copies ran while one was open for 4% -> 4% of each run, Pallas kernels for 30% -> 30%
where the time goes in v2:
time: 87.2 us; the launch traced here: 86.9 us
  starting transfers between devices  41.2 us (47%)
  Pallas kernels  32.3 us (37%)
  local copies, waits for them, and re-layouts  6.94 us (8%)
  waiting for transfers between devices  5.49 us (6%)
  between operations  0.94 us (1%)
    pallas_call x15, Pallas kernels, call(): pl.pallas_call(kernel, out_shape=out_shape, in_specs=specs or [VMEM] * le...  32.3 us
    ppermute x6, starting transfers between devices, exchange(): halos.append(lax.ppermute(sends[2 * d + 1], axis, up))  17.8 us
    ppermute x6, starting transfers between devices, exchange(): halos.append(lax.ppermute(sends[2 * d], axis, down))  12.4 us
    ppermute x6, starting transfers between devices, exchange(): lax.ppermute(sends[4 + part], 'gz', pairs + [(j, i) for i, j in pairs])  10.9 us
    unnamed x16, local copies, waits for them, and re-layouts  6.9 us
    ppermute x6, waiting for transfers between devices, exchange(): lax.ppermute(sends[4 + part], 'gz', pairs + [(j, i) for i, j in pairs])  2.76 us
    ppermute x6, waiting for transfers between devices, exchange(): halos.append(lax.ppermute(sends[2 * d], axis, down))  2.72 us
  transfers between devices with their start and end apart: 18, of which 6 were waited for; matrix products, arithmetic and copies ran while one was open for 4% of the time, Pallas kernels for 30%

profile of v2, /device:TPU:57, one launch (start us, length us, event | category | flops | bytes accessed | tf_op | source)
XLA Modules:
  0.0 86.9 jit_solution(8217968731690927750)
XLA Ops:
  0.6 0.0 copy-start.3
  0.6 1.6 %copy.8 = bf16[4,4,2,175,128]{4,3,2,1,0:T(8,128)(2,1)S(1)} copy(bf16[4,4,2,175,128]{4,2,3,1,0:T(2,128)(2,1)} %param.7) | data formatting | bytes 2867200 | tf_op args[1]
  2.2 0.0 copy-done.3
  2.2 0.0 copy-start
  2.3 0.0 copy-start.4
  2.3 0.3 shard_map.77
  2.7 6.1 %collective-permute-start = (bf16[4,152,128]{2,1,0:T(8,128)(2,1)S(1)}, bf16[4,152,128]{2,1,0:T(8,128)(2,1)S(1)}, u32[]{:S(2)}, u32[]{:S(2)}) collective-permute-start(bf16[4,152,128]{2,1,0:T(8,128)(2,1)S(1)} %get-tuple-element.35), channel_id=1, source_target_pairs={{0,32},{32,64},{64,96},{96,128},{128,160},{160,192},{192,224},{224... | collective-permute-start | bytes 466952 | tf_op jit(solution)/shard_map/ppermute | solution.py:421
  8.8 2.3 %collective-permute-start.1 = (bf16[4,152,128]{2,1,0:T(8,128)(2,1)S(1)}, bf16[4,152,128]{2,1,0:T(8,128)(2,1)S(1)}, u32[]{:S(2)}, u32[]{:S(2)}) collective-permute-start(bf16[4,152,128]{2,1,0:T(8,128)(2,1)S(1)} %get-tuple-element.36), channel_id=1, source_target_pairs={{32,0},{64,32},{96,64},{128,96},{160,128},{192,160},{224,192},{0,2... | collective-permute-start | bytes 466952 | tf_op jit(solution)/shard_map/ppermute | solution.py:422
  11.1 1.1 %shard_map.80 = (bf16[4,152,128]{2,1,0:T(8,128)(2,1)S(1)}, bf16[4,152,128]{2,1,0:T(8,128)(2,1)S(1)}, bf16[8,152,128]{2,1,0:T(8,128)(2,1)S(1)}, bf16[8,152,128]{2,1,0:T(8,128)(2,1)S(1)}) custom-call(bf16[32,175,128]{2,1,0:T(8,128)(2,1)S(1)} %bitcast.15, bf16[6,80,175]{2,1,0:T(8,128)(2,1)S(1)} %pad.4.bt_ref.refs_8_.refs_12_), custom_call_target="tpu_custom_call" | custom-call | flops 1000 | tf_op jit(solution)/shard_map/pallas_call | solution.py:34
  12.2 0.8 collective-permute-start.2
  13.0 3.6 %collective-permute-start.3 = (bf16[8,152,128]{2,1,0:T(8,128)(2,1)S(1)}, bf16[8,152,128]{2,1,0:T(8,128)(2,1)S(1)}, u32[]{:S(2)}, u32[]{:S(2)}) collective-permute-start(bf16[8,152,128]{2,1,0:T(8,128)(2,1)S(1)} %get-tuple-element.39), channel_id=1, source_target_pairs={{1,2},{2,1},{5,6},{6,5},{9,10},{10,9},{13,14},{14,13},{17,18},{18,... | collective-permute-start | bytes 933896 | tf_op jit(solution)/shard_map/ppermute | solution.py:425
  16.6 1.6 %collective-permute-start.4 = (bf16[4,152,128]{2,1,0:T(8,128)(2,1)S(1)}, bf16[4,152,128]{2,1,0:T(8,128)(2,1)S(1)}, u32[]{:S(2)}, u32[]{:S(2)}) collective-permute-start(bf16[4,152,128]{2,1,0:T(8,128)(2,1)S(1)} %get-tuple-element.40), channel_id=1, source_target_pairs={{0,4},{4,8},{8,12},{12,16},{16,20},{20,24},{24,28},{28,0},{1,5},{5... | collective-permute-start | bytes 466952 | tf_op jit(solution)/shard_map/ppermute | solution.py:421
  18.3 0.0 copy-done.4
  18.3 0.8 copy.9
  19.1 0.0 copy-start.2
  19.1 3.4 %shard_map.78 = (bf16[32,6,80,80]{3,2,1,0:T(8,128)(2,1)S(1)}, bf16[6,175,128]{2,1,0:T(8,128)(2,1)S(1)}, bf16[175,480]{1,0:T(8,128)(2,1)S(1)}) custom-call(bf16[32,6,75,75]{3,2,1,0:T(8,128)(2,1)S(1)} %bitcast.17, s32[32,6,15]{2,1,0:T(8,128)S(1)} %bitcast.21, bf16[6,80,175]{2,1,0:T(8,128)(2,1)S(1)} %pad.4.bt_ref.refs_8_.refs_12_), custom_call_target="tpu_custom_call" | custom-call | flops 1000 | tf_op jit(solution)/shard_map/pallas_call | solution.py:34
  22.5 0.0 copy-start.1
  22.5 0.2 copy.11
  22.7 1.6 %copy-done.1 = bf16[4,4,2,175,175]{4,2,3,1,0:T(2,128)(2,1)S(1)} copy-done((bf16[4,4,2,175,175]{4,2,3,1,0:T(2,128)(2,1)S(1)}, bf16[4,4,2,175,175]{4,2,3,1,0:T(2,128)(2,1)}, u32[]{:S(2)}) %copy-start.1) | copy-done | bytes 1960024
  24.3 0.5 copy.12
  24.8 0.0 collective-permute-done.low_ref.refs_0_
  24.8 0.2 collective-permute-start.5
  25.0 4.8 %shard_map.81.refs_5_.refs_9_ = f32[32,175,128]{2,1,0:T(8,128)S(1)} custom-call(bf16[32,175,128]{2,1,0:T(8,128)(2,1)S(1)} %bitcast.16, bf16[32,175,128]{2,1,0:T(8,128)(2,1)S(1)} %bitcast.18, bf16[32,6,80,80]{3,2,1,0:T(8,128)(2,1)S(1)} %get-tuple-element.37.j_ref.refs_7_.refs_11_.refs_4_.refs_8_, bf16[6,80,175]{2,1,0:T(8,128)(2,1)S(1)} %pad.4.bt_ref.refs_8_.refs_12_, ...), custom_call_target="tpu_custom_call" | custom-call | flops 1000 | tf_op jit(solution)/shard_map/pallas_call | solution.py:34
  29.8 0.0 collective-permute-done.1.high_ref
  29.8 0.3 shard_map.79.refs_0_
  30.1 0.0 collective-permute-done.4.refs_3_.refs_7_
  30.1 0.6 collective-permute-done.5.refs_4_.refs_8_
  30.7 0.0 collective-permute-done.2.refs_1_.refs_5_
  30.7 0.0 collective-permute-done.3.refs_2_.refs_6_
  30.7 1.8 %shard_map.82 = (bf16[32,175,128]{2,1,0:T(8,128)(2,1)S(1)}, bf16[4,152,128]{2,1,0:T(8,128)(2,1)S(1)}, bf16[4,152,128]{2,1,0:T(8,128)(2,1)S(1)}, bf16[4,152,128]{...) custom-call(bf16[16,80,128]{2,1,0:T(8,128)(2,1)S(1)} %shard_map.79.r, ...), custom_call_target="tpu_custom_call" | custom-call | flops 1000 | tf_op jit(solution)/shard_map/pallas_call | solution.py:34
  32.5 2.6 %collective-permute-start.6 = (bf16[4,152,128]{2,1,0:T(8,128)(2,1)S(1)}, bf16[4,152,128]{2,1,0:T(8,128)(2,1)S(1)}, u32[]{:S(2)}, u32[]{:S(2)}) collective-permute-start(bf16[4,152,128]{2,1,0:T(8,128)(2,1)S(1)} %get-tuple-element.44), channel_id=1, source_target_pairs={{0,32},{32,64},{64,96},{96,128},{128,160},{160,192},{192,224},{224... | collective-permute-start | bytes 466952 | tf_op jit(solution)/shard_map/ppermute | solution.py:421
  35.1 5.0 %collective-permute-start.7 = (bf16[4,152,128]{2,1,0:T(8,128)(2,1)S(1)}, bf16[4,152,128]{2,1,0:T(8,128)(2,1)S(1)}, u32[]{:S(2)}, u32[]{:S(2)}) collective-permute-start(bf16[4,152,128]{2,1,0:T(8,128)(2,1)S(1)} %get-tuple-element.45), channel_id=1, source_target_pairs={{32,0},{64,32},{96,64},{128,96},{160,128},{192,160},{224,192},{0,2... | collective-permute-start | bytes 466952 | tf_op jit(solution)/shard_map/ppermute | solution.py:422
  40.1 1.8 %shard_map.84 = (bf16[32,175,128]{2,1,0:T(8,128)(2,1)S(1)}, bf16[4,152,128]{2,1,0:T(8,128)(2,1)S(1)}, bf16[4,152,128]{2,1,0:T(8,128)(2,1)S(1)}, bf16[8,152,128]{2,1,0:T(8,128)(2,1)S(1)}, bf16[8,152,128]{2,1,0:T(8,128)(2,1)S(1)}) custom-call(bf16[32,175,128]{2,1,0:T(8,128)(2,1)S(1)} %get-tuple-element.46.refs_0_, ...), custom_call_target="tpu_custom_call" | custom-call | flops 1000 | tf_op jit(solution)/shard_map/pallas_call | solution.py:34
  41.9 0.1 collective-permute-start.8
  42.0 3.2 %collective-permute-start.9 = (bf16[8,152,128]{2,1,0:T(8,128)(2,1)S(1)}, bf16[8,152,128]{2,1,0:T(8,128)(2,1)S(1)}, u32[]{:S(2)}, u32[]{:S(2)}) collective-permute-start(bf16[8,152,128]{2,1,0:T(8,128)(2,1)S(1)} %get-tuple-element.52), channel_id=1, source_target_pairs={{1,2},{2,1},{5,6},{6,5},{9,10},{10,9},{13,14},{14,13},{17,18},{18,... | collective-permute-start | bytes 933896 | tf_op jit(solution)/shard_map/ppermute | solution.py:425
  45.2 1.7 %collective-permute-start.10 = (bf16[4,152,128]{2,1,0:T(8,128)(2,1)S(1)}, bf16[4,152,128]{2,1,0:T(8,128)(2,1)S(1)}, u32[]{:S(2)}, u32[]{:S(2)}) collective-permute-start(bf16[4,152,128]{2,1,0:T(8,128)(2,1)S(1)} %get-tuple-element.53), channel_id=1, source_target_pairs={{0,4},{4,8},{8,12},{12,16},{16,20},{20,24},{24,28},{28,0},{1,5},{5... | collective-permute-start | bytes 466952 | tf_op jit(solution)/shard_map/ppermute | solution.py:421
  46.9 3.9 %shard_map.85.refs_1_.p_ref.refs_5_.refs_9_ = bf16[32,6,80,80]{3,2,1,0:T(8,128)(2,1)S(1)} custom-call(s32[32,6,15]{2,1,0:T(8,128)S(1)} %bitcast.22, bf16[32,175,128]{2,1,0:T(8,128)(2,1)S(1)} %get-tuple-element.55._.a_ref), custom_call_target="tpu_custom_call" | custom-call | flops 1000 | tf_op jit(solution)/shard_map/pallas_call | solution.py:34
  50.9 0.0 collective-permute-done.6.low_ref.refs_0_
  50.9 0.2 collective-permute-start.11
  51.1 4.8 %shard_map.86.refs_5_.refs_9_ = f32[32,175,128]{2,1,0:T(8,128)S(1)} custom-call(bf16[32,175,128]{2,1,0:T(8,128)(2,1)S(1)} %get-tuple-element.55._.a_ref, bf16[32,175,128]{2,1,0:T(8,128)(2,1)S(1)} %bitcast.19, bf16[32,6,80,80]{3,2,1,0:T(8,128)(2,1)S(1)} %get-tuple-element.37.j_ref.refs_7_.refs_11_.refs_4_.refs_8_, ...), custom_call_target="tpu_custom_call" | custom-call | flops 1000 | tf_op jit(solution)/shard_map/pallas_call | solution.py:34
  55.8 0.0 collective-permute-done.7.high_ref
  55.8 0.3 shard_map.83.refs_0_
  56.1 0.0 collective-permute-done.10.refs_3_.refs_7_
  56.1 0.6 collective-permute-done.11.refs_4_.refs_8_
  56.8 0.0 collective-permute-done.8.refs_1_.refs_5_
  56.8 0.6 collective-permute-done.9.refs_2_.refs_6_
  57.3 1.8 %shard_map.87 = (bf16[32,175,128]{2,1,0:T(8,128)(2,1)S(1)}, bf16[4,152,128]{2,1,0:T(8,128)(2,1)S(1)}, bf16[4,152,128]{2,1,0:T(8,128)(2,1)S(1)}, bf16[4,152,128]{...) custom-call(bf16[16,80,128]{2,1,0:T(8,128)(2,1)S(1)} %shard_map.83.r, ...), custom_call_target="tpu_custom_call" | custom-call | flops 1000 | tf_op jit(solution)/shard_map/pallas_call | solution.py:34
  59.2 2.8 %collective-permute-start.16 = (bf16[4,152,128]{2,1,0:T(8,128)(2,1)S(1)}, bf16[4,152,128]{2,1,0:T(8,128)(2,1)S(1)}, u32[]{:S(2)}, u32[]{:S(2)}) collective-permute-start(bf16[4,152,128]{2,1,0:T(8,128)(2,1)S(1)} %get-tuple-element.66.refs_3_), channel_id=1, source_target_pairs={{0,32},{32,64},{64,96},{96,128},{128,160},{160,192},{192,224},{224... | collective-permute-start | bytes 466952 | tf_op jit(solution)/shard_map/ppermute | solution.py:421
  61.9 4.8 %collective-permute-start.17 = (bf16[4,152,128]{2,1,0:T(8,128)(2,1)S(1)}, bf16[4,152,128]{2,1,0:T(8,128)(2,1)S(1)}, u32[]{:S(2)}, u32[]{:S(2)}) collective-permute-start(bf16[4,152,128]{2,1,0:T(8,128)(2,1)S(1)} %get-tuple-element.67.refs_2_), channel_id=1, source_target_pairs={{32,0},{64,32},{96,64},{128,96},{160,128},{192,160},{224,192},{0,2... | collective-permute-start | bytes 466952 | tf_op jit(solution)/shard_map/ppermute | solution.py:422
  66.7 1.8 %shard_map.88 = (bf16[32,175,128]{2,1,0:T(8,128)(2,1)S(1)}, bf16[4,152,128]{2,1,0:T(8,128)(2,1)S(1)}, bf16[4,152,128]{2,1,0:T(8,128)(2,1)S(1)}, bf16[8,152,128]{2,1,0:T(8,128)(2,1)S(1)}, bf16[8,152,128]{2,1,0:T(8,128)(2,1)S(1)}) custom-call(bf16[32,175,128]{2,1,0:T(8,128)(2,1)S(1)} %get-tuple-element.56.refs_0_, ...), custom_call_target="tpu_custom_call" | custom-call | flops 1000 | tf_op jit(solution)/shard_map/pallas_call | solution.py:34
  68.5 0.1 collective-permute-start.12
  68.6 3.1 %collective-permute-start.13 = (bf16[8,152,128]{2,1,0:T(8,128)(2,1)S(1)}, bf16[8,152,128]{2,1,0:T(8,128)(2,1)S(1)}, u32[]{:S(2)}, u32[]{:S(2)}) collective-permute-start(bf16[8,152,128]{2,1,0:T(8,128)(2,1)S(1)} %get-tuple-element.63.refs_5_), channel_id=1, source_target_pairs={{1,2},{2,1},{5,6},{6,5},{9,10},{10,9},{13,14},{14,13},{17,18},{18,... | collective-permute-start | bytes 933896 | tf_op jit(solution)/shard_map/ppermute | solution.py:425
  71.8 3.0 %collective-permute-start.14 = (bf16[4,152,128]{2,1,0:T(8,128)(2,1)S(1)}, bf16[4,152,128]{2,1,0:T(8,128)(2,1)S(1)}, u32[]{:S(2)}, u32[]{:S(2)}) collective-permute-start(bf16[4,152,128]{2,1,0:T(8,128)(2,1)S(1)} %get-tuple-element.64.refs_7_), channel_id=1, source_target_pairs={{0,4},{4,8},{8,12},{12,16},{16,20},{20,24},{24,28},{28,0},{1,5},{5... | collective-permute-start | bytes 466952 | tf_op jit(solution)/shard_map/ppermute | solution.py:421
  74.8 2.2 %copy.13 = bf16[4,4,2,175,128]{4,2,3,1,0:T(2,128)(2,1)} copy(bf16[4,4,2,175,128]{4,3,2,1,0:T(8,128)(2,1)S(1)} %bitcast.20) | data formatting | bytes 2867200
  77.0 0.0 collective-permute-done.16._.refs_0_
  77.0 0.0 collective-permute-start.15
  77.0 4.0 %shard_map.89.refs_6_ = f32[32,8,128]{2,1,0:T(8,128)S(1)} custom-call(bf16[32,175,128]{2,1,0:T(8,128)(2,1)S(1)} %get-tuple-element.61.a_ref, bf16[32,6,80,80]{3,2,1,0:T(8,128)(2,1)S(1)} %get-tuple-element.37.j_ref.refs_7_.refs_11_.refs_4_.refs_8_, bf16[32,6,80,80]{3,2,1,0:T(8,128)(2,1)S(1)} %shard_map.85.refs_1_.p_ref.refs_5_.refs_9_, ...), custom_call_target="tpu_custom_call" | custom-call | flops 1000 | tf_op jit(solution)/shard_map/pallas_call | solution.py:34
  80.9 0.0 collective-permute-done.17.refs_1_
  80.9 0.3 shard_map.90.refs_10_
  81.3 0.0 collective-permute-done.14.refs_2_
  81.3 1.5 %collective-permute-done.15.refs_3_ = bf16[4,152,128]{2,1,0:T(8,128)(2,1)S(1)} collective-permute-done((bf16[4,152,128]{2,1,0:T(8,128)(2,1)S(1)}, bf16[4,152,128]{2,1,0:T(8,128)(2,1)S(1)}, u32[]{:S(2)}, u32[]{:S(2)}) %collective-permute-start.15) | collective-permute-done | bytes 155680 | tf_op jit(solution)/shard_map/ppermute | solution.py:422
  82.8 0.5 collective-permute-done.12.refs_0_
  83.3 1.7 %collective-permute-done.13.refs_1_ = bf16[8,152,128]{2,1,0:T(8,128)(2,1)S(1)} collective-permute-done((bf16[8,152,128]{2,1,0:T(8,128)(2,1)S(1)}, bf16[8,152,128]{2,1,0:T(8,128)(2,1)S(1)}, u32[]{:S(2)}, u32[]{:S(2)}) %collective-permute-start.13) | collective-permute-done | bytes 311328 | tf_op jit(solution)/shard_map/ppermute | solution.py:425
  85.0 1.9 %shard_map.91 = f32[16,6,2,128]{3,2,1,0:T(2,128)} custom-call(bf16[8,152,128]{2,1,0:T(8,128)(2,1)S(1)} %collective-permute-done.12.refs_0_, bf16[8,152,128]{2,1,0:T(8,128)(2,1)S(1)} %collective-permute-done.13.refs_1_, bf16[4,152,128]{2,1,0:T(8,128)(2,1)S(1)} %collective-permute-done.14.refs_2_, bf16[4,152,128]{2,1,0:T(8,128)(2,1)S(1)} %collective-permute-done.15.refs_3_, ...), custom_call_target="tpu_custom_call" | custom-call | flops 1000 | tf_op jit(solution)/shard_map/pallas_call | solution.py:34
  (4 shorter events, 0.1 us)
Async XLA Ops:
  0.6 1.6 %copy-start.3 = (bf16[6,175,75]{1,2,0:T(8,128)(2,1)S(1)}, bf16[6,175,75]{1,2,0:T(8,128)(2,1)}, u32[]{:S(2)}) copy-start(bf16[6,175,75]{1,2,0:T(8,128)(2,1)} %param.10) | copy-start | bytes 472504
  2.2 16.1 %copy-start = (bf16[4,4,2,6,75,75]{5,2,4,3,1,0:T(2,128)(2,1)S(1)}, bf16[4,4,2,6,75,75]{5,2,4,3,1,0:T(2,128)(2,1)}, u32[]{:S(2)}) copy-start(bf16[4,4,2,6,75,75]{5,2,4,3,1,0:T(2,128)(2,1)} %param.9) | copy-start | bytes 6480004
  2.3 16.0 %copy-start.4 = (s32[4,4,2,6,15]{4,2,3,1,0:T(2,128)S(1)}, s32[4,4,2,6,15]{4,2,3,1,0:T(2,128)}, u32[]{:S(2)}) copy-start(s32[4,4,2,6,15]{4,2,3,1,0:T(2,128)} %param.11) | copy-start | bytes 34564
  2.7 22.2 %collective-permute-start = (bf16[4,152,128]{2,1,0:T(8,128)(2,1)S(1)}, bf16[4,152,128]{2,1,0:T(8,128)(2,1)S(1)}, u32[]{:S(2)}, u32[]{:S(2)}) collective-permute-start(bf16[4,152,128]{2,1,0:T(8,128)(2,1)S(1)} %get-tuple-element.35), channel_id=1, source_target_pairs={{0,32},{32,64},{64,96},{96,128},{128,160},{160,192},{192,224},{224... | collective-permute-start | bytes 466952 | tf_op jit(solution)/shard_map/ppermute | solution.py:421
  8.8 21.0 %collective-permute-start.1 = (bf16[4,152,128]{2,1,0:T(8,128)(2,1)S(1)}, bf16[4,152,128]{2,1,0:T(8,128)(2,1)S(1)}, u32[]{:S(2)}, u32[]{:S(2)}) collective-permute-start(bf16[4,152,128]{2,1,0:T(8,128)(2,1)S(1)} %get-tuple-element.36), channel_id=1, source_target_pairs={{32,0},{64,32},{96,64},{128,96},{160,128},{192,160},{224,192},{0,2... | collective-permute-start | bytes 466952 | tf_op jit(solution)/shard_map/ppermute | solution.py:422
  12.2 18.5 %collective-permute-start.2 = (bf16[8,152,128]{2,1,0:T(8,128)(2,1)S(1)}, bf16[8,152,128]{2,1,0:T(8,128)(2,1)S(1)}, u32[]{:S(2)}, u32[]{:S(2)}) collective-permute-start(bf16[8,152,128]{2,1,0:T(8,128)(2,1)S(1)} %get-tuple-element.38), channel_id=1, source_target_pairs={{0,1},{2,3},{1,0},{3,2},{4,5},{6,7},{5,4},{7,6},{8,9},{10,11},{9,8... | collective-permute-start | bytes 933896 | tf_op jit(solution)/shard_map/ppermute | solution.py:425
  13.0 17.7 %collective-permute-start.3 = (bf16[8,152,128]{2,1,0:T(8,128)(2,1)S(1)}, bf16[8,152,128]{2,1,0:T(8,128)(2,1)S(1)}, u32[]{:S(2)}, u32[]{:S(2)}) collective-permute-start(bf16[8,152,128]{2,1,0:T(8,128)(2,1)S(1)} %get-tuple-element.39), channel_id=1, source_target_pairs={{1,2},{2,1},{5,6},{6,5},{9,10},{10,9},{13,14},{14,13},{17,18},{18,... | collective-permute-start | bytes 933896 | tf_op jit(solution)/shard_map/ppermute | solution.py:425
  16.6 13.5 %collective-permute-start.4 = (bf16[4,152,128]{2,1,0:T(8,128)(2,1)S(1)}, bf16[4,152,128]{2,1,0:T(8,128)(2,1)S(1)}, u32[]{:S(2)}, u32[]{:S(2)}) collective-permute-start(bf16[4,152,128]{2,1,0:T(8,128)(2,1)S(1)} %get-tuple-element.40), channel_id=1, source_target_pairs={{0,4},{4,8},{8,12},{12,16},{16,20},{20,24},{24,28},{28,0},{1,5},{5... | collective-permute-start | bytes 466952 | tf_op jit(solution)/shard_map/ppermute | solution.py:421
  19.1 3.4 %copy-start.2 = (bf16[4,4,2,175,128]{4,2,3,1,0:T(2,128)(2,1)S(1)}, bf16[4,4,2,175,128]{4,2,3,1,0:T(2,128)(2,1)}, u32[]{:S(2)}) copy-start(bf16[4,4,2,175,128]{4,2,3,1,0:T(2,128)(2,1)} %param.6) | copy-start | bytes 4300804
  22.5 1.8 %copy-start.1 = (bf16[4,4,2,175,175]{4,2,3,1,0:T(2,128)(2,1)S(1)}, bf16[4,4,2,175,175]{4,2,3,1,0:T(2,128)(2,1)}, u32[]{:S(2)}) copy-start(bf16[4,4,2,175,175]{4,2,3,1,0:T(2,128)(2,1)} %param.8) | copy-start | bytes 5880004
  24.8 5.9 %collective-permute-start.5 = (bf16[4,152,128]{2,1,0:T(8,128)(2,1)S(1)}, bf16[4,152,128]{2,1,0:T(8,128)(2,1)S(1)}, u32[]{:S(2)}, u32[]{:S(2)}) collective-permute-start(bf16[4,152,128]{2,1,0:T(8,128)(2,1)S(1)} %get-tuple-element.41), channel_id=1, source_target_pairs={{4,0},{8,4},{12,8},{16,12},{20,16},{24,20},{28,24},{0,28},{5,1},{9... | collective-permute-start | bytes 466952 | tf_op jit(solution)/shard_map/ppermute | solution.py:422
  32.5 18.3 %collective-permute-start.6 = (bf16[4,152,128]{2,1,0:T(8,128)(2,1)S(1)}, bf16[4,152,128]{2,1,0:T(8,128)(2,1)S(1)}, u32[]{:S(2)}, u32[]{:S(2)}) collective-permute-start(bf16[4,152,128]{2,1,0:T(8,128)(2,1)S(1)} %get-tuple-element.44), channel_id=1, source_target_pairs={{0,32},{32,64},{64,96},{96,128},{128,160},{160,192},{192,224},{224... | collective-permute-start | bytes 466952 | tf_op jit(solution)/shard_map/ppermute | solution.py:421
  35.1 20.7 %collective-permute-start.7 = (bf16[4,152,128]{2,1,0:T(8,128)(2,1)S(1)}, bf16[4,152,128]{2,1,0:T(8,128)(2,1)S(1)}, u32[]{:S(2)}, u32[]{:S(2)}) collective-permute-start(bf16[4,152,128]{2,1,0:T(8,128)(2,1)S(1)} %get-tuple-element.45), channel_id=1, source_target_pairs={{32,0},{64,32},{96,64},{128,96},{160,128},{192,160},{224,192},{0,2... | collective-permute-start | bytes 466952 | tf_op jit(solution)/shard_map/ppermute | solution.py:422
  41.9 14.9 %collective-permute-start.8 = (bf16[8,152,128]{2,1,0:T(8,128)(2,1)S(1)}, bf16[8,152,128]{2,1,0:T(8,128)(2,1)S(1)}, u32[]{:S(2)}, u32[]{:S(2)}) collective-permute-start(bf16[8,152,128]{2,1,0:T(8,128)(2,1)S(1)} %get-tuple-element.51), channel_id=1, source_target_pairs={{0,1},{2,3},{1,0},{3,2},{4,5},{6,7},{5,4},{7,6},{8,9},{10,11},{9,8... | collective-permute-start | bytes 933896 | tf_op jit(solution)/shard_map/ppermute | solution.py:425
  42.0 15.3 %collective-permute-start.9 = (bf16[8,152,128]{2,1,0:T(8,128)(2,1)S(1)}, bf16[8,152,128]{2,1,0:T(8,128)(2,1)S(1)}, u32[]{:S(2)}, u32[]{:S(2)}) collective-permute-start(bf16[8,152,128]{2,1,0:T(8,128)(2,1)S(1)} %get-tuple-element.52), channel_id=1, source_target_pairs={{1,2},{2,1},{5,6},{6,5},{9,10},{10,9},{13,14},{14,13},{17,18},{18,... | collective-permute-start | bytes 933896 | tf_op jit(solution)/shard_map/ppermute | solution.py:425
  45.2 10.9 %collective-permute-start.10 = (bf16[4,152,128]{2,1,0:T(8,128)(2,1)S(1)}, bf16[4,152,128]{2,1,0:T(8,128)(2,1)S(1)}, u32[]{:S(2)}, u32[]{:S(2)}) collective-permute-start(bf16[4,152,128]{2,1,0:T(8,128)(2,1)S(1)} %get-tuple-element.53), channel_id=1, source_target_pairs={{0,4},{4,8},{8,12},{12,16},{16,20},{20,24},{24,28},{28,0},{1,5},{5... | collective-permute-start | bytes 466952 | tf_op jit(solution)/shard_map/ppermute | solution.py:421
  50.9 5.9 %collective-permute-start.11 = (bf16[4,152,128]{2,1,0:T(8,128)(2,1)S(1)}, bf16[4,152,128]{2,1,0:T(8,128)(2,1)S(1)}, u32[]{:S(2)}, u32[]{:S(2)}) collective-permute-start(bf16[4,152,128]{2,1,0:T(8,128)(2,1)S(1)} %get-tuple-element.54), channel_id=1, source_target_pairs={{4,0},{8,4},{12,8},{16,12},{20,16},{24,20},{28,24},{0,28},{5,1},{9... | collective-permute-start | bytes 466952 | tf_op jit(solution)/shard_map/ppermute | solution.py:422
  59.2 17.8 %collective-permute-start.16 = (bf16[4,152,128]{2,1,0:T(8,128)(2,1)S(1)}, bf16[4,152,128]{2,1,0:T(8,128)(2,1)S(1)}, u32[]{:S(2)}, u32[]{:S(2)}) collective-permute-start(bf16[4,152,128]{2,1,0:T(8,128)(2,1)S(1)} %get-tuple-element.66.refs_3_), channel_id=1, source_target_pairs={{0,32},{32,64},{64,96},{96,128},{128,160},{160,192},{192,224},{224... | collective-permute-start | bytes 466952 | tf_op jit(solution)/shard_map/ppermute | solution.py:421
  61.9 19.0 %collective-permute-start.17 = (bf16[4,152,128]{2,1,0:T(8,128)(2,1)S(1)}, bf16[4,152,128]{2,1,0:T(8,128)(2,1)S(1)}, u32[]{:S(2)}, u32[]{:S(2)}) collective-permute-start(bf16[4,152,128]{2,1,0:T(8,128)(2,1)S(1)} %get-tuple-element.67.refs_2_), channel_id=1, source_target_pairs={{32,0},{64,32},{96,64},{128,96},{160,128},{192,160},{224,192},{0,2... | collective-permute-start | bytes 466952 | tf_op jit(solution)/shard_map/ppermute | solution.py:422
  68.5 14.8 %collective-permute-start.12 = (bf16[8,152,128]{2,1,0:T(8,128)(2,1)S(1)}, bf16[8,152,128]{2,1,0:T(8,128)(2,1)S(1)}, u32[]{:S(2)}, u32[]{:S(2)}) collective-permute-start(bf16[8,152,128]{2,1,0:T(8,128)(2,1)S(1)} %get-tuple-element.62.refs_4_), channel_id=1, source_target_pairs={{0,1},{2,3},{1,0},{3,2},{4,5},{6,7},{5,4},{7,6},{8,9},{10,11},{9,8... | collective-permute-start | bytes 933896 | tf_op jit(solution)/shard_map/ppermute | solution.py:425
  68.6 16.4 %collective-permute-start.13 = (bf16[8,152,128]{2,1,0:T(8,128)(2,1)S(1)}, bf16[8,152,128]{2,1,0:T(8,128)(2,1)S(1)}, u32[]{:S(2)}, u32[]{:S(2)}) collective-permute-start(bf16[8,152,128]{2,1,0:T(8,128)(2,1)S(1)} %get-tuple-element.63.refs_5_), channel_id=1, source_target_pairs={{1,2},{2,1},{5,6},{6,5},{9,10},{10,9},{13,14},{14,13},{17,18},{18,... | collective-permute-start | bytes 933896 | tf_op jit(solution)/shard_map/ppermute | solution.py:425
  71.8 9.5 %collective-permute-start.14 = (bf16[4,152,128]{2,1,0:T(8,128)(2,1)S(1)}, bf16[4,152,128]{2,1,0:T(8,128)(2,1)S(1)}, u32[]{:S(2)}, u32[]{:S(2)}) collective-permute-start(bf16[4,152,128]{2,1,0:T(8,128)(2,1)S(1)} %get-tuple-element.64.refs_7_), channel_id=1, source_target_pairs={{0,4},{4,8},{8,12},{12,16},{16,20},{20,24},{24,28},{28,0},{1,5},{5... | collective-permute-start | bytes 466952 | tf_op jit(solution)/shard_map/ppermute | solution.py:421
  77.0 5.9 %collective-permute-start.15 = (bf16[4,152,128]{2,1,0:T(8,128)(2,1)S(1)}, bf16[4,152,128]{2,1,0:T(8,128)(2,1)S(1)}, u32[]{:S(2)}, u32[]{:S(2)}) collective-permute-start(bf16[4,152,128]{2,1,0:T(8,128)(2,1)S(1)} %get-tuple-element.65.refs_6_), channel_id=1, source_target_pairs={{4,0},{8,4},{12,8},{16,12},{20,16},{24,20},{28,24},{0,28},{5,1},{9... | collective-permute-start | bytes 466952 | tf_op jit(solution)/shard_map/ppermute | solution.py:422

commit v3 on v2

--- a/solution.py
+++ b/solution.py
@@ -17,9 +17,10 @@
 LANES = 128
 BF = jnp.bfloat16
 F32 = jnp.float32
-PARAMS = pltpu.CompilerParams(vmem_limit_bytes=20 * 1024 * 1024)
+MIB = 1024 * 1024
 VMEM = pl.BlockSpec(memory_space=pltpu.VMEM)
 ANY = pl.BlockSpec(memory_space=pl.ANY)
+HBM = pl.BlockSpec(memory_space=pltpu.HBM)
 
 
 def mm(a, b):
@@ -30,14 +31,14 @@
     return lax.dot_general(a, b, (((1,), (1,)), ((), ())), preferred_element_type=F32)
 
 
-def call(kernel, out_shape, operands, flops, scratch=(), specs=None):
+def call(kernel, out_shape, operands, flops, scratch=(), specs=None, vmem=12):
     return pl.pallas_call(
         kernel,
         out_shape=out_shape,
         in_specs=specs or [VMEM] * len(operands),
         out_specs=jax.tree.map(lambda _: VMEM, out_shape),
         scratch_shapes=list(scratch),
-        compiler_params=PARAMS,
+        compiler_params=pltpu.CompilerParams(vmem_limit_bytes=vmem * MIB),
         cost_estimate=pl.CostEstimate(flops=flops, bytes_accessed=0, transcendentals=0),
     )(*operands)
 
@@ -80,15 +81,20 @@
             for z in range(self.nz)
         ]
 
+    def of_planes(self, planes):
+        return [(e, x, y, z, faces) for x, side in planes for e, y, z, faces in self.work(x, side)]
+
+    def two_at_once(self, visit):
+        lax.fori_loop(0, self.nx // 2, lambda i, carry: (visit([2 * i, 2 * i + 1]), carry)[1], 0)
+
     def every_plane(self, visit):
         lax.fori_loop(0, self.nx, lambda x, carry: (visit(x), carry)[1], 0)
 
-    def inner_planes(self, visit):
-        lax.fori_loop(1, self.nx - 1, lambda x, carry: (visit(x, None), carry)[1], 0)
-
-    def end_planes(self, visit):
-        visit(0, 0)
-        visit(self.nx - 1, 1)
+    def inner_planes(self):
+        return [(x, None) for x in range(1, self.nx - 1)]
+
+    def end_planes(self):
+        return [(0, 0), (self.nx - 1, 1)]
 
     def near_local(self, face, x, y, z):
         dx, dy, dz = [(-1, 0, 0), (1, 0, 0), (0, -1, 0), (0, 1, 0), (0, 0, -1), (0, 0, 1)][face]
@@ -106,42 +112,70 @@
     return jnp.where(even_in_z(), *((second, first) if f == 4 else (first, second)))
 
 
-def send_traces(block, x, work, values, bt, sends):
-    traces = [
-        mm(jnp.concatenate([bt[f] for f in faces], axis=0), a).astype(BF)
-        for (_, _, _, faces), a in zip(work, values)
-    ]
-    sides = {}
-    for (_, y, z, faces), t in zip(work, traces):
+def send_traces(block, work, values, bt, sends):
+    traces = [mm(jnp.concatenate([bt[f] for f in w[4]], axis=0), a).astype(BF) for w, a in zip(work, values)]
+    low = None
+    for (_, x, y, z, faces), t in zip(work, traces):
         for i, f in enumerate(faces):
             piece = t[i * PAD : i * PAD + PAIR]
             if f < 4:
                 sends[f][block.slot(f, x, y, z)] = piece
+            elif f == 4:
+                low = piece
             else:
-                sides[f, y] = piece
-    for y in sorted({y for _, y in sides}):
-        place, low, high = block.slot(4, x, y, 0), sides[4, y], sides[5, y]
-        sends[4][place] = jnp.where(even_in_z(), high, low)
-        sends[5][place] = jnp.where(even_in_z(), low, high)
-
-
-def first_sends(block, a, bt):
-    def along_x(a_ref, bt_ref, *sends):
-        def visit(x, side):
-            work = [(e, y, z, [side]) for e, y, z, _ in block.work(x, None)]
-            send_traces(block, x, work, [a_ref[w[0]] for w in work], bt_ref, sends)
-
-        block.end_planes(visit)
+                sends[4][block.slot(4, x, y, z)] = jnp.where(even_in_z(), piece, low)
+                sends[5][block.slot(4, x, y, z)] = jnp.where(even_in_z(), low, piece)
+
+
+def first_sends(block, warm_start, a, trace_basis, bt):
+    width = trace_basis.shape[-1]
+    half = block.ny
+
+    def along_x(w_ref, b_ref, low_ref, high_ref, w_buf, b_buf, sems):
+        copies = [
+            pltpu.make_async_copy(b_ref.at[pl.ds(0, 2)], b_buf, sems.at[0]),
+            pltpu.make_async_copy(w_ref.at[pl.ds(0, half)], w_buf.at[pl.ds(0, half)], sems.at[1]),
+            pltpu.make_async_copy(
+                w_ref.at[pl.ds((block.nx - 1) * half, half)], w_buf.at[pl.ds(half, half)], sems.at[2]
+            ),
+        ]
+        for copy in copies:
+            copy.start()
+        rows = lax.broadcasted_iota(jnp.int32, (block.c, block.nz * block.c), 0)
+        cols = lax.broadcasted_iota(jnp.int32, (block.c, block.nz * block.c), 1)
+        spread = [(cols == block.nz * rows + z).astype(BF) for z in range(block.nz)]
+        none = jnp.zeros((PAD - width, block.c), BF)
+        copies[0].wait()
+        basis = [jnp.concatenate([b_buf[side], none], axis=0) for side in range(2)]
+        wide = [
+            jnp.concatenate([mm(basis[side], spread[z]).astype(BF) for z in range(block.nz)], axis=0)
+            for side in range(2)
+        ]
+        for side, out_ref in enumerate((low_ref, high_ref)):
+            copies[1 + side].wait()
+            columns = [w_buf[side * half + y].reshape(block.nz * block.c, block.r) for y in range(half)]
+            traces = [mm(wide[side], column).astype(BF) for column in columns]
+            for y, t in enumerate(traces):
+                for z in range(block.nz):
+                    out_ref[block.slot(side, 0, y, z)] = t[z * PAD : z * PAD + PAIR]
 
     def others(a_ref, bt_ref, *sends):
-        def visit(x):
-            work = block.work(x, None)
-            send_traces(block, x, work, [a_ref[w[0]] for w in work], bt_ref, (None, None) + sends)
-
-        block.every_plane(visit)
-
+        def visit(planes):
+            work = block.of_planes([(x, None) for x in planes])
+            send_traces(block, work, [a_ref[w[0]] for w in work], bt_ref, (None, None) + sends)
+
+        block.two_at_once(visit)
+
+    nx, ny, nz, c, r = warm_start.shape
+    columns = warm_start.transpose(0, 1, 3, 2, 4).reshape(nx * ny, c, nz, r)
     shapes = block.send_shapes()
-    first = call(along_x, shapes[:2], [a, bt], FIRST)
+    scratch = [
+        pltpu.VMEM((2 * ny, c, nz, r), BF),
+        pltpu.VMEM((2, width, c), BF),
+        pltpu.SemaphoreType.DMA((3,)),
+    ]
+    raw = [pltpu.with_memory_space_constraint(v, pltpu.HBM) for v in (columns, trace_basis.transpose(0, 2, 1))]
+    first = call(along_x, shapes[:2], raw, FIRST, scratch, [HBM, HBM])
     return [*first, *call(others, shapes[2:], [a, bt], SECOND)]
 
 
@@ -193,14 +227,14 @@
         eye = (rows == lax.broadcasted_iota(jnp.int32, (PAD, VARS * modes), 1)).astype(BF)
 
         def elements(step, carry):
-            places = [4 * step + i for i in range(4)]
+            places = [8 * step + i for i in range(8)]
             values = [[mm_t(eye, turn).astype(BF) for turn in one_hots(o_ref, e)] for e in places]
             for e, value in zip(places, values):
                 for f in range(group):
                     p_ref[e, f] = value[f]
             return carry
 
-        lax.fori_loop(0, count // 4, elements, 0)
+        lax.fori_loop(0, count // 8, elements, 0)
 
     shape = jax.ShapeDtypeStruct((count, group, PAD, PAD), BF)
     return call(kernel, shape, [orientation, after], PREP, specs=[VMEM, ANY])
@@ -244,24 +278,35 @@
         fill_traces(block, a_ref, bt_ref, t_ref)
         none = jnp.zeros((PAD, block.r), BF)
 
-        def plane(x):
-            work = [(e, y, z, local_faces(block, y, z)) for e, y, z, _ in block.work(x, None)]
-            fluxes = [
-                [mm(j_ref[e, f], t_ref[block.near_local(f, x, y, z)]).astype(BF) for f in faces]
-                for e, y, z, faces in work
+        def near_fluxes(j_ref, e, x, y, z, faces):
+            fluxes = []
+            for i in range(0, len(faces), 2):
+                some = faces[i : i + 2]
+                near = jnp.concatenate([t_ref[block.near_local(f, x, y, z)] for f in some], axis=1)
+                both = mm(jnp.concatenate([j_ref[e, f] for f in some], axis=0), near).astype(BF)
+                for k in range(len(some)):
+                    fluxes.append(both[k * PAD : (k + 1) * PAD, k * block.r : (k + 1) * block.r])
+            return fluxes
+
+        def planes(step, carry):
+            work = [
+                (e, x, y, z, local_faces(block, y, z))
+                for x in (2 * step, 2 * step + 1)
+                for e, y, z, _ in block.work(x, None)
             ]
-            full = [
-                jnp.concatenate([dict(zip(w[3], flux)).get(f, none) for f in range(6)], axis=0)
-                for w, flux in zip(work, fluxes)
-            ]
+            full = []
+            for e, x, y, z, faces in work:
+                fluxes = dict(zip(faces, near_fluxes(j_ref, e, x, y, z, faces)))
+                full.append(jnp.concatenate([fluxes.get(f, none) for f in range(6)], axis=0))
             rest = []
             for i in range(0, len(work), 2):
                 both = mm(ball_ref[...], jnp.concatenate(full[i : i + 2], axis=1))
                 rest += [both[:, : block.r], both[:, block.r :]]
             for w, value in zip(work, rest):
                 r_ref[w[0]] = s_ref[w[0]].astype(F32) - value
-
-        block.every_plane(plane)
+            return carry
+
+        lax.fori_loop(0, block.nx // 2, planes, 0)
 
     count = block.nx * block.plane
     traces = pltpu.VMEM(((block.nx + 2) * block.plane, 6, PAD, block.r), BF)
@@ -281,60 +326,57 @@
 def x_fluxes(block, halos, jp):
     def kernel(low_ref, high_ref, j_ref, out_ref):
         near = (low_ref, high_ref)
-
-        def visit(x, side):
-            work = block.work(x, None)
-            fluxes = [
-                mm(j_ref[e, side, :, :PAIR], near[side][block.slot(side, x, y, z)]).astype(BF)
-                for e, y, z, _ in work
-            ]
-            for i, flux in enumerate(fluxes):
-                out_ref[side * block.plane + i] = flux
-
-        block.end_planes(visit)
+        fluxes = [
+            mm(j_ref[e, side, :, :PAIR], near[side][block.slot(side, x, y, z)]).astype(BF)
+            for x, side in block.end_planes()
+            for e, y, z, _ in block.work(x, None)
+        ]
+        for i, flux in enumerate(fluxes):
+            out_ref[i] = flux
 
     shape = jax.ShapeDtypeStruct((2 * block.plane, PAD, block.r), BF)
     return call(kernel, shape, [*halos, jp], WAIT)
 
 
 def finish_sweep(block, halos, residual, inverse, jp, bt, bc):
-    def plane(x, x_side, ready, near, sends, r_ref, v_ref, j_ref, bt_ref, bc_ref, a_ref):
-        work = block.work(x, x_side)
+    def finish(work, ready, near, r_ref, v_ref, j_ref, bc_ref):
         fluxes = [
             [
-                ready[x_side * block.plane + i]
+                ready[i]
                 if f < 2
                 else mm(j_ref[e, f, :, :PAIR], pick(near, f, block.slot(f, x, y, z))).astype(BF)
                 for f in faces
             ]
-            for i, (e, y, z, faces) in enumerate(work)
+            for i, (e, x, y, z, faces) in enumerate(work)
         ]
-        rest = [(r_ref[w[0]] - coupled(bc_ref, w[3], flux)).astype(BF) for w, flux in zip(work, fluxes)]
-        values = [mm(v_ref[w[0]], value).astype(BF) for w, value in zip(work, rest)]
-        send_traces(block, x, work, values, bt_ref, sends)
+        rest = [(r_ref[w[0]] - coupled(bc_ref, w[4], flux)).astype(BF) for w, flux in zip(work, fluxes)]
+        return [mm(v_ref[w[0]], value).astype(BF) for w, value in zip(work, rest)]
+
+    def write(work, values, bt_ref, sends, a_ref):
+        send_traces(block, work, values, bt_ref, sends)
         for w, value in zip(work, values):
             a_ref[w[0]] = value
 
     def ends(*refs):
-        ready, near, fixed, (a_ref, *sends) = refs[0], by_face(refs[1:5]), refs[5:10], refs[10:]
-        block.end_planes(lambda x, side: plane(x, side, ready, near, sends, *fixed, a_ref))
+        ready, near, fixed, (bt_ref, a_ref, *sends) = refs[0], by_face(refs[1:5]), refs[5:9], refs[9:]
+        work = block.of_planes(block.end_planes())
+        values = finish(work, ready, near, *fixed)
+        write([(e, x, y, z, faces[:1]) for e, x, y, z, faces in work], values, bt_ref, sends, a_ref)
 
     def inner(*refs):
-        done, near, fixed, (a_ref, *sends) = refs[:5], by_face(refs[5:9]), refs[9:14], refs[14:]
-        sends = [None, None, *sends]
-        block.inner_planes(lambda x, side: plane(x, side, None, near, sends, *fixed, a_ref))
-        for have, want in zip(done, [a_ref, *sends[2:]]):
-            step = want.shape[0] // block.nx
-            for x in (0, block.nx - 1):
-                want[x * step : (x + 1) * step] = have[x * step : (x + 1) * step]
-
-    fixed = [residual, inverse, jp, bt, bc]
+        done_ref, near, fixed, (bt_ref, a_ref, *sends) = refs[0], by_face(refs[1:5]), refs[5:9], refs[9:]
+        work = block.of_planes(block.inner_planes())
+        outer = block.of_planes([(x, None) for x, _ in block.end_planes()])
+        values = finish(work, None, near, *fixed)
+        write(work + outer, values + [done_ref[w[0]] for w in outer], bt_ref, [None, None, *sends], a_ref)
+
+    fixed = [residual, inverse, jp, bc, bt]
     shapes = block.send_shapes()
     whole = jax.ShapeDtypeStruct((block.nx * block.plane, block.c, block.r), BF)
     ready = x_fluxes(block, halos[:2], jp)
-    part, *sends = call(ends, [whole] + shapes, [ready, *z_then_y(halos), *fixed], FIRST)
-    a, *rest = call(inner, [whole] + shapes[2:], [part, *sends[2:], *z_then_y(halos), *fixed], SECOND)
-    return a, [*sends[:2], *rest]
+    part, *sends = call(ends, [whole] + shapes[:2], [ready, *z_then_y(halos), *fixed], FIRST)
+    a, *rest = call(inner, [whole] + shapes[2:], [part, *z_then_y(halos), *fixed], SECOND)
+    return a, [*sends, *rest]
 
 
 def local_gradient(block, a, jp, p, bt, after):
@@ -369,9 +411,9 @@
 
 
 def finish_gradient(block, halos, owns, inside, jp, p):
-    def add(x, work, near, own, j_ref, p_ref, g_ref):
+    def add(work, near, own, j_ref, p_ref, g_ref):
         total = []
-        for e, y, z, faces in work:
+        for e, x, y, z, faces in work:
             rows = [jnp.zeros((1, block.r), F32)] * 8
             for f in faces:
                 place = block.slot(f, x, y, z)
@@ -385,27 +427,26 @@
     def along_x(*refs):
         near, own, (j_ref, p_ref, g_ref, out_ref) = refs[:2], refs[2:4], refs[4:]
 
-        def visit(x, side):
-            work = [(e, y, z, [side]) for e, y, z, _ in block.work(x, None)]
-            for w, value in zip(work, add(x, work, near, own, j_ref, p_ref, g_ref)):
+        for x, side in block.end_planes():
+            work = [(e, x, y, z, [side]) for e, y, z, _ in block.work(x, None)]
+            for w, value in zip(work, add(work, near, own, j_ref, p_ref, g_ref)):
                 out_ref[w[0]] = value
-
-        block.end_planes(visit)
         kept = slice(block.plane, (block.nx - 1) * block.plane)
         out_ref[kept] = g_ref[kept]
 
     def others(*refs):
         near, own, (j_ref, p_ref, g_ref, out_ref) = by_face(refs[:4]), by_face(refs[4:8]), refs[8:]
 
-        def visit(x):
-            work = block.work(x, None)
-            total = add(x, work, near, own, j_ref, p_ref, g_ref)
-            for y in range(block.ny):
+        def visit(planes):
+            work = block.of_planes([(x, None) for x in planes])
+            total = add(work, near, own, j_ref, p_ref, g_ref)
+            for i in range(0, len(work), block.nz):
+                _, x, y, _, _ = work[i]
                 for f in range(6):
-                    rows = [g[f : f + 1] for g in total[y * block.nz : (y + 1) * block.nz]]
+                    rows = [g[f : f + 1] for g in total[i : i + block.nz]]
                     out_ref[x * block.ny + y, f] = jnp.concatenate(rows, axis=0)
 
-        block.every_plane(visit)
+        block.two_at_once(visit)
 
     inside = call(along_x, inside, [*halos[:2], *owns[:2], jp, p, inside], WAIT)
     shape = jax.ShapeDtypeStruct((block.nx * block.ny, 6, block.nz, block.r), F32)
@@ -436,7 +477,7 @@
 
     bt = jnp.pad(trace_basis.transpose(0, 2, 1), ((0, 0), (0, gap), (0, 0)))
     adjoint = warm_start.reshape(count, c, r)
-    sends = first_sends(block, adjoint, bt)
+    sends = first_sends(block, warm_start, adjoint, trace_basis, bt)
 
     source = adjoint_source.reshape(count, c, r)
     inverse = block_inverse.reshape(count, c, c)
@@ -451,6 +492,9 @@
             p = permutations(block, turns, adjoint)
             after.append(p)
         residual = local_residual(block, adjoint, source, jp, bt, ball, after)
+        if sweep == 0:
+            inverse, residual = lax.optimization_barrier((block_inverse, residual))
+            inverse = inverse.reshape(count, c, c)
         adjoint, sends = finish_sweep(block, halos, residual, inverse, jp, bt, bc)
     halos = exchange(sends)
     inside = local_gradient(block, adjoint, jp, p, bt, halos[0])

time: 87.2 us -> 86.2 us (0.989)
  waiting for transfers between devices: 5.49 us -> 8.57 us
  local copies, waits for them, and re-layouts: 6.94 us -> 3.93 us
  Pallas kernels: 32.3 us -> 30.9 us
    ppermute x6, waiting for transfers between devices: 2.76 us -> 6.9 us  [exchange(): lax.ppermute(sends[4 + part], 'gz', pairs + [(j, i) for i, j in pairs])]
    unnamed x16 -> x17, local copies, waits for them, and re-layouts: 6.9 us -> 3.41 us
    pallas_call x15, Pallas kernels: 32.3 us -> 30.9 us  [call(): pl.pallas_call(kernel, out_shape=out_shape, in_specs=specs or [VMEM] * le...]
    ppermute x6, starting transfers between devices: 12.4 us -> 13.8 us  [exchange(): halos.append(lax.ppermute(sends[2 * d], axis, down))]
    ppermute x6, waiting for transfers between devices: 2.72 us -> 1.39 us  [exchange(): halos.append(lax.ppermute(sends[2 * d], axis, down))]
    ppermute x6, starting transfers between devices: 17.8 us -> 16.7 us  [exchange(): halos.append(lax.ppermute(sends[2 * d + 1], axis, up))]
  transfers between devices with their start and end apart: 18 -> 18, of which waited for: 6 -> 10; matrix products, arithmetic and copies ran while one was open for 4% -> 5% of each run, Pallas kernels for 30% -> 28%
where the time goes in v3:
time: 86.2 us; the launch traced here: 86 us
  starting transfers between devices  41.7 us (48%)
  Pallas kernels  30.9 us (36%)
  waiting for transfers between devices  8.57 us (10%)
  local copies, waits for them, and re-layouts  3.93 us (5%)
  between operations  0.93 us (1%)
    pallas_call x15, Pallas kernels, call(): pl.pallas_call(kernel, out_shape=out_shape, in_specs=specs or [VMEM] * le...  30.9 us
    ppermute x6, starting transfers between devices, exchange(): halos.append(lax.ppermute(sends[2 * d + 1], axis, up))  16.7 us
    ppermute x6, starting transfers between devices, exchange(): halos.append(lax.ppermute(sends[2 * d], axis, down))  13.8 us
    ppermute x6, starting transfers between devices, exchange(): lax.ppermute(sends[4 + part], 'gz', pairs + [(j, i) for i, j in pairs])  11.2 us
    ppermute x6, waiting for transfers between devices, exchange(): lax.ppermute(sends[4 + part], 'gz', pairs + [(j, i) for i, j in pairs])  6.9 us
    unnamed x17, local copies, waits for them, and re-layouts  3.41 us
  transfers between devices with their start and end apart: 18, of which 10 were waited for; matrix products, arithmetic and copies ran while one was open for 5% of the time, Pallas kernels for 28%

profile of v3, /device:TPU:57, one launch (start us, length us, event | category | flops | bytes accessed | tf_op | source)
XLA Modules:
  0.0 86.0 jit_solution(14676057076666563641)
XLA Ops:
  0.6 0.0 copy-start
  0.6 1.9 %shard_map.77 = (bf16[4,152,128]{2,1,0:T(8,128)(2,1)S(1)}, bf16[4,152,128]{2,1,0:T(8,128)(2,1)S(1)}) custom-call(bf16[16,175,2,128]{3,2,1,0:T(2,128)(2,1)} %bitcast.25, bf16[6,75,175]{2,1,0:T(8,128)(2,1)} %bitcast.26), custom_call_target="tpu_custom_call" | custom-call | flops 1000 | tf_op jit(solution)/shard_map/pallas_call | solution.py:35
  2.6 0.0 copy-start.4
  2.6 6.1 %collective-permute-start = (bf16[4,152,128]{2,1,0:T(8,128)(2,1)S(1)}, bf16[4,152,128]{2,1,0:T(8,128)(2,1)S(1)}, u32[]{:S(2)}, u32[]{:S(2)}) collective-permute-start(bf16[4,152,128]{2,1,0:T(8,128)(2,1)S(1)} %get-tuple-element.29), channel_id=1, source_target_pairs={{0,32},{32,64},{64,96},{96,128},{128,160},{160,192},{192,224},{224... | collective-permute-start | bytes 466952 | tf_op jit(solution)/shard_map/ppermute | solution.py:462
  8.7 2.3 %collective-permute-start.1 = (bf16[4,152,128]{2,1,0:T(8,128)(2,1)S(1)}, bf16[4,152,128]{2,1,0:T(8,128)(2,1)S(1)}, u32[]{:S(2)}, u32[]{:S(2)}) collective-permute-start(bf16[4,152,128]{2,1,0:T(8,128)(2,1)S(1)} %get-tuple-element.30), channel_id=1, source_target_pairs={{32,0},{64,32},{96,64},{128,96},{160,128},{192,160},{224,192},{0,2... | collective-permute-start | bytes 466952 | tf_op jit(solution)/shard_map/ppermute | solution.py:463
  10.9 0.0 copy-done
  11.0 0.2 copy.10
  11.1 0.0 copy-done.4
  11.2 0.0 copy-start.5
  11.2 0.8 shard_map.80
  12.1 0.8 collective-permute-start.2
  12.9 3.6 %collective-permute-start.3 = (bf16[8,152,128]{2,1,0:T(8,128)(2,1)S(1)}, bf16[8,152,128]{2,1,0:T(8,128)(2,1)S(1)}, u32[]{:S(2)}, u32[]{:S(2)}) collective-permute-start(bf16[8,152,128]{2,1,0:T(8,128)(2,1)S(1)} %get-tuple-element.33), channel_id=1, source_target_pairs={{1,2},{2,1},{5,6},{6,5},{9,10},{10,9},{13,14},{14,13},{17,18},{18,... | collective-permute-start | bytes 933896 | tf_op jit(solution)/shard_map/ppermute | solution.py:466
  16.5 1.6 %collective-permute-start.4 = (bf16[4,152,128]{2,1,0:T(8,128)(2,1)S(1)}, bf16[4,152,128]{2,1,0:T(8,128)(2,1)S(1)}, u32[]{:S(2)}, u32[]{:S(2)}) collective-permute-start(bf16[4,152,128]{2,1,0:T(8,128)(2,1)S(1)} %get-tuple-element.34), channel_id=1, source_target_pairs={{0,4},{4,8},{8,12},{12,16},{16,20},{20,24},{24,28},{28,0},{1,5},{5... | collective-permute-start | bytes 466952 | tf_op jit(solution)/shard_map/ppermute | solution.py:462
  18.2 0.0 copy-done.5
  18.2 0.0 copy-done.1
  18.2 0.8 copy.8
  19.0 0.0 copy-start.3
  19.0 3.4 %shard_map.78 = (bf16[32,6,80,80]{3,2,1,0:T(8,128)(2,1)S(1)}, bf16[6,175,128]{2,1,0:T(8,128)(2,1)S(1)}, bf16[175,480]{1,0:T(8,128)(2,1)S(1)}) custom-call(bf16[32,6,75,75]{3,2,1,0:T(8,128)(2,1)S(1)} %bitcast.17, s32[32,6,15]{2,1,0:T(8,128)S(1)} %bitcast.23, bf16[6,80,175]{2,1,0:T(8,128)(2,1)S(1)} %pad.4.bt_ref.refs_9_), custom_call_target="tpu_custom_call" | custom-call | flops 1000 | tf_op jit(solution)/shard_map/pallas_call | solution.py:35
  22.4 0.2 copy.11
  22.6 0.0 collective-permute-done.low_ref.refs_0_
  22.6 0.5 collective-permute-start.5
  23.1 4.3 %shard_map.81.refs_5_ = f32[32,175,128]{2,1,0:T(8,128)S(1)} custom-call(bf16[32,175,128]{2,1,0:T(8,128)(2,1)S(1)} %bitcast.21, bf16[32,175,128]{2,1,0:T(8,128)(2,1)S(1)} %bitcast.18, bf16[32,6,80,80]{3,2,1,0:T(8,128)(2,1)S(1)} %get-tuple-element.31.j_ref.refs_7_.refs_4_.refs_8_, bf16[6,80,175]{2,1,0:T(8,128)(2,1)S(1)} %pad.4.bt_ref.refs_9_, ...), custom_call_target="tpu_custom_call" | custom-call | flops 1000 | tf_op jit(solution)/shard_map/pallas_call | solution.py:35
  27.4 0.5 copy.12
  27.9 0.0 collective-permute-done.1.high_ref
  27.9 0.3 shard_map.79.refs_0_
  28.2 0.0 collective-permute-done.4.refs_3_
  28.2 0.2 collective-permute-done.5.refs_4_
  28.5 1.2 %collective-permute-done.2.refs_1_ = bf16[8,152,128]{2,1,0:T(8,128)(2,1)S(1)} collective-permute-done((bf16[8,152,128]{2,1,0:T(8,128)(2,1)S(1)}, bf16[8,152,128]{2,1,0:T(8,128)(2,1)S(1)}, u32[]{:S(2)}, u32[]{:S(2)}) %collective-permute-start.2) | collective-permute-done | bytes 311328 | tf_op jit(solution)/shard_map/ppermute | solution.py:466
  29.7 0.5 collective-permute-done.3.refs_2_
  30.2 1.6 %shard_map.82 = (bf16[32,175,128]{2,1,0:T(8,128)(2,1)S(1)}, bf16[4,152,128]{2,1,0:T(8,128)(2,1)S(1)}, bf16[4,152,128]{2,1,0:T(8,128)(2,1)S(1)}) custom-call(bf16[16,80,128]{2,1,0:T(8,128)(2,1)S(1)} %shard_map.79.refs_0_, bf16[8,152,128]{2,1,0:T(8,128)(2,1)S(1)} %collective-permute-done.2.refs_1_, bf16[8,152,128]{2,1,0:T(8,128)(2,1)S(1)} %collective-permute-done.3.refs_2_, ...), custom_call_target="tpu_custom_call" | custom-call | flops 1000 | tf_op jit(solution)/shard_map/pallas_call | solution.py:35
  31.7 3.1 %collective-permute-start.6 = (bf16[4,152,128]{2,1,0:T(8,128)(2,1)S(1)}, bf16[4,152,128]{2,1,0:T(8,128)(2,1)S(1)}, u32[]{:S(2)}, u32[]{:S(2)}) collective-permute-start(bf16[4,152,128]{2,1,0:T(8,128)(2,1)S(1)} %get-tuple-element.40), channel_id=1, source_target_pairs={{0,32},{32,64},{64,96},{96,128},{128,160},{160,192},{192,224},{224... | collective-permute-start | bytes 466952 | tf_op jit(solution)/shard_map/ppermute | solution.py:462
  34.8 4.5 %collective-permute-start.7 = (bf16[4,152,128]{2,1,0:T(8,128)(2,1)S(1)}, bf16[4,152,128]{2,1,0:T(8,128)(2,1)S(1)}, u32[]{:S(2)}, u32[]{:S(2)}) collective-permute-start(bf16[4,152,128]{2,1,0:T(8,128)(2,1)S(1)} %get-tuple-element.41), channel_id=1, source_target_pairs={{32,0},{64,32},{96,64},{128,96},{160,128},{192,160},{224,192},{0,2... | collective-permute-start | bytes 466952 | tf_op jit(solution)/shard_map/ppermute | solution.py:463
  39.3 1.8 %shard_map.84 = (bf16[32,175,128]{2,1,0:T(8,128)(2,1)S(1)}, bf16[4,152,128]{2,1,0:T(8,128)(2,1)S(1)}, bf16[4,152,128]{2,1,0:T(8,128)(2,1)S(1)}, bf16[8,152,128]{2,1,0:T(8,128)(2,1)S(1)}, bf16[8,152,128]{2,1,0:T(8,128)(2,1)S(1)}) custom-call(bf16[32,175,128]{2,1,0:T(8,128)(2,1)S(1)} %get-tuple-element.42.refs_0_, ...), custom_call_target="tpu_custom_call" | custom-call | flops 1000 | tf_op jit(solution)/shard_map/pallas_call | solution.py:35
  41.1 0.2 collective-permute-start.8
  41.2 3.4 %collective-permute-start.9 = (bf16[8,152,128]{2,1,0:T(8,128)(2,1)S(1)}, bf16[8,152,128]{2,1,0:T(8,128)(2,1)S(1)}, u32[]{:S(2)}, u32[]{:S(2)}) collective-permute-start(bf16[8,152,128]{2,1,0:T(8,128)(2,1)S(1)} %get-tuple-element.44), channel_id=1, source_target_pairs={{1,2},{2,1},{5,6},{6,5},{9,10},{10,9},{13,14},{14,13},{17,18},{18,... | collective-permute-start | bytes 933896 | tf_op jit(solution)/shard_map/ppermute | solution.py:466
  44.7 1.7 %collective-permute-start.10 = (bf16[4,152,128]{2,1,0:T(8,128)(2,1)S(1)}, bf16[4,152,128]{2,1,0:T(8,128)(2,1)S(1)}, u32[]{:S(2)}, u32[]{:S(2)}) collective-permute-start(bf16[4,152,128]{2,1,0:T(8,128)(2,1)S(1)} %get-tuple-element.45), channel_id=1, source_target_pairs={{0,4},{4,8},{8,12},{12,16},{16,20},{20,24},{24,28},{28,0},{1,5},{5... | collective-permute-start | bytes 466952 | tf_op jit(solution)/shard_map/ppermute | solution.py:462
  46.4 3.0 %shard_map.85.refs_1_.p_ref.refs_5_.refs_9_ = bf16[32,6,80,80]{3,2,1,0:T(8,128)(2,1)S(1)} custom-call(s32[32,6,15]{2,1,0:T(8,128)S(1)} %bitcast.24, bf16[32,175,128]{2,1,0:T(8,128)(2,1)S(1)} %get-tuple-element.47._.a_ref), custom_call_target="tpu_custom_call" | custom-call | flops 1000 | tf_op jit(solution)/shard_map/pallas_call | solution.py:35
  49.3 0.0 collective-permute-done.6.low_ref.refs_0_
  49.4 0.6 collective-permute-start.11
  50.0 4.3 %shard_map.86.refs_5_ = f32[32,175,128]{2,1,0:T(8,128)S(1)} custom-call(bf16[32,175,128]{2,1,0:T(8,128)(2,1)S(1)} %get-tuple-element.47._.a_ref, bf16[32,175,128]{2,1,0:T(8,128)(2,1)S(1)} %bitcast.19, bf16[32,6,80,80]{3,2,1,0:T(8,128)(2,1)S(1)} %get-tuple-element.31.j_ref.refs_7_.refs_4_.refs_8_, bf16[6,80,175]{2,1,0:T(8,128)(2,1)S(1)} %pad.4.bt_ref.refs_9_, ...), custom_call_target="tpu_custom_call" | custom-call | flops 1000 | tf_op jit(solution)/shard_map/pallas_call | solution.py:35
  54.3 0.0 collective-permute-done.7.high_ref
  54.3 0.3 shard_map.83.refs_0_
  54.6 0.0 collective-permute-done.10.refs_3_
  54.7 0.6 collective-permute-done.11.refs_4_
  55.2 0.3 collective-permute-done.8.refs_1_
  55.5 1.5 %collective-permute-done.9.refs_2_ = bf16[8,152,128]{2,1,0:T(8,128)(2,1)S(1)} collective-permute-done((bf16[8,152,128]{2,1,0:T(8,128)(2,1)S(1)}, bf16[8,152,128]{2,1,0:T(8,128)(2,1)S(1)}, u32[]{:S(2)}, u32[]{:S(2)}) %collective-permute-start.9) | collective-permute-done | bytes 311328 | tf_op jit(solution)/shard_map/ppermute | solution.py:466
  57.1 1.6 %shard_map.87 = (bf16[32,175,128]{2,1,0:T(8,128)(2,1)S(1)}, bf16[4,152,128]{2,1,0:T(8,128)(2,1)S(1)}, bf16[4,152,128]{2,1,0:T(8,128)(2,1)S(1)}) custom-call(bf16[16,80,128]{2,1,0:T(8,128)(2,1)S(1)} %shard_map.83.refs_0_, bf16[8,152,128]{2,1,0:T(8,128)(2,1)S(1)} %collective-permute-done.8.refs_1_, bf16[8,152,128]{2,1,0:T(8,128)(2,1)S(1)} %collective-permute-done.9.refs_2_, ...), custom_call_target="tpu_custom_call" | custom-call | flops 1000 | tf_op jit(solution)/shard_map/pallas_call | solution.py:35
  58.6 2.6 %collective-permute-start.16 = (bf16[4,152,128]{2,1,0:T(8,128)(2,1)S(1)}, bf16[4,152,128]{2,1,0:T(8,128)(2,1)S(1)}, u32[]{:S(2)}, u32[]{:S(2)}) collective-permute-start(bf16[4,152,128]{2,1,0:T(8,128)(2,1)S(1)} %get-tuple-element.54.refs_3_), channel_id=1, source_target_pairs={{0,32},{32,64},{64,96},{96,128},{128,160},{160,192},{192,224},{224... | collective-permute-start | bytes 466952 | tf_op jit(solution)/shard_map/ppermute | solution.py:462
  61.2 5.0 %collective-permute-start.17 = (bf16[4,152,128]{2,1,0:T(8,128)(2,1)S(1)}, bf16[4,152,128]{2,1,0:T(8,128)(2,1)S(1)}, u32[]{:S(2)}, u32[]{:S(2)}) collective-permute-start(bf16[4,152,128]{2,1,0:T(8,128)(2,1)S(1)} %get-tuple-element.55.refs_2_), channel_id=1, source_target_pairs={{32,0},{64,32},{96,64},{128,96},{160,128},{192,160},{224,192},{0,2... | collective-permute-start | bytes 466952 | tf_op jit(solution)/shard_map/ppermute | solution.py:463
  66.2 1.8 %shard_map.88 = (bf16[32,175,128]{2,1,0:T(8,128)(2,1)S(1)}, bf16[4,152,128]{2,1,0:T(8,128)(2,1)S(1)}, bf16[4,152,128]{2,1,0:T(8,128)(2,1)S(1)}, bf16[8,152,128]{2,1,0:T(8,128)(2,1)S(1)}, bf16[8,152,128]{2,1,0:T(8,128)(2,1)S(1)}) custom-call(bf16[32,175,128]{2,1,0:T(8,128)(2,1)S(1)} %get-tuple-element.48.refs_0_, ...), custom_call_target="tpu_custom_call" | custom-call | flops 1000 | tf_op jit(solution)/shard_map/pallas_call | solution.py:35
  68.0 0.3 collective-permute-start.12
  68.3 2.8 %collective-permute-start.13 = (bf16[8,152,128]{2,1,0:T(8,128)(2,1)S(1)}, bf16[8,152,128]{2,1,0:T(8,128)(2,1)S(1)}, u32[]{:S(2)}, u32[]{:S(2)}) collective-permute-start(bf16[8,152,128]{2,1,0:T(8,128)(2,1)S(1)} %get-tuple-element.51.refs_5_), channel_id=1, source_target_pairs={{1,2},{2,1},{5,6},{6,5},{9,10},{10,9},{13,14},{14,13},{17,18},{18,... | collective-permute-start | bytes 933896 | tf_op jit(solution)/shard_map/ppermute | solution.py:466
  71.1 1.6 %collective-permute-start.14 = (bf16[4,152,128]{2,1,0:T(8,128)(2,1)S(1)}, bf16[4,152,128]{2,1,0:T(8,128)(2,1)S(1)}, u32[]{:S(2)}, u32[]{:S(2)}) collective-permute-start(bf16[4,152,128]{2,1,0:T(8,128)(2,1)S(1)} %get-tuple-element.52.refs_7_), channel_id=1, source_target_pairs={{0,4},{4,8},{8,12},{12,16},{16,20},{20,24},{24,28},{28,0},{1,5},{5... | collective-permute-start | bytes 466952 | tf_op jit(solution)/shard_map/ppermute | solution.py:462
  72.7 2.2 %copy.13 = bf16[4,4,2,175,128]{4,2,3,1,0:T(2,128)(2,1)} copy(bf16[4,4,2,175,128]{4,3,2,1,0:T(8,128)(2,1)S(1)} %bitcast.22) | data formatting | bytes 2867200
  74.9 0.3 collective-permute-done.16._.refs_0_
  75.2 0.9 %collective-permute-start.15 = (bf16[4,152,128]{2,1,0:T(8,128)(2,1)S(1)}, bf16[4,152,128]{2,1,0:T(8,128)(2,1)S(1)}, u32[]{:S(2)}, u32[]{:S(2)}) collective-permute-start(bf16[4,152,128]{2,1,0:T(8,128)(2,1)S(1)} %get-tuple-element.53.refs_6_), channel_id=1, source_target_pairs={{4,0},{8,4},{12,8},{16,12},{20,16},{24,20},{28,24},{0,28},{5,1},{9... | collective-permute-start | bytes 466952 | tf_op jit(solution)/shard_map/ppermute | solution.py:463
  76.1 4.0 %shard_map.89.refs_6_ = f32[32,8,128]{2,1,0:T(8,128)S(1)} custom-call(bf16[32,175,128]{2,1,0:T(8,128)(2,1)S(1)} %get-tuple-element.49.a_ref, bf16[32,6,80,80]{3,2,1,0:T(8,128)(2,1)S(1)} %get-tuple-element.31.j_ref.refs_7_.refs_4_.refs_8_, bf16[32,6,80,80]{3,2,1,0:T(8,128)(2,1)S(1)} %shard_map.85.refs_1_.p_ref.refs_5_.refs_9_, ...), custom_call_target="tpu_custom_call" | custom-call | flops 1000 | tf_op jit(solution)/shard_map/pallas_call | solution.py:35
  80.1 0.0 collective-permute-done.17.refs_1_
  80.1 0.3 shard_map.90.refs_10_
  80.5 0.0 collective-permute-done.14.refs_2_
  80.5 0.6 collective-permute-done.15.refs_3_
  81.0 2.4 %collective-permute-done.12.refs_0_ = bf16[8,152,128]{2,1,0:T(8,128)(2,1)S(1)} collective-permute-done((bf16[8,152,128]{2,1,0:T(8,128)(2,1)S(1)}, bf16[8,152,128]{2,1,0:T(8,128)(2,1)S(1)}, u32[]{:S(2)}, u32[]{:S(2)}) %collective-permute-start.12) | collective-permute-done | bytes 311328 | tf_op jit(solution)/shard_map/ppermute | solution.py:466
  83.4 1.0 %collective-permute-done.13.refs_1_ = bf16[8,152,128]{2,1,0:T(8,128)(2,1)S(1)} collective-permute-done((bf16[8,152,128]{2,1,0:T(8,128)(2,1)S(1)}, bf16[8,152,128]{2,1,0:T(8,128)(2,1)S(1)}, u32[]{:S(2)}, u32[]{:S(2)}) %collective-permute-start.13) | collective-permute-done | bytes 311328 | tf_op jit(solution)/shard_map/ppermute | solution.py:466
  84.4 1.6 %shard_map.91 = f32[16,6,2,128]{3,2,1,0:T(2,128)} custom-call(bf16[8,152,128]{2,1,0:T(8,128)(2,1)S(1)} %collective-permute-done.12.refs_0_, bf16[8,152,128]{2,1,0:T(8,128)(2,1)S(1)} %collective-permute-done.13.refs_1_, bf16[4,152,128]{2,1,0:T(8,128)(2,1)S(1)} %collective-permute-done.14.refs_2_, bf16[4,152,128]{2,1,0:T(8,128)(2,1)S(1)} %collective-permute-done.15.refs_3_, ...), custom_call_target="tpu_custom_call" | custom-call | flops 1000 | tf_op jit(solution)/shard_map/pallas_call | solution.py:35
  (6 shorter events, 0.1 us)
Async XLA Ops:
  0.6 10.3 %copy-start = (bf16[4,4,2,175,128]{4,2,3,1,0:T(2,128)(2,1)S(1)}, bf16[4,4,2,175,128]{4,2,3,1,0:T(2,128)(2,1)}, u32[]{:S(2)}) copy-start(bf16[4,4,2,175,128]{4,2,3,1,0:T(2,128)(2,1)} %param.7) | copy-start | bytes 4300804
  2.6 8.6 %copy-start.4 = (bf16[6,175,75]{1,2,0:T(8,128)(2,1)S(1)}, bf16[6,175,75]{1,2,0:T(8,128)(2,1)}, u32[]{:S(2)}) copy-start(bf16[6,175,75]{1,2,0:T(8,128)(2,1)} %param.10) | copy-start | bytes 472504
  2.6 20.0 %collective-permute-start = (bf16[4,152,128]{2,1,0:T(8,128)(2,1)S(1)}, bf16[4,152,128]{2,1,0:T(8,128)(2,1)S(1)}, u32[]{:S(2)}, u32[]{:S(2)}) collective-permute-start(bf16[4,152,128]{2,1,0:T(8,128)(2,1)S(1)} %get-tuple-element.29), channel_id=1, source_target_pairs={{0,32},{32,64},{64,96},{96,128},{128,160},{160,192},{192,224},{224... | collective-permute-start | bytes 466952 | tf_op jit(solution)/shard_map/ppermute | solution.py:462
  8.7 19.2 %collective-permute-start.1 = (bf16[4,152,128]{2,1,0:T(8,128)(2,1)S(1)}, bf16[4,152,128]{2,1,0:T(8,128)(2,1)S(1)}, u32[]{:S(2)}, u32[]{:S(2)}) collective-permute-start(bf16[4,152,128]{2,1,0:T(8,128)(2,1)S(1)} %get-tuple-element.30), channel_id=1, source_target_pairs={{32,0},{64,32},{96,64},{128,96},{160,128},{192,160},{224,192},{0,2... | collective-permute-start | bytes 466952 | tf_op jit(solution)/shard_map/ppermute | solution.py:463
  11.0 7.2 %copy-start.1 = (bf16[4,4,2,6,75,75]{5,2,4,3,1,0:T(2,128)(2,1)S(1)}, bf16[4,4,2,6,75,75]{5,2,4,3,1,0:T(2,128)(2,1)}, u32[]{:S(2)}) copy-start(bf16[4,4,2,6,75,75]{5,2,4,3,1,0:T(2,128)(2,1)} %param.9) | copy-start | bytes 6480004
  11.2 7.0 %copy-start.5 = (s32[4,4,2,6,15]{4,2,3,1,0:T(2,128)S(1)}, s32[4,4,2,6,15]{4,2,3,1,0:T(2,128)}, u32[]{:S(2)}) copy-start(s32[4,4,2,6,15]{4,2,3,1,0:T(2,128)} %param.11) | copy-start | bytes 34564
  12.1 17.6 %collective-permute-start.2 = (bf16[8,152,128]{2,1,0:T(8,128)(2,1)S(1)}, bf16[8,152,128]{2,1,0:T(8,128)(2,1)S(1)}, u32[]{:S(2)}, u32[]{:S(2)}) collective-permute-start(bf16[8,152,128]{2,1,0:T(8,128)(2,1)S(1)} %get-tuple-element.32), channel_id=1, source_target_pairs={{0,1},{2,3},{1,0},{3,2},{4,5},{6,7},{5,4},{7,6},{8,9},{10,11},{9,8... | collective-permute-start | bytes 933896 | tf_op jit(solution)/shard_map/ppermute | solution.py:466
  12.9 17.3 %collective-permute-start.3 = (bf16[8,152,128]{2,1,0:T(8,128)(2,1)S(1)}, bf16[8,152,128]{2,1,0:T(8,128)(2,1)S(1)}, u32[]{:S(2)}, u32[]{:S(2)}) collective-permute-start(bf16[8,152,128]{2,1,0:T(8,128)(2,1)S(1)} %get-tuple-element.33), channel_id=1, source_target_pairs={{1,2},{2,1},{5,6},{6,5},{9,10},{10,9},{13,14},{14,13},{17,18},{18,... | collective-permute-start | bytes 933896 | tf_op jit(solution)/shard_map/ppermute | solution.py:466
  16.5 11.7 %collective-permute-start.4 = (bf16[4,152,128]{2,1,0:T(8,128)(2,1)S(1)}, bf16[4,152,128]{2,1,0:T(8,128)(2,1)S(1)}, u32[]{:S(2)}, u32[]{:S(2)}) collective-permute-start(bf16[4,152,128]{2,1,0:T(8,128)(2,1)S(1)} %get-tuple-element.34), channel_id=1, source_target_pairs={{0,4},{4,8},{8,12},{12,16},{16,20},{20,24},{24,28},{28,0},{1,5},{5... | collective-permute-start | bytes 466952 | tf_op jit(solution)/shard_map/ppermute | solution.py:462
  19.0 3.4 %copy-start.3 = (bf16[4,4,2,175,128]{4,2,3,1,0:T(2,128)(2,1)S(1)}, bf16[4,4,2,175,128]{4,2,3,1,0:T(2,128)(2,1)}, u32[]{:S(2)}) copy-start(bf16[4,4,2,175,128]{4,2,3,1,0:T(2,128)(2,1)} %param.6) | copy-start | bytes 4300804
  22.6 5.9 %collective-permute-start.5 = (bf16[4,152,128]{2,1,0:T(8,128)(2,1)S(1)}, bf16[4,152,128]{2,1,0:T(8,128)(2,1)S(1)}, u32[]{:S(2)}, u32[]{:S(2)}) collective-permute-start(bf16[4,152,128]{2,1,0:T(8,128)(2,1)S(1)} %get-tuple-element.35), channel_id=1, source_target_pairs={{4,0},{8,4},{12,8},{16,12},{20,16},{24,20},{28,24},{0,28},{5,1},{9... | collective-permute-start | bytes 466952 | tf_op jit(solution)/shard_map/ppermute | solution.py:463
  23.1 4.3 %copy-start.2 = (bf16[4,4,2,175,175]{4,2,3,1,0:T(2,128)(2,1)S(1)}, bf16[4,4,2,175,175]{4,2,3,1,0:T(2,128)(2,1)}, u32[]{:S(2)}) copy-start(bf16[4,4,2,175,175]{4,2,3,1,0:T(2,128)(2,1)} %param.8) | copy-start | bytes 5880004
  31.7 17.6 %collective-permute-start.6 = (bf16[4,152,128]{2,1,0:T(8,128)(2,1)S(1)}, bf16[4,152,128]{2,1,0:T(8,128)(2,1)S(1)}, u32[]{:S(2)}, u32[]{:S(2)}) collective-permute-start(bf16[4,152,128]{2,1,0:T(8,128)(2,1)S(1)} %get-tuple-element.40), channel_id=1, source_target_pairs={{0,32},{32,64},{64,96},{96,128},{128,160},{160,192},{192,224},{224... | collective-permute-start | bytes 466952 | tf_op jit(solution)/shard_map/ppermute | solution.py:462
  34.8 19.5 %collective-permute-start.7 = (bf16[4,152,128]{2,1,0:T(8,128)(2,1)S(1)}, bf16[4,152,128]{2,1,0:T(8,128)(2,1)S(1)}, u32[]{:S(2)}, u32[]{:S(2)}) collective-permute-start(bf16[4,152,128]{2,1,0:T(8,128)(2,1)S(1)} %get-tuple-element.41), channel_id=1, source_target_pairs={{32,0},{64,32},{96,64},{128,96},{160,128},{192,160},{224,192},{0,2... | collective-permute-start | bytes 466952 | tf_op jit(solution)/shard_map/ppermute | solution.py:463
  41.1 14.5 %collective-permute-start.8 = (bf16[8,152,128]{2,1,0:T(8,128)(2,1)S(1)}, bf16[8,152,128]{2,1,0:T(8,128)(2,1)S(1)}, u32[]{:S(2)}, u32[]{:S(2)}) collective-permute-start(bf16[8,152,128]{2,1,0:T(8,128)(2,1)S(1)} %get-tuple-element.43), channel_id=1, source_target_pairs={{0,1},{2,3},{1,0},{3,2},{4,5},{6,7},{5,4},{7,6},{8,9},{10,11},{9,8... | collective-permute-start | bytes 933896 | tf_op jit(solution)/shard_map/ppermute | solution.py:466
  41.2 15.8 %collective-permute-start.9 = (bf16[8,152,128]{2,1,0:T(8,128)(2,1)S(1)}, bf16[8,152,128]{2,1,0:T(8,128)(2,1)S(1)}, u32[]{:S(2)}, u32[]{:S(2)}) collective-permute-start(bf16[8,152,128]{2,1,0:T(8,128)(2,1)S(1)} %get-tuple-element.44), channel_id=1, source_target_pairs={{1,2},{2,1},{5,6},{6,5},{9,10},{10,9},{13,14},{14,13},{17,18},{18,... | collective-permute-start | bytes 933896 | tf_op jit(solution)/shard_map/ppermute | solution.py:466
  44.7 10.0 %collective-permute-start.10 = (bf16[4,152,128]{2,1,0:T(8,128)(2,1)S(1)}, bf16[4,152,128]{2,1,0:T(8,128)(2,1)S(1)}, u32[]{:S(2)}, u32[]{:S(2)}) collective-permute-start(bf16[4,152,128]{2,1,0:T(8,128)(2,1)S(1)} %get-tuple-element.45), channel_id=1, source_target_pairs={{0,4},{4,8},{8,12},{12,16},{16,20},{20,24},{24,28},{28,0},{1,5},{5... | collective-permute-start | bytes 466952 | tf_op jit(solution)/shard_map/ppermute | solution.py:462
  49.4 5.9 %collective-permute-start.11 = (bf16[4,152,128]{2,1,0:T(8,128)(2,1)S(1)}, bf16[4,152,128]{2,1,0:T(8,128)(2,1)S(1)}, u32[]{:S(2)}, u32[]{:S(2)}) collective-permute-start(bf16[4,152,128]{2,1,0:T(8,128)(2,1)S(1)} %get-tuple-element.46), channel_id=1, source_target_pairs={{4,0},{8,4},{12,8},{16,12},{20,16},{24,20},{28,24},{0,28},{5,1},{9... | collective-permute-start | bytes 466952 | tf_op jit(solution)/shard_map/ppermute | solution.py:463
  58.6 16.5 %collective-permute-start.16 = (bf16[4,152,128]{2,1,0:T(8,128)(2,1)S(1)}, bf16[4,152,128]{2,1,0:T(8,128)(2,1)S(1)}, u32[]{:S(2)}, u32[]{:S(2)}) collective-permute-start(bf16[4,152,128]{2,1,0:T(8,128)(2,1)S(1)} %get-tuple-element.54.refs_3_), channel_id=1, source_target_pairs={{0,32},{32,64},{64,96},{96,128},{128,160},{160,192},{192,224},{224... | collective-permute-start | bytes 466952 | tf_op jit(solution)/shard_map/ppermute | solution.py:462
  61.2 18.9 %collective-permute-start.17 = (bf16[4,152,128]{2,1,0:T(8,128)(2,1)S(1)}, bf16[4,152,128]{2,1,0:T(8,128)(2,1)S(1)}, u32[]{:S(2)}, u32[]{:S(2)}) collective-permute-start(bf16[4,152,128]{2,1,0:T(8,128)(2,1)S(1)} %get-tuple-element.55.refs_2_), channel_id=1, source_target_pairs={{32,0},{64,32},{96,64},{128,96},{160,128},{192,160},{224,192},{0,2... | collective-permute-start | bytes 466952 | tf_op jit(solution)/shard_map/ppermute | solution.py:463
  68.0 15.5 %collective-permute-start.12 = (bf16[8,152,128]{2,1,0:T(8,128)(2,1)S(1)}, bf16[8,152,128]{2,1,0:T(8,128)(2,1)S(1)}, u32[]{:S(2)}, u32[]{:S(2)}) collective-permute-start(bf16[8,152,128]{2,1,0:T(8,128)(2,1)S(1)} %get-tuple-element.50.refs_4_), channel_id=1, source_target_pairs={{0,1},{2,3},{1,0},{3,2},{4,5},{6,7},{5,4},{7,6},{8,9},{10,11},{9,8... | collective-permute-start | bytes 933896 | tf_op jit(solution)/shard_map/ppermute | solution.py:466
  68.3 16.2 %collective-permute-start.13 = (bf16[8,152,128]{2,1,0:T(8,128)(2,1)S(1)}, bf16[8,152,128]{2,1,0:T(8,128)(2,1)S(1)}, u32[]{:S(2)}, u32[]{:S(2)}) collective-permute-start(bf16[8,152,128]{2,1,0:T(8,128)(2,1)S(1)} %get-tuple-element.51.refs_5_), channel_id=1, source_target_pairs={{1,2},{2,1},{5,6},{6,5},{9,10},{10,9},{13,14},{14,13},{17,18},{18,... | collective-permute-start | bytes 933896 | tf_op jit(solution)/shard_map/ppermute | solution.py:466
  71.1 9.4 %collective-permute-start.14 = (bf16[4,152,128]{2,1,0:T(8,128)(2,1)S(1)}, bf16[4,152,128]{2,1,0:T(8,128)(2,1)S(1)}, u32[]{:S(2)}, u32[]{:S(2)}) collective-permute-start(bf16[4,152,128]{2,1,0:T(8,128)(2,1)S(1)} %get-tuple-element.52.refs_7_), channel_id=1, source_target_pairs={{0,4},{4,8},{8,12},{12,16},{16,20},{20,24},{24,28},{28,0},{1,5},{5... | collective-permute-start | bytes 466952 | tf_op jit(solution)/shard_map/ppermute | solution.py:462
  75.2 5.9 %collective-permute-start.15 = (bf16[4,152,128]{2,1,0:T(8,128)(2,1)S(1)}, bf16[4,152,128]{2,1,0:T(8,128)(2,1)S(1)}, u32[]{:S(2)}, u32[]{:S(2)}) collective-permute-start(bf16[4,152,128]{2,1,0:T(8,128)(2,1)S(1)} %get-tuple-element.53.refs_6_), channel_id=1, source_target_pairs={{4,0},{8,4},{12,8},{16,12},{20,16},{24,20},{28,24},{0,28},{5,1},{9... | collective-permute-start | bytes 466952 | tf_op jit(solution)/shard_map/ppermute | solution.py:463

commit v4 on v3

--- a/solution.py
+++ b/solution.py
@@ -12,6 +12,7 @@
 LOCAL = 1000
 PREP = 1000
 WAIT = 2500000000
+WAIT_Z = 2500000000
 PAIR = 76
 PAD = 80
 LANES = 128
@@ -31,12 +32,12 @@
     return lax.dot_general(a, b, (((1,), (1,)), ((), ())), preferred_element_type=F32)
 
 
-def call(kernel, out_shape, operands, flops, scratch=(), specs=None, vmem=12):
+def call(kernel, out_shape, operands, flops, scratch=(), specs=None, outs=None, vmem=12):
     return pl.pallas_call(
         kernel,
         out_shape=out_shape,
         in_specs=specs or [VMEM] * len(operands),
-        out_specs=jax.tree.map(lambda _: VMEM, out_shape),
+        out_specs=outs or jax.tree.map(lambda _: VMEM, out_shape),
         scratch_shapes=list(scratch),
         compiler_params=pltpu.CompilerParams(vmem_limit_bytes=vmem * MIB),
         cost_estimate=pl.CostEstimate(flops=flops, bytes_accessed=0, transcendentals=0),
@@ -44,23 +45,32 @@
 
 
 class Block:
-    def __init__(self, nx, ny, nz, c, r):
+    def __init__(self, nx, ny, nz, c, r, split=False):
+        self.split = split
         self.nx, self.ny, self.nz, self.c, self.r = nx, ny, nz, c, r
         self.plane = ny * nz
+
+    def parted(self):
+        return Block(self.nx, self.ny, self.nz, self.c, self.r, True)
 
     def send_shapes(self):
         rows = self.nz * PAIR
         x = jax.ShapeDtypeStruct((self.ny, rows, self.r), BF)
         y = jax.ShapeDtypeStruct((self.nx, rows, self.r), BF)
-        z = jax.ShapeDtypeStruct((self.nx * self.ny // 2, 2 * PAIR, self.r), BF)
-        return [x, x, y, y, z, z]
+        planes = [2, 2, self.nx - 2, self.nx - 2] if self.split else [self.nx] * 2
+        z = [jax.ShapeDtypeStruct((n * self.ny // 2, 2 * PAIR, self.r), BF) for n in planes]
+        return [x, x, y, y, *z]
+
+    def z_buffers(self, x):
+        return (6, 7) if self.split and 0 < x < self.nx - 1 else (4, 5)
 
     def slot(self, face, x, y, z):
         if face < 2:
             return (y, pl.ds(z * PAIR, PAIR))
         if face < 4:
             return (x, pl.ds(z * PAIR, PAIR))
-        return (x * (self.ny // 2) + y // 2, pl.ds((y % 2) * PAIR, PAIR))
+        plane = {0: 0, self.nx - 1: 1}.get(x, x - 1) if self.split else x
+        return (plane * (self.ny // 2) + y // 2, pl.ds((y % 2) * PAIR, PAIR))
 
     def halo_faces(self, x_side, y, z):
         faces = [] if x_side is None else [x_side]
@@ -105,10 +115,11 @@
     return lax.rem(lax.axis_index("gz"), 2) == 0
 
 
-def pick(near, f, place):
+def pick(block, near, f, x, y, z):
+    place = block.slot(f, x, y, z)
     if f < 4:
         return near[f][place]
-    first, second = near[4][place], near[5][place]
+    first, second = (near[i][place] for i in block.z_buffers(x))
     return jnp.where(even_in_z(), *((second, first) if f == 4 else (first, second)))
 
 
@@ -123,8 +134,16 @@
             elif f == 4:
                 low = piece
             else:
-                sends[4][block.slot(4, x, y, z)] = jnp.where(even_in_z(), piece, low)
-                sends[5][block.slot(4, x, y, z)] = jnp.where(even_in_z(), low, piece)
+                first, second = (sends[i] for i in block.z_buffers(x))
+                first[block.slot(4, x, y, z)] = jnp.where(even_in_z(), piece, low)
+                second[block.slot(4, x, y, z)] = jnp.where(even_in_z(), low, piece)
+
+
+def only(work, faces):
+    return [(*w[:4], [f for f in w[4] if f in faces]) for w in work]
+
+
+X, Y, Z = (0, 1), (2, 3), (4, 5)
 
 
 def first_sends(block, warm_start, a, trace_basis, bt):
@@ -191,12 +210,14 @@
     count, group, width, _ = jacobian.shape
     many = 8
 
-    def kernel(j_ref, o_ref, bt_ref, jp_ref, bc_ref, ball_ref):
+    def kernel(j_ref, o_ref, bt_ref, jp_ref, p_ref, bc_ref, ball_ref):
         for f in range(group):
             basis = bt_ref[f].astype(F32).T.astype(BF)
             ball_ref[:, f * PAD : (f + 1) * PAD] = basis
             bc_ref[f] = jnp.concatenate([basis, jnp.zeros((block.c, LANES - PAD), BF)], axis=1)
         none = jnp.zeros((PAD - width, PAD), BF)
+        rows = lax.broadcasted_iota(jnp.int32, (PAD, width), 0)
+        eye = (rows == lax.broadcasted_iota(jnp.int32, (PAD, width), 1)).astype(BF)
 
         def elements(step, carry):
             places = [many * step + i for i in range(many)]
@@ -205,8 +226,10 @@
                 [mm_t(j_ref[e, f], turn[f]).astype(BF) for f in range(group)]
                 for e, turn in zip(places, turned)
             ]
-            for e, values in zip(places, moved):
+            placed = [[mm_t(eye, turn[f]).astype(BF) for f in range(group)] for turn in turned]
+            for e, values, perms in zip(places, moved, placed):
                 for f in range(group):
+                    p_ref[e, f] = perms[f]
                     jp_ref[e, f, :width] = values[f]
                     jp_ref[e, f, width:] = none
             return carry
@@ -216,28 +239,7 @@
     shape = jax.ShapeDtypeStruct((count, group, PAD, PAD), BF)
     bc = jax.ShapeDtypeStruct((group, block.c, LANES), BF)
     ball = jax.ShapeDtypeStruct((block.c, group * PAD), BF)
-    return call(kernel, [shape, bc, ball], [jacobian, orientation, bt], PREP)
-
-
-def permutations(block, orientation, after):
-    count, group, modes = orientation.shape
-
-    def kernel(o_ref, _, p_ref):
-        rows = lax.broadcasted_iota(jnp.int32, (PAD, VARS * modes), 0)
-        eye = (rows == lax.broadcasted_iota(jnp.int32, (PAD, VARS * modes), 1)).astype(BF)
-
-        def elements(step, carry):
-            places = [8 * step + i for i in range(8)]
-            values = [[mm_t(eye, turn).astype(BF) for turn in one_hots(o_ref, e)] for e in places]
-            for e, value in zip(places, values):
-                for f in range(group):
-                    p_ref[e, f] = value[f]
-            return carry
-
-        lax.fori_loop(0, count // 8, elements, 0)
-
-    shape = jax.ShapeDtypeStruct((count, group, PAD, PAD), BF)
-    return call(kernel, shape, [orientation, after], PREP, specs=[VMEM, ANY])
+    return call(kernel, [shape, shape, bc, ball], [jacobian, orientation, bt], PREP)
 
 
 def fill_traces(block, a_ref, bt_ref, t_ref):
@@ -323,64 +325,94 @@
     return (None, None) + tuple(refs[2:4]) + tuple(refs[:2])
 
 
-def x_fluxes(block, halos, jp):
-    def kernel(low_ref, high_ref, j_ref, out_ref):
-        near = (low_ref, high_ref)
-        fluxes = [
-            mm(j_ref[e, side, :, :PAIR], near[side][block.slot(side, x, y, z)]).astype(BF)
-            for x, side in block.end_planes()
-            for e, y, z, _ in block.work(x, None)
-        ]
+def z_fluxes(block, halos, jp, after):
+    def kernel(first_ref, second_ref, j_ref, _, out_ref):
+        near = [None] * 4 + [first_ref, second_ref]
+        work = only(block.of_planes(block.end_planes()), Z)
+        fluxes = [mm(j_ref[e, f[0], :, :PAIR], pick(block, near, f[0], x, y, z)).astype(BF) for e, x, y, z, f in work]
         for i, flux in enumerate(fluxes):
             out_ref[i] = flux
 
     shape = jax.ShapeDtypeStruct((2 * block.plane, PAD, block.r), BF)
-    return call(kernel, shape, [*halos, jp], WAIT)
-
-
-def finish_sweep(block, halos, residual, inverse, jp, bt, bc):
+    return call(kernel, shape, [*halos, jp, after], WAIT_Z, specs=[VMEM, VMEM, VMEM, ANY])
+
+
+def x_fluxes(block, halos, jp, along_z=()):
+    count = 2 * block.plane
+
+    def kernel(low_ref, high_ref, j_ref, *refs):
+        near = (low_ref, high_ref)
+        work = only(block.of_planes(block.end_planes()), X)
+        fluxes = [mm(j_ref[e, f[0], :, :PAIR], pick(block, near, f[0], x, y, z)).astype(BF) for e, x, y, z, f in work]
+        for i, flux in enumerate(fluxes):
+            refs[-1][i] = flux
+        for ref in refs[:-1]:
+            refs[-1][count:] = ref[...]
+
+    shape = jax.ShapeDtypeStruct((count * (1 + len(along_z)), PAD, block.r), BF)
+    return call(kernel, shape, [*halos, jp, *along_z], WAIT)
+
+
+def finish_sweep(block, later, halos, residual, inverse, jp, bt, bc):
     def finish(work, ready, near, r_ref, v_ref, j_ref, bc_ref):
-        fluxes = [
-            [
-                ready[i]
-                if f < 2
-                else mm(j_ref[e, f, :, :PAIR], pick(near, f, block.slot(f, x, y, z))).astype(BF)
-                for f in faces
-            ]
-            for i, (e, x, y, z, faces) in enumerate(work)
-        ]
+        def flux(i, e, x, y, z, f):
+            if f in X:
+                return ready[i]
+            if ready is not None and block.split and f in Z:
+                return ready[2 * block.plane + i]
+            return mm(j_ref[e, f, :, :PAIR], pick(block, near, f, x, y, z)).astype(BF)
+
+        fluxes = [[flux(i, e, x, y, z, f) for f in faces] for i, (e, x, y, z, faces) in enumerate(work)]
         rest = [(r_ref[w[0]] - coupled(bc_ref, w[4], flux)).astype(BF) for w, flux in zip(work, fluxes)]
         return [mm(v_ref[w[0]], value).astype(BF) for w, value in zip(work, rest)]
 
-    def write(work, values, bt_ref, sends, a_ref):
-        send_traces(block, work, values, bt_ref, sends)
+    first = X + Z if later.split else X
+
+    def ends(*refs):
+        count = 2 if block.split else 4
+        ready, near, refs = refs[0], (None, None, *refs[1 : 1 + count]), refs[1 + count :]
+        fixed, (bt_ref, a_ref, *sends) = refs[:4], refs[4:]
+        work = block.of_planes(block.end_planes())
+        values = finish(work, ready, near, *fixed)
+        send_traces(later, only(work, first), values, bt_ref, [*sends[:2], None, None, *sends[2:]])
         for w, value in zip(work, values):
             a_ref[w[0]] = value
 
-    def ends(*refs):
-        ready, near, fixed, (bt_ref, a_ref, *sends) = refs[0], by_face(refs[1:5]), refs[5:9], refs[9:]
-        work = block.of_planes(block.end_planes())
-        values = finish(work, ready, near, *fixed)
-        write([(e, x, y, z, faces[:1]) for e, x, y, z, faces in work], values, bt_ref, sends, a_ref)
-
     def inner(*refs):
-        done_ref, near, fixed, (bt_ref, a_ref, *sends) = refs[0], by_face(refs[1:5]), refs[5:9], refs[9:]
+        done_ref, fixed, (bt_ref, a_ref, *sends) = refs[0], refs[5:9], refs[9:]
+        near = (None, None, *refs[1:3], *((None, None) if block.split else ()), *refs[3:5])
+        sends = [None, None, *sends[:2], *((None, None) if later.split else ()), *sends[2:]]
         work = block.of_planes(block.inner_planes())
-        outer = block.of_planes([(x, None) for x, _ in block.end_planes()])
+        outer = [(*w, done_ref[w[0]]) for w in block.of_planes(block.end_planes())]
         values = finish(work, None, near, *fixed)
-        write(work + outer, values + [done_ref[w[0]] for w in outer], bt_ref, [None, None, *sends], a_ref)
+        passed = only(outer, [f for f in range(6) if f not in first])
+        passed = [(w, o[5]) for w, o in zip(passed, outer) if w[4]]
+        send_traces(later, work, values, bt_ref, sends)
+        send_traces(later, [w for w, _ in passed], [v for _, v in passed], bt_ref, sends)
+        for w, value in zip(work, values):
+            a_ref[w[0]] = value
+        for w in outer:
+            a_ref[w[0]] = w[5]
 
     fixed = [residual, inverse, jp, bc, bt]
-    shapes = block.send_shapes()
+    shapes = later.send_shapes()
     whole = jax.ShapeDtypeStruct((block.nx * block.plane, block.c, block.r), BF)
-    ready = x_fluxes(block, halos[:2], jp)
-    part, *sends = call(ends, [whole] + shapes[:2], [ready, *z_then_y(halos), *fixed], FIRST)
-    a, *rest = call(inner, [whole] + shapes[2:], [part, *z_then_y(halos), *fixed], SECOND)
-    return a, [*sends, *rest]
+    early = [z_fluxes(block, halos[4:6], jp, residual)] if block.split else []
+    ready = x_fluxes(block, halos[:2], jp, early)
+    z = [] if block.split else halos[4:]
+    leaving = shapes[:2] + (shapes[4:6] if later.split else [])
+    part, *lead = call(ends, [whole] + leaving, [ready, *halos[2:4], *z, *fixed], FIRST)
+    operands = [part, *halos[2:4], *halos[-2:], *fixed]
+    a, *rest = call(inner, [whole] + shapes[2:4] + shapes[-2:], operands, SECOND)
+    return a, [*lead[:2], *rest[:2], *lead[2:], *rest[2:]]
 
 
 def local_gradient(block, a, jp, p, bt, after):
-    def kernel(a_ref, j_ref, p_ref, bt_ref, _, g_ref, t_ref):
+    columns = a.reshape(block.nx * block.ny, block.nz, block.c, block.r).transpose(0, 2, 1, 3)
+
+    def kernel(a_ref, w_ref, j_ref, p_ref, bt_ref, _, g_ref, out_ref, t_ref, sem):
+        leave = pltpu.make_async_copy(w_ref, out_ref, sem)
+        leave.start()
         fill_traces(block, a_ref, bt_ref, t_ref)
 
         def plane(x, carry):
@@ -398,16 +430,16 @@
             return carry
 
         lax.fori_loop(0, block.nx, plane, 0)
+        leave.wait()
 
     count = block.nx * block.plane
-    return call(
-        kernel,
-        jax.ShapeDtypeStruct((count, 8, block.r), F32),
-        [a, jp, p, bt, after],
-        LOCAL,
-        [pltpu.VMEM(((block.nx + 2) * block.plane, 6, PAD, block.r), BF)],
-        [VMEM] * 4 + [ANY],
-    )
+    shapes = [jax.ShapeDtypeStruct((count, 8, block.r), F32), jax.ShapeDtypeStruct(columns.shape, BF)]
+    scratch = [
+        pltpu.VMEM(((block.nx + 2) * block.plane, 6, PAD, block.r), BF),
+        pltpu.SemaphoreType.DMA(()),
+    ]
+    operands = [a, columns, jp, p, bt, after]
+    return call(kernel, shapes, operands, LOCAL, scratch, [VMEM] * 5 + [ANY], outs=[VMEM, HBM])
 
 
 def finish_gradient(block, halos, owns, inside, jp, p):
@@ -416,10 +448,9 @@
         for e, x, y, z, faces in work:
             rows = [jnp.zeros((1, block.r), F32)] * 8
             for f in faces:
-                place = block.slot(f, x, y, z)
                 both = jnp.concatenate([j_ref[e, f, :, :PAIR], p_ref[e, f, :, :PAIR]], axis=0)
-                both = mm(both, pick(near, f, place))
-                gap = pick(own, f, place).astype(F32) - both[PAD : PAD + PAIR]
+                both = mm(both, pick(block, near, f, x, y, z))
+                gap = pick(block, own, f, x, y, z).astype(F32) - both[PAD : PAD + PAIR]
                 rows[f] = jnp.sum(gap * both[:PAIR], axis=0, keepdims=True)
             total.append(g_ref[e] + jnp.concatenate(rows, axis=0))
         return total
@@ -461,9 +492,9 @@
         down = [(j, i) for i, j in up]
         halos.append(lax.ppermute(sends[2 * d + 1], axis, up))
         halos.append(lax.ppermute(sends[2 * d], axis, down))
-    for part, start in enumerate((0, 1)):
-        pairs = [(i, i + 1) for i in range(start, lax.axis_size("gz") - 1, 2)]
-        halos.append(lax.ppermute(sends[4 + part], "gz", pairs + [(j, i) for i, j in pairs]))
+    for i in range(4, len(sends)):
+        pairs = [(j, j + 1) for j in range(i % 2, lax.axis_size("gz") - 1, 2)]
+        halos.append(lax.ppermute(sends[i], "gz", pairs + [(k, j) for j, k in pairs]))
     return halos
 
 
@@ -483,24 +514,24 @@
     inverse = block_inverse.reshape(count, c, c)
     turns = orientation.reshape(count, 6, modes)
     jacobian = face_jacobian.reshape(count, 6, width, width)
-    jp, bc, ball = prepared(block, jacobian, turns, bt)
-
+    jp, p, bc, ball = prepared(block, jacobian, turns, bt)
+
+    parted = block.parted()
     for sweep in range(SWEEPS):
         halos = exchange(sends)
-        after = [halos[0]]
-        if sweep == SWEEPS - 1:
-            p = permutations(block, turns, adjoint)
-            after.append(p)
+        now, later = (block, parted) if sweep == 0 else (parted, block)
+        after = [halos[0] if sweep == 0 else halos[4]]
         residual = local_residual(block, adjoint, source, jp, bt, ball, after)
         if sweep == 0:
             inverse, residual = lax.optimization_barrier((block_inverse, residual))
             inverse = inverse.reshape(count, c, c)
-        adjoint, sends = finish_sweep(block, halos, residual, inverse, jp, bt, bc)
+        adjoint, sends = finish_sweep(now, later, halos, residual, inverse, jp, bt, bc)
     halos = exchange(sends)
-    inside = local_gradient(block, adjoint, jp, p, bt, halos[0])
+    inside, adjoint = local_gradient(block, adjoint, jp, p, bt, halos[0])
+    adjoint = adjoint.reshape(nx, ny, c, nz, r).transpose(0, 1, 3, 2, 4)
     gradient = finish_gradient(block, halos, sends, inside, jp, p)
     gradient = gradient.reshape(nx, ny, 6, nz, r).transpose(0, 1, 3, 2, 4)
-    return (adjoint.reshape(warm_start.shape), gradient)
+    return (adjoint, gradient)
 
 
 def solution(mesh):

time: 86.2 us -> 84.8 us (0.984)
  waiting for transfers between devices: 8.57 us -> 6.51 us
  starting transfers between devices: 41.7 us -> 43.4 us
  local copies, waits for them, and re-layouts: 3.93 us -> 2.8 us
    ppermute x6 -> x8, waiting for transfers between devices: 6.9 us -> 1.55 us  [exchange(): lax.ppermute(sends[i], 'gz', pairs + [(k, j) for j, k in pairs])]
    ppermute x6, waiting for transfers between devices: 0.28 us -> 3.57 us  [exchange(): halos.append(lax.ppermute(sends[2 * d + 1], axis, up))]
    ppermute x6, starting transfers between devices: 16.7 us -> 14 us  [exchange(): halos.append(lax.ppermute(sends[2 * d + 1], axis, up))]
    ppermute x6 -> x8, starting transfers between devices: 11.2 us -> 13.5 us  [exchange(): lax.ppermute(sends[i], 'gz', pairs + [(k, j) for j, k in pairs])]
    unnamed x17 -> x16, local copies, waits for them, and re-layouts: 3.41 us -> 1.21 us
    ppermute x6, starting transfers between devices: 13.8 us -> 15.8 us  [exchange(): halos.append(lax.ppermute(sends[2 * d], axis, down))]
    reshape x0 -> x1, local copies, waits for them, and re-layouts: none -> 1.11 us  [local_gradient(): a.reshape(block.nx * block.ny, block.nz, block.c, block.r)]
  transfers between devices with their start and end apart: 18 -> 20, of which waited for: 10 -> 5; matrix products, arithmetic and copies ran while one was open for 5% -> 3% of each run, Pallas kernels for 28% -> 30%
where the time goes in v4:
time: 84.8 us; the launch traced here: 83.8 us
  starting transfers between devices  43.4 us (51%)
  Pallas kernels  30.2 us (36%)
  waiting for transfers between devices  6.51 us (8%)
  local copies, waits for them, and re-layouts  2.8 us (3%)
  between operations  0.97 us (1%)
    pallas_call x15, Pallas kernels, call(): pl.pallas_call(kernel, out_shape=out_shape, in_specs=specs or [VMEM] * le...  30.2 us
    ppermute x6, starting transfers between devices, exchange(): halos.append(lax.ppermute(sends[2 * d], axis, down))  15.8 us
    ppermute x6, starting transfers between devices, exchange(): halos.append(lax.ppermute(sends[2 * d + 1], axis, up))  14 us
    ppermute x8, starting transfers between devices, exchange(): lax.ppermute(sends[i], 'gz', pairs + [(k, j) for j, k in pairs])  13.5 us
    ppermute x6, waiting for transfers between devices, exchange(): halos.append(lax.ppermute(sends[2 * d + 1], axis, up))  3.57 us
  transfers between devices with their start and end apart: 20, of which 5 were waited for; matrix products, arithmetic and copies ran while one was open for 3% of the time, Pallas kernels for 30%

profile of v4, /device:TPU:57, one launch (start us, length us, event | category | flops | bytes accessed | tf_op | source)
XLA Modules:
  0.0 83.8 jit_solution(1703253416909870052)
XLA Ops:
  0.6 1.9 %shard_map.77 = (bf16[4,152,128]{2,1,0:T(8,128)(2,1)S(1)}, bf16[4,152,128]{2,1,0:T(8,128)(2,1)S(1)}) custom-call(bf16[16,175,2,128]{3,2,1,0:T(2,128)(2,1)} %bitcast.31, bf16[6,75,175]{2,1,0:T(8,128)(2,1)} %bitcast.32), custom_call_target="tpu_custom_call" | custom-call | flops 1000 | tf_op jit(solution)/shard_map/pallas_call | solution.py:36
  2.6 0.0 copy-start.4
  2.6 6.1 %collective-permute-start = (bf16[4,152,128]{2,1,0:T(8,128)(2,1)S(1)}, bf16[4,152,128]{2,1,0:T(8,128)(2,1)S(1)}, u32[]{:S(2)}, u32[]{:S(2)}) collective-permute-start(bf16[4,152,128]{2,1,0:T(8,128)(2,1)S(1)} %get-tuple-element.34), channel_id=1, source_target_pairs={{0,32},{32,64},{64,96},{96,128},{128,160},{160,192},{192,224},{224... | collective-permute-start | bytes 466952 | tf_op jit(solution)/shard_map/ppermute | solution.py:493
  8.7 2.3 %collective-permute-start.1 = (bf16[4,152,128]{2,1,0:T(8,128)(2,1)S(1)}, bf16[4,152,128]{2,1,0:T(8,128)(2,1)S(1)}, u32[]{:S(2)}, u32[]{:S(2)}) collective-permute-start(bf16[4,152,128]{2,1,0:T(8,128)(2,1)S(1)} %get-tuple-element.35), channel_id=1, source_target_pairs={{32,0},{64,32},{96,64},{128,96},{160,128},{192,160},{224,192},{0,2... | collective-permute-start | bytes 466952 | tf_op jit(solution)/shard_map/ppermute | solution.py:494
  11.0 0.2 copy.15
  11.1 0.0 copy-done.4
  11.2 0.0 copy-start.5
  11.2 0.8 %shard_map.80 = (bf16[4,152,128]{2,1,0:T(8,128)(2,1)S(1)}, bf16[4,152,128]{2,1,0:T(8,128)(2,1)S(1)}, bf16[8,152,128]{2,1,0:T(8,128)(2,1)S(1)}, bf16[8,152,128]{2,1,0:T(8,128)(2,1)S(1)}) custom-call(bf16[32,175,128]{2,1,0:T(8,128)(2,1)S(1)} %bitcast.26, bf16[6,80,175]{2,1,0:T(8,128)(2,1)S(1)} %pad.4.bt_ref.refs_9_.refs_7_), custom_call_target="tpu_custom_call" | custom-call | flops 1000 | tf_op jit(solution)/shard_map/pallas_call | solution.py:36
  12.1 0.8 collective-permute-start.4
  12.9 3.6 %collective-permute-start.5 = (bf16[8,152,128]{2,1,0:T(8,128)(2,1)S(1)}, bf16[8,152,128]{2,1,0:T(8,128)(2,1)S(1)}, u32[]{:S(2)}, u32[]{:S(2)}) collective-permute-start(bf16[8,152,128]{2,1,0:T(8,128)(2,1)S(1)} %get-tuple-element.40), channel_id=1, source_target_pairs={{1,2},{2,1},{5,6},{6,5},{9,10},{10,9},{13,14},{14,13},{17,18},{18,... | collective-permute-start | bytes 933896 | tf_op jit(solution)/shard_map/ppermute | solution.py:497
  16.5 1.6 %collective-permute-start.2 = (bf16[4,152,128]{2,1,0:T(8,128)(2,1)S(1)}, bf16[4,152,128]{2,1,0:T(8,128)(2,1)S(1)}, u32[]{:S(2)}, u32[]{:S(2)}) collective-permute-start(bf16[4,152,128]{2,1,0:T(8,128)(2,1)S(1)} %get-tuple-element.37), channel_id=1, source_target_pairs={{0,4},{4,8},{8,12},{12,16},{16,20},{20,24},{24,28},{28,0},{1,5},{5... | collective-permute-start | bytes 466952 | tf_op jit(solution)/shard_map/ppermute | solution.py:493
  18.2 0.8 copy.13
  19.0 0.0 copy-start.3
  19.0 5.4 %shard_map.78 = (bf16[32,6,80,80]{3,2,1,0:T(8,128)(2,1)S(1)}, bf16[32,6,80,80]{3,2,1,0:T(8,128)(2,1)S(1)}, bf16[6,175,128]{2,1,0:T(8,128)(2,1)S(1)}, bf16[175,480]{1,0:T(8,128)(2,1)S(1)}) custom-call(bf16[32,6,75,75]{3,2,1,0:T(8,128)(2,1)S(1)} %bitcast.23, s32[32,6,15]{2,1,0:T(8,128)S(1)} %bitcast.30, bf16[6,80,175]{2,1,0:T(8,128)(2,1)S(1)} %pad.4.bt_ref.refs_9_.refs_7_), custom_call_target="tpu_custom_call" | custom-call | flops 1000 | tf_op jit(solution)/shard_map/pallas_call | solution.py:36
  24.4 0.2 copy.16
  24.6 0.0 collective-permute-done.low_ref.refs_0_
  24.7 0.2 collective-permute-start.3
  24.9 4.3 %shard_map.81.refs_5_ = f32[32,175,128]{2,1,0:T(8,128)S(1)} custom-call(bf16[32,175,128]{2,1,0:T(8,128)(2,1)S(1)} %bitcast.27, bf16[32,175,128]{2,1,0:T(8,128)(2,1)S(1)} %bitcast.24, bf16[32,6,80,80]{3,2,1,0:T(8,128)(2,1)S(1)} %get-tuple-element.36.j_ref.refs_7_.refs_5_.refs_4_.refs_8_, bf16[6,80,175]{2,1,0:T(8,128)(2,1)S(1)} %pad.4.bt_ref.refs_9_.refs_7_, ...), custom_call_target="tpu_custom_call" | custom-call | flops 1000 | tf_op jit(solution)/shard_map/pallas_call | solution.py:36
  29.2 0.4 copy.17
  29.6 0.0 collective-permute-done.1.high_ref
  29.6 0.3 shard_map.79.refs_0_
  30.0 0.0 collective-permute-done.2.refs_1_
  30.0 0.6 collective-permute-done.3.refs_2_
  30.5 0.0 collective-permute-done.4.refs_3_
  30.5 0.0 collective-permute-done.5.refs_4_
  30.5 1.7 %shard_map.82 = (bf16[32,175,128]{2,1,0:T(8,128)(2,1)S(1)}, bf16[4,152,128]{2,1,0:T(8,128)(2,1)S(1)}, bf16[4,152,128]{2,1,0:T(8,128)(2,1)S(1)}, bf16[4,152,128]{2,1,0:T(8,128)(2,1)S(1)}, bf16[4,152,128]{2,1,0:T(8,128)(2,1)S(1)}) custom-call(bf16[16,80,128]{2,1,0:T(8,128)(2,1)S(1)} %shard_map.79.refs_0_, ...), custom_call_target="tpu_custom_call" | custom-call | flops 1000 | tf_op jit(solution)/shard_map/pallas_call | solution.py:36
  32.3 0.1 collective-permute-start.8
  32.4 3.1 %collective-permute-start.9 = (bf16[4,152,128]{2,1,0:T(8,128)(2,1)S(1)}, bf16[4,152,128]{2,1,0:T(8,128)(2,1)S(1)}, u32[]{:S(2)}, u32[]{:S(2)}) collective-permute-start(bf16[4,152,128]{2,1,0:T(8,128)(2,1)S(1)} %get-tuple-element.48), channel_id=1, source_target_pairs={{1,2},{2,1},{5,6},{6,5},{9,10},{10,9},{13,14},{14,13},{17,18},{18,... | collective-permute-start | bytes 466952 | tf_op jit(solution)/shard_map/ppermute | solution.py:497
  35.5 1.7 %collective-permute-start.6 = (bf16[4,152,128]{2,1,0:T(8,128)(2,1)S(1)}, bf16[4,152,128]{2,1,0:T(8,128)(2,1)S(1)}, u32[]{:S(2)}, u32[]{:S(2)}) collective-permute-start(bf16[4,152,128]{2,1,0:T(8,128)(2,1)S(1)} %get-tuple-element.45), channel_id=1, source_target_pairs={{0,32},{32,64},{64,96},{96,128},{128,160},{160,192},{192,224},{224... | collective-permute-start | bytes 466952 | tf_op jit(solution)/shard_map/ppermute | solution.py:493
  37.2 5.9 %collective-permute-start.7 = (bf16[4,152,128]{2,1,0:T(8,128)(2,1)S(1)}, bf16[4,152,128]{2,1,0:T(8,128)(2,1)S(1)}, u32[]{:S(2)}, u32[]{:S(2)}) collective-permute-start(bf16[4,152,128]{2,1,0:T(8,128)(2,1)S(1)} %get-tuple-element.46), channel_id=1, source_target_pairs={{32,0},{64,32},{96,64},{128,96},{160,128},{192,160},{224,192},{0,2... | collective-permute-start | bytes 466952 | tf_op jit(solution)/shard_map/ppermute | solution.py:494
  43.1 1.6 %shard_map.83 = (bf16[32,175,128]{2,1,0:T(8,128)(2,1)S(1)}, bf16[4,152,128]{2,1,0:T(8,128)(2,1)S(1)}, bf16[4,152,128]{2,1,0:T(8,128)(2,1)S(1)}, bf16[4,152,128]{2,1,0:T(8,128)(2,1)S(1)}, bf16[4,152,128]{2,1,0:T(8,128)(2,1)S(1)}) custom-call(bf16[32,175,128]{2,1,0:T(8,128)(2,1)S(1)} %get-tuple-element.49.refs_0_, ...), custom_call_target="tpu_custom_call" | custom-call | flops 1000 | tf_op jit(solution)/shard_map/pallas_call | solution.py:36
  44.7 1.7 %collective-permute-start.10 = (bf16[4,152,128]{2,1,0:T(8,128)(2,1)S(1)}, bf16[4,152,128]{2,1,0:T(8,128)(2,1)S(1)}, u32[]{:S(2)}, u32[]{:S(2)}) collective-permute-start(bf16[4,152,128]{2,1,0:T(8,128)(2,1)S(1)} %get-tuple-element.51), channel_id=1, source_target_pairs={{0,4},{4,8},{8,12},{12,16},{16,20},{20,24},{24,28},{28,0},{1,5},{5... | collective-permute-start | bytes 466952 | tf_op jit(solution)/shard_map/ppermute | solution.py:493
  46.4 0.0 collective-permute-done.8.refs_0_.first_ref
  46.4 0.2 collective-permute-start.11
  46.6 4.3 %shard_map.84._.refs_3_.refs_5_ = f32[32,175,128]{2,1,0:T(8,128)S(1)} custom-call(bf16[32,175,128]{2,1,0:T(8,128)(2,1)S(1)} %get-tuple-element.50.a_ref, bf16[32,175,128]{2,1,0:T(8,128)(2,1)S(1)} %bitcast.25, bf16[32,6,80,80]{3,2,1,0:T(8,128)(2,1)S(1)} %get-tuple-element.36.j_ref.refs_7_.refs_5_.refs_4_.refs_8_, ...), custom_call_target="tpu_custom_call" | custom-call | flops 1000 | tf_op jit(solution)/shard_map/pallas_call | solution.py:36
  50.9 0.0 collective-permute-done.9.second_ref
  50.9 0.3 collective-permute-start.12
  51.2 0.3 shard_map.85.refs_0_
  51.5 2.5 %collective-permute-done.6.low_ref = bf16[4,152,128]{2,1,0:T(8,128)(2,1)S(1)} collective-permute-done((bf16[4,152,128]{2,1,0:T(8,128)(2,1)S(1)}, bf16[4,152,128]{2,1,0:T(8,128)(2,1)S(1)}, u32[]{:S(2)}, u32[]{:S(2)}) %collective-permute-start.6) | collective-permute-done | bytes 155680 | tf_op jit(solution)/shard_map/ppermute | solution.py:493
  54.0 2.0 %collective-permute-start.13 = (bf16[4,152,128]{2,1,0:T(8,128)(2,1)S(1)}, bf16[4,152,128]{2,1,0:T(8,128)(2,1)S(1)}, u32[]{:S(2)}, u32[]{:S(2)}) collective-permute-start(bf16[4,152,128]{2,1,0:T(8,128)(2,1)S(1)} %get-tuple-element.55), channel_id=1, source_target_pairs={{1,2},{2,1},{5,6},{6,5},{9,10},{10,9},{13,14},{14,13},{17,18},{18,... | collective-permute-start | bytes 466952 | tf_op jit(solution)/shard_map/ppermute | solution.py:497
  56.0 0.0 collective-permute-done.7.high_ref
  56.0 0.3 shard_map.86.refs_0_
  56.3 0.0 collective-permute-done.10.refs_1_
  56.3 0.0 collective-permute-done.11.refs_2_
  56.3 1.4 %shard_map.87 = (bf16[32,175,128]{2,1,0:T(8,128)(2,1)S(1)}, bf16[4,152,128]{2,1,0:T(8,128)(2,1)S(1)}, bf16[4,152,128]{2,1,0:T(8,128)(2,1)S(1)}) custom-call(bf16[32,80,128]{2,1,0:T(8,128)(2,1)S(1)} %shard_map.86.refs_0_, bf16[4,152,128]{2,1,0:T(8,128)(2,1)S(1)} %collective-permute-done.10.refs_1_, bf16[4,152,128]{2,1,0:T(8,128)(2,1)S(1)} %collective-permute-done.11.refs_2_, ...), custom_call_target="tpu_custom_call" | custom-call | flops 1000 | tf_op jit(solution)/shard_map/pallas_call | solution.py:36
  57.8 1.1 %collective-permute-start.14 = (bf16[4,152,128]{2,1,0:T(8,128)(2,1)S(1)}, bf16[4,152,128]{2,1,0:T(8,128)(2,1)S(1)}, u32[]{:S(2)}, u32[]{:S(2)}) collective-permute-start(bf16[4,152,128]{2,1,0:T(8,128)(2,1)S(1)} %get-tuple-element.58.refs_3_), channel_id=1, source_target_pairs={{0,32},{32,64},{64,96},{96,128},{128,160},{160,192},{192,224},{224... | collective-permute-start | bytes 466952 | tf_op jit(solution)/shard_map/ppermute | solution.py:493
  58.8 6.5 %collective-permute-start.19 = (bf16[4,152,128]{2,1,0:T(8,128)(2,1)S(1)}, bf16[4,152,128]{2,1,0:T(8,128)(2,1)S(1)}, u32[]{:S(2)}, u32[]{:S(2)}) collective-permute-start(bf16[4,152,128]{2,1,0:T(8,128)(2,1)S(1)} %get-tuple-element.64.refs_2_), channel_id=1, source_target_pairs={{32,0},{64,32},{96,64},{128,96},{160,128},{192,160},{224,192},{0,2... | collective-permute-start | bytes 466952 | tf_op jit(solution)/shard_map/ppermute | solution.py:494
  65.3 0.0 collective-permute-done.12.refs_3_
  65.3 0.0 collective-permute-done.13.refs_4_
  65.3 1.8 %shard_map.88 = (bf16[32,175,128]{2,1,0:T(8,128)(2,1)S(1)}, bf16[4,152,128]{2,1,0:T(8,128)(2,1)S(1)}, bf16[4,152,128]{2,1,0:T(8,128)(2,1)S(1)}, bf16[8,152,128]{2,1,0:T(8,128)(2,1)S(1)}, bf16[8,152,128]{2,1,0:T(8,128)(2,1)S(1)}) custom-call(bf16[32,175,128]{2,1,0:T(8,128)(2,1)S(1)} %get-tuple-element.53.refs_0_, ...), custom_call_target="tpu_custom_call" | custom-call | flops 1000 | tf_op jit(solution)/shard_map/pallas_call | solution.py:36
  67.1 0.1 collective-permute-start.15
  67.2 3.5 %collective-permute-start.16 = (bf16[8,152,128]{2,1,0:T(8,128)(2,1)S(1)}, bf16[8,152,128]{2,1,0:T(8,128)(2,1)S(1)}, u32[]{:S(2)}, u32[]{:S(2)}) collective-permute-start(bf16[8,152,128]{2,1,0:T(8,128)(2,1)S(1)} %get-tuple-element.61.refs_5_), channel_id=1, source_target_pairs={{1,2},{2,1},{5,6},{6,5},{9,10},{10,9},{13,14},{14,13},{17,18},{18,... | collective-permute-start | bytes 933896 | tf_op jit(solution)/shard_map/ppermute | solution.py:497
  70.7 1.9 %collective-permute-start.17 = (bf16[4,152,128]{2,1,0:T(8,128)(2,1)S(1)}, bf16[4,152,128]{2,1,0:T(8,128)(2,1)S(1)}, u32[]{:S(2)}, u32[]{:S(2)}) collective-permute-start(bf16[4,152,128]{2,1,0:T(8,128)(2,1)S(1)} %get-tuple-element.62.refs_7_), channel_id=1, source_target_pairs={{0,4},{4,8},{8,12},{12,16},{16,20},{20,24},{24,28},{28,0},{1,5},{5... | collective-permute-start | bytes 466952 | tf_op jit(solution)/shard_map/ppermute | solution.py:493
  72.6 1.1 %copy.20 = bf16[16,2,175,128]{3,1,2,0:T(2,128)(2,1)S(1)} copy(bf16[16,2,175,128]{3,2,1,0:T(8,128)(2,1)S(1)} %bitcast.28) | data formatting | bytes 2867200 | tf_op jit(solution)/shard_map/reshape | solution.py:411
  73.7 1.1 %collective-permute-done.14._.refs_0_ = bf16[4,152,128]{2,1,0:T(8,128)(2,1)S(1)} collective-permute-done((bf16[4,152,128]{2,1,0:T(8,128)(2,1)S(1)}, bf16[4,152,128]{2,1,0:T(8,128)(2,1)S(1)}, u32[]{:S(2)}, u32[]{:S(2)}) %collective-permute-start.14) | collective-permute-done | bytes 155680 | tf_op jit(solution)/shard_map/ppermute | solution.py:493
  74.8 0.7 collective-permute-start.18
  75.5 4.0 %shard_map.89 = (f32[32,8,128]{2,1,0:T(8,128)S(1)}, bf16[16,175,2,128]{3,2,1,0:T(2,128)(2,1)}) custom-call(bf16[32,175,128]{2,1,0:T(8,128)(2,1)S(1)} %get-tuple-element.56.a_ref, bf16[16,175,2,128]{3,2,1,0:T(2,128)(2,1)S(1)} %bitcast.29, bf16[32,6,80,80]{3,2,1,0:T(8,128)(2,1)S(1)} %get-tuple-element.36.j_ref.refs_7_.refs_5_.refs_4_.refs_8_, ...), custom_call_target="tpu_custom_call" | custom-call | flops 1000 | tf_op jit(solution)/shard_map/pallas_call | solution.py:36
  79.5 0.0 collective-permute-done.19.refs_1_
  79.5 0.4 shard_map.90.refs_10_
  79.9 0.0 collective-permute-done.17.refs_2_
  79.9 0.8 collective-permute-done.18.refs_3_
  80.7 0.0 collective-permute-done.15.refs_0_
  80.7 1.5 %collective-permute-done.16.refs_1_ = bf16[8,152,128]{2,1,0:T(8,128)(2,1)S(1)} collective-permute-done((bf16[8,152,128]{2,1,0:T(8,128)(2,1)S(1)}, bf16[8,152,128]{2,1,0:T(8,128)(2,1)S(1)}, u32[]{:S(2)}, u32[]{:S(2)}) %collective-permute-start.16) | collective-permute-done | bytes 311328 | tf_op jit(solution)/shard_map/ppermute | solution.py:497
  82.2 1.6 %shard_map.91 = f32[16,6,2,128]{3,2,1,0:T(2,128)} custom-call(bf16[8,152,128]{2,1,0:T(8,128)(2,1)S(1)} %collective-permute-done.15.refs_0_, bf16[8,152,128]{2,1,0:T(8,128)(2,1)S(1)} %collective-permute-done.16.refs_1_, bf16[4,152,128]{2,1,0:T(8,128)(2,1)S(1)} %collective-permute-done.17.refs_2_, bf16[4,152,128]{2,1,0:T(8,128)(2,1)S(1)} %collective-permute-done.18.refs_3_, ...), custom_call_target="tpu_custom_call" | custom-call | flops 1000 | tf_op jit(solution)/shard_map/pallas_call | solution.py:36
  (10 shorter events, 0.1 us)
Async XLA Ops:
  0.6 10.3 %copy-start = (bf16[4,4,2,175,128]{4,2,3,1,0:T(2,128)(2,1)S(1)}, bf16[4,4,2,175,128]{4,2,3,1,0:T(2,128)(2,1)}, u32[]{:S(2)}) copy-start(bf16[4,4,2,175,128]{4,2,3,1,0:T(2,128)(2,1)} %param.7) | copy-start | bytes 4300804
  2.6 8.6 %copy-start.4 = (bf16[6,175,75]{1,2,0:T(8,128)(2,1)S(1)}, bf16[6,175,75]{1,2,0:T(8,128)(2,1)}, u32[]{:S(2)}) copy-start(bf16[6,175,75]{1,2,0:T(8,128)(2,1)} %param.10) | copy-start | bytes 472504
  2.6 22.1 %collective-permute-start = (bf16[4,152,128]{2,1,0:T(8,128)(2,1)S(1)}, bf16[4,152,128]{2,1,0:T(8,128)(2,1)S(1)}, u32[]{:S(2)}, u32[]{:S(2)}) collective-permute-start(bf16[4,152,128]{2,1,0:T(8,128)(2,1)S(1)} %get-tuple-element.34), channel_id=1, source_target_pairs={{0,32},{32,64},{64,96},{96,128},{128,160},{160,192},{192,224},{224... | collective-permute-start | bytes 466952 | tf_op jit(solution)/shard_map/ppermute | solution.py:493
  8.7 21.0 %collective-permute-start.1 = (bf16[4,152,128]{2,1,0:T(8,128)(2,1)S(1)}, bf16[4,152,128]{2,1,0:T(8,128)(2,1)S(1)}, u32[]{:S(2)}, u32[]{:S(2)}) collective-permute-start(bf16[4,152,128]{2,1,0:T(8,128)(2,1)S(1)} %get-tuple-element.35), channel_id=1, source_target_pairs={{32,0},{64,32},{96,64},{128,96},{160,128},{192,160},{224,192},{0,2... | collective-permute-start | bytes 466952 | tf_op jit(solution)/shard_map/ppermute | solution.py:494
  11.0 7.2 %copy-start.1 = (bf16[4,4,2,6,75,75]{5,2,4,3,1,0:T(2,128)(2,1)S(1)}, bf16[4,4,2,6,75,75]{5,2,4,3,1,0:T(2,128)(2,1)}, u32[]{:S(2)}) copy-start(bf16[4,4,2,6,75,75]{5,2,4,3,1,0:T(2,128)(2,1)} %param.9) | copy-start | bytes 6480004
  11.2 7.0 %copy-start.5 = (s32[4,4,2,6,15]{4,2,3,1,0:T(2,128)S(1)}, s32[4,4,2,6,15]{4,2,3,1,0:T(2,128)}, u32[]{:S(2)}) copy-start(s32[4,4,2,6,15]{4,2,3,1,0:T(2,128)} %param.11) | copy-start | bytes 34564
  12.1 18.5 %collective-permute-start.4 = (bf16[8,152,128]{2,1,0:T(8,128)(2,1)S(1)}, bf16[8,152,128]{2,1,0:T(8,128)(2,1)S(1)}, u32[]{:S(2)}, u32[]{:S(2)}) collective-permute-start(bf16[8,152,128]{2,1,0:T(8,128)(2,1)S(1)} %get-tuple-element.39), channel_id=1, source_target_pairs={{0,1},{2,3},{1,0},{3,2},{4,5},{6,7},{5,4},{7,6},{8,9},{10,11},{9,8... | collective-permute-start | bytes 933896 | tf_op jit(solution)/shard_map/ppermute | solution.py:497
  12.9 17.7 %collective-permute-start.5 = (bf16[8,152,128]{2,1,0:T(8,128)(2,1)S(1)}, bf16[8,152,128]{2,1,0:T(8,128)(2,1)S(1)}, u32[]{:S(2)}, u32[]{:S(2)}) collective-permute-start(bf16[8,152,128]{2,1,0:T(8,128)(2,1)S(1)} %get-tuple-element.40), channel_id=1, source_target_pairs={{1,2},{2,1},{5,6},{6,5},{9,10},{10,9},{13,14},{14,13},{17,18},{18,... | collective-permute-start | bytes 933896 | tf_op jit(solution)/shard_map/ppermute | solution.py:497
  16.5 13.4 %collective-permute-start.2 = (bf16[4,152,128]{2,1,0:T(8,128)(2,1)S(1)}, bf16[4,152,128]{2,1,0:T(8,128)(2,1)S(1)}, u32[]{:S(2)}, u32[]{:S(2)}) collective-permute-start(bf16[4,152,128]{2,1,0:T(8,128)(2,1)S(1)} %get-tuple-element.37), channel_id=1, source_target_pairs={{0,4},{4,8},{8,12},{12,16},{16,20},{20,24},{24,28},{28,0},{1,5},{5... | collective-permute-start | bytes 466952 | tf_op jit(solution)/shard_map/ppermute | solution.py:493
  19.0 5.5 %copy-start.3 = (bf16[4,4,2,175,128]{4,2,3,1,0:T(2,128)(2,1)S(1)}, bf16[4,4,2,175,128]{4,2,3,1,0:T(2,128)(2,1)}, u32[]{:S(2)}) copy-start(bf16[4,4,2,175,128]{4,2,3,1,0:T(2,128)(2,1)} %param.6) | copy-start | bytes 4300804
  24.7 5.9 %collective-permute-start.3 = (bf16[4,152,128]{2,1,0:T(8,128)(2,1)S(1)}, bf16[4,152,128]{2,1,0:T(8,128)(2,1)S(1)}, u32[]{:S(2)}, u32[]{:S(2)}) collective-permute-start(bf16[4,152,128]{2,1,0:T(8,128)(2,1)S(1)} %get-tuple-element.38), channel_id=1, source_target_pairs={{4,0},{8,4},{12,8},{16,12},{20,16},{24,20},{28,24},{0,28},{5,1},{9... | collective-permute-start | bytes 466952 | tf_op jit(solution)/shard_map/ppermute | solution.py:494
  24.9 4.3 %copy-start.2 = (bf16[4,4,2,175,175]{4,2,3,1,0:T(2,128)(2,1)S(1)}, bf16[4,4,2,175,175]{4,2,3,1,0:T(2,128)(2,1)}, u32[]{:S(2)}) copy-start(bf16[4,4,2,175,175]{4,2,3,1,0:T(2,128)(2,1)} %param.8) | copy-start | bytes 5880004
  32.3 14.1 %collective-permute-start.8 = (bf16[4,152,128]{2,1,0:T(8,128)(2,1)S(1)}, bf16[4,152,128]{2,1,0:T(8,128)(2,1)S(1)}, u32[]{:S(2)}, u32[]{:S(2)}) collective-permute-start(bf16[4,152,128]{2,1,0:T(8,128)(2,1)S(1)} %get-tuple-element.47), channel_id=1, source_target_pairs={{0,1},{2,3},{1,0},{3,2},{4,5},{6,7},{5,4},{7,6},{8,9},{10,11},{9,8... | collective-permute-start | bytes 466952 | tf_op jit(solution)/shard_map/ppermute | solution.py:497
  32.4 18.5 %collective-permute-start.9 = (bf16[4,152,128]{2,1,0:T(8,128)(2,1)S(1)}, bf16[4,152,128]{2,1,0:T(8,128)(2,1)S(1)}, u32[]{:S(2)}, u32[]{:S(2)}) collective-permute-start(bf16[4,152,128]{2,1,0:T(8,128)(2,1)S(1)} %get-tuple-element.48), channel_id=1, source_target_pairs={{1,2},{2,1},{5,6},{6,5},{9,10},{10,9},{13,14},{14,13},{17,18},{18,... | collective-permute-start | bytes 466952 | tf_op jit(solution)/shard_map/ppermute | solution.py:497
  35.5 18.4 %collective-permute-start.6 = (bf16[4,152,128]{2,1,0:T(8,128)(2,1)S(1)}, bf16[4,152,128]{2,1,0:T(8,128)(2,1)S(1)}, u32[]{:S(2)}, u32[]{:S(2)}) collective-permute-start(bf16[4,152,128]{2,1,0:T(8,128)(2,1)S(1)} %get-tuple-element.45), channel_id=1, source_target_pairs={{0,32},{32,64},{64,96},{96,128},{128,160},{160,192},{192,224},{224... | collective-permute-start | bytes 466952 | tf_op jit(solution)/shard_map/ppermute | solution.py:493
  37.2 18.8 %collective-permute-start.7 = (bf16[4,152,128]{2,1,0:T(8,128)(2,1)S(1)}, bf16[4,152,128]{2,1,0:T(8,128)(2,1)S(1)}, u32[]{:S(2)}, u32[]{:S(2)}) collective-permute-start(bf16[4,152,128]{2,1,0:T(8,128)(2,1)S(1)} %get-tuple-element.46), channel_id=1, source_target_pairs={{32,0},{64,32},{96,64},{128,96},{160,128},{192,160},{224,192},{0,2... | collective-permute-start | bytes 466952 | tf_op jit(solution)/shard_map/ppermute | solution.py:494
  44.7 11.6 %collective-permute-start.10 = (bf16[4,152,128]{2,1,0:T(8,128)(2,1)S(1)}, bf16[4,152,128]{2,1,0:T(8,128)(2,1)S(1)}, u32[]{:S(2)}, u32[]{:S(2)}) collective-permute-start(bf16[4,152,128]{2,1,0:T(8,128)(2,1)S(1)} %get-tuple-element.51), channel_id=1, source_target_pairs={{0,4},{4,8},{8,12},{12,16},{16,20},{20,24},{24,28},{28,0},{1,5},{5... | collective-permute-start | bytes 466952 | tf_op jit(solution)/shard_map/ppermute | solution.py:493
  46.4 9.9 %collective-permute-start.11 = (bf16[4,152,128]{2,1,0:T(8,128)(2,1)S(1)}, bf16[4,152,128]{2,1,0:T(8,128)(2,1)S(1)}, u32[]{:S(2)}, u32[]{:S(2)}) collective-permute-start(bf16[4,152,128]{2,1,0:T(8,128)(2,1)S(1)} %get-tuple-element.52), channel_id=1, source_target_pairs={{4,0},{8,4},{12,8},{16,12},{20,16},{24,20},{28,24},{0,28},{5,1},{9... | collective-permute-start | bytes 466952 | tf_op jit(solution)/shard_map/ppermute | solution.py:494
  50.9 14.4 %collective-permute-start.12 = (bf16[4,152,128]{2,1,0:T(8,128)(2,1)S(1)}, bf16[4,152,128]{2,1,0:T(8,128)(2,1)S(1)}, u32[]{:S(2)}, u32[]{:S(2)}) collective-permute-start(bf16[4,152,128]{2,1,0:T(8,128)(2,1)S(1)} %get-tuple-element.54), channel_id=1, source_target_pairs={{0,1},{2,3},{1,0},{3,2},{4,5},{6,7},{5,4},{7,6},{8,9},{10,11},{9,8... | collective-permute-start | bytes 466952 | tf_op jit(solution)/shard_map/ppermute | solution.py:497
  54.0 11.4 %collective-permute-start.13 = (bf16[4,152,128]{2,1,0:T(8,128)(2,1)S(1)}, bf16[4,152,128]{2,1,0:T(8,128)(2,1)S(1)}, u32[]{:S(2)}, u32[]{:S(2)}) collective-permute-start(bf16[4,152,128]{2,1,0:T(8,128)(2,1)S(1)} %get-tuple-element.55), channel_id=1, source_target_pairs={{1,2},{2,1},{5,6},{6,5},{9,10},{10,9},{13,14},{14,13},{17,18},{18,... | collective-permute-start | bytes 466952 | tf_op jit(solution)/shard_map/ppermute | solution.py:497
  57.8 17.1 %collective-permute-start.14 = (bf16[4,152,128]{2,1,0:T(8,128)(2,1)S(1)}, bf16[4,152,128]{2,1,0:T(8,128)(2,1)S(1)}, u32[]{:S(2)}, u32[]{:S(2)}) collective-permute-start(bf16[4,152,128]{2,1,0:T(8,128)(2,1)S(1)} %get-tuple-element.58.refs_3_), channel_id=1, source_target_pairs={{0,32},{32,64},{64,96},{96,128},{128,160},{160,192},{192,224},{224... | collective-permute-start | bytes 466952 | tf_op jit(solution)/shard_map/ppermute | solution.py:493
  58.8 20.7 %collective-permute-start.19 = (bf16[4,152,128]{2,1,0:T(8,128)(2,1)S(1)}, bf16[4,152,128]{2,1,0:T(8,128)(2,1)S(1)}, u32[]{:S(2)}, u32[]{:S(2)}) collective-permute-start(bf16[4,152,128]{2,1,0:T(8,128)(2,1)S(1)} %get-tuple-element.64.refs_2_), channel_id=1, source_target_pairs={{32,0},{64,32},{96,64},{128,96},{160,128},{192,160},{224,192},{0,2... | collective-permute-start | bytes 466952 | tf_op jit(solution)/shard_map/ppermute | solution.py:494
  67.1 13.6 %collective-permute-start.15 = (bf16[8,152,128]{2,1,0:T(8,128)(2,1)S(1)}, bf16[8,152,128]{2,1,0:T(8,128)(2,1)S(1)}, u32[]{:S(2)}, u32[]{:S(2)}) collective-permute-start(bf16[8,152,128]{2,1,0:T(8,128)(2,1)S(1)} %get-tuple-element.60.refs_4_), channel_id=1, source_target_pairs={{0,1},{2,3},{1,0},{3,2},{4,5},{6,7},{5,4},{7,6},{8,9},{10,11},{9,8... | collective-permute-start | bytes 933896 | tf_op jit(solution)/shard_map/ppermute | solution.py:497
  67.2 15.0 %collective-permute-start.16 = (bf16[8,152,128]{2,1,0:T(8,128)(2,1)S(1)}, bf16[8,152,128]{2,1,0:T(8,128)(2,1)S(1)}, u32[]{:S(2)}, u32[]{:S(2)}) collective-permute-start(bf16[8,152,128]{2,1,0:T(8,128)(2,1)S(1)} %get-tuple-element.61.refs_5_), channel_id=1, source_target_pairs={{1,2},{2,1},{5,6},{6,5},{9,10},{10,9},{13,14},{14,13},{17,18},{18,... | collective-permute-start | bytes 933896 | tf_op jit(solution)/shard_map/ppermute | solution.py:497
  70.7 9.1 %collective-permute-start.17 = (bf16[4,152,128]{2,1,0:T(8,128)(2,1)S(1)}, bf16[4,152,128]{2,1,0:T(8,128)(2,1)S(1)}, u32[]{:S(2)}, u32[]{:S(2)}) collective-permute-start(bf16[4,152,128]{2,1,0:T(8,128)(2,1)S(1)} %get-tuple-element.62.refs_7_), channel_id=1, source_target_pairs={{0,4},{4,8},{8,12},{12,16},{16,20},{20,24},{24,28},{28,0},{1,5},{5... | collective-permute-start | bytes 466952 | tf_op jit(solution)/shard_map/ppermute | solution.py:493
  74.8 5.9 %collective-permute-start.18 = (bf16[4,152,128]{2,1,0:T(8,128)(2,1)S(1)}, bf16[4,152,128]{2,1,0:T(8,128)(2,1)S(1)}, u32[]{:S(2)}, u32[]{:S(2)}) collective-permute-start(bf16[4,152,128]{2,1,0:T(8,128)(2,1)S(1)} %get-tuple-element.63.refs_6_), channel_id=1, source_target_pairs={{4,0},{8,4},{12,8},{16,12},{20,16},{24,20},{28,24},{0,28},{5,1},{9... | collective-permute-start | bytes 466952 | tf_op jit(solution)/shard_map/ppermute | solution.py:494

commit v5 on v4

--- a/solution.py
+++ b/solution.py
@@ -111,32 +111,37 @@
         return (x + 1 + dx) * self.plane + (y + dy) * self.nz + (z + dz), face ^ 1
 
 
-def even_in_z():
-    return lax.rem(lax.axis_index("gz"), 2) == 0
+def even(axis):
+    return lax.rem(lax.axis_index(axis), 2) == 0
 
 
 def pick(block, near, f, x, y, z):
     place = block.slot(f, x, y, z)
-    if f < 4:
+    if f < 2:
         return near[f][place]
-    first, second = (near[i][place] for i in block.z_buffers(x))
-    return jnp.where(even_in_z(), *((second, first) if f == 4 else (first, second)))
+    axis, buffers = ("gy", (2, 3)) if f < 4 else ("gz", block.z_buffers(x))
+    first, second = (near[i][place] for i in buffers)
+    return jnp.where(even(axis), *((first, second) if f % 2 else (second, first)))
 
 
 def send_traces(block, work, values, bt, sends):
     traces = [mm(jnp.concatenate([bt[f] for f in w[4]], axis=0), a).astype(BF) for w, a in zip(work, values)]
-    low = None
+    low = {}
     for (_, x, y, z, faces), t in zip(work, traces):
         for i, f in enumerate(faces):
             piece = t[i * PAD : i * PAD + PAIR]
-            if f < 4:
+            if f < 2:
                 sends[f][block.slot(f, x, y, z)] = piece
-            elif f == 4:
-                low = piece
-            else:
-                first, second = (sends[i] for i in block.z_buffers(x))
-                first[block.slot(4, x, y, z)] = jnp.where(even_in_z(), piece, low)
-                second[block.slot(4, x, y, z)] = jnp.where(even_in_z(), low, piece)
+                continue
+            where = (2, z) if f < 4 else (4, y)
+            if f % 2 == 0:
+                low[where] = piece
+                continue
+            axis, buffers = ("gy", (2, 3)) if f < 4 else ("gz", block.z_buffers(x))
+            first, second = (sends[i] for i in buffers)
+            place, other = block.slot(f, x, y, z), low.pop(where)
+            first[place] = jnp.where(even(axis), piece, other)
+            second[place] = jnp.where(even(axis), other, piece)
 
 
 def only(work, faces):
@@ -222,15 +227,14 @@
         def elements(step, carry):
             places = [many * step + i for i in range(many)]
             turned = [one_hots(o_ref, e) for e in places]
-            moved = [
-                [mm_t(j_ref[e, f], turn[f]).astype(BF) for f in range(group)]
+            both = [
+                [mm_t(jnp.concatenate([eye, j_ref[e, f]], axis=0), turn[f]).astype(BF) for f in range(group)]
                 for e, turn in zip(places, turned)
             ]
-            placed = [[mm_t(eye, turn[f]).astype(BF) for f in range(group)] for turn in turned]
-            for e, values, perms in zip(places, moved, placed):
+            for e, values in zip(places, both):
                 for f in range(group):
-                    p_ref[e, f] = perms[f]
-                    jp_ref[e, f, :width] = values[f]
+                    p_ref[e, f] = values[f][:PAD]
+                    jp_ref[e, f, :width] = values[f][PAD:]
                     jp_ref[e, f, width:] = none
             return carry
 
@@ -485,16 +489,14 @@
 
 
 def exchange(sends):
-    halos = []
-    for d, axis in enumerate(("gx", "gy")):
+    count = lax.axis_size("gx")
+    up = [(i, (i + 1) % count) for i in range(count)]
+    halos = [lax.ppermute(sends[1], "gx", up), lax.ppermute(sends[0], "gx", [(j, i) for i, j in up])]
+    for i, send in enumerate(sends[2:]):
+        axis = "gy" if i < 2 else "gz"
         count = lax.axis_size(axis)
-        up = [(i, (i + 1) % count) for i in range(count)]
-        down = [(j, i) for i, j in up]
-        halos.append(lax.ppermute(sends[2 * d + 1], axis, up))
-        halos.append(lax.ppermute(sends[2 * d], axis, down))
-    for i in range(4, len(sends)):
-        pairs = [(j, j + 1) for j in range(i % 2, lax.axis_size("gz") - 1, 2)]
-        halos.append(lax.ppermute(sends[i], "gz", pairs + [(k, j) for j, k in pairs]))
+        pairs = [(j, (j + 1) % count) for j in range(i % 2, count if axis == "gy" else count - 1, 2)]
+        halos.append(lax.ppermute(send, axis, pairs + [(k, j) for j, k in pairs]))
     return halos
 
 

time: 84.8 us -> 84.8 us (level)
  starting transfers between devices: 43.4 us -> 45.5 us
  Pallas kernels: 30.2 us -> 28.4 us
  waiting for transfers between devices: 6.51 us -> 5.66 us
    ppermute x20, starting transfers between devices: 43.4 us -> 45.5 us  [the longest x14 22 us: exchange(): halos.append(lax.ppermute(send, axis, pairs + [(k, j) for j, k in pairs]))]
    pallas_call x15, Pallas kernels: 30.2 us -> 28.4 us  [call(): pl.pallas_call(kernel, out_shape=out_shape, in_specs=specs or [VMEM] * le...]
    ppermute x20, waiting for transfers between devices: 6.51 us -> 5.66 us  [the longest x14 3.55 us: exchange(): halos.append(lax.ppermute(send, axis, pairs + [(k, j) for j, k in pairs]))]
  transfers between devices with their start and end apart: 20 -> 20, of which waited for: 5 -> 5; matrix products, arithmetic and copies ran while one was open for 3% -> 3% of each run, Pallas kernels for 30% -> 28%
where the time goes in v5:
time: 84.8 us; the launch traced here: 83.4 us
  starting transfers between devices  45.5 us (54%)
  Pallas kernels  28.4 us (33%)
  waiting for transfers between devices  5.66 us (7%)
  local copies, waits for them, and re-layouts  2.81 us (3%)
  between operations  1 us (1%)
    pallas_call x15, Pallas kernels, call(): pl.pallas_call(kernel, out_shape=out_shape, in_specs=specs or [VMEM] * le...  28.4 us
    ppermute x14, starting transfers between devices, exchange(): halos.append(lax.ppermute(send, axis, pairs + [(k, j) for j, k in pairs]))  22 us
    ppermute x3, starting transfers between devices, exchange(): lax.ppermute(sends[0], 'gx', [(j, i) for i, j in up])  14.6 us
    ppermute x3, starting transfers between devices, exchange(): lax.ppermute(sends[1], 'gx', up)  8.86 us
    ppermute x14, waiting for transfers between devices, exchange(): halos.append(lax.ppermute(send, axis, pairs + [(k, j) for j, k in pairs]))  3.55 us
    ppermute x3, waiting for transfers between devices, exchange(): lax.ppermute(sends[1], 'gx', up)  2.1 us
  transfers between devices with their start and end apart: 20, of which 5 were waited for; matrix products, arithmetic and copies ran while one was open for 3% of the time, Pallas kernels for 28%

profile of v5, /device:TPU:57, one launch (start us, length us, event | category | flops | bytes accessed | tf_op | source)
XLA Modules:
  0.0 83.4 jit_solution(17001479589365864339)
XLA Ops:
  0.6 1.9 %shard_map.77 = (bf16[4,152,128]{2,1,0:T(8,128)(2,1)S(1)}, bf16[4,152,128]{2,1,0:T(8,128)(2,1)S(1)}) custom-call(bf16[16,175,2,128]{3,2,1,0:T(2,128)(2,1)} %bitcast.31, bf16[6,75,175]{2,1,0:T(8,128)(2,1)} %bitcast.32), custom_call_target="tpu_custom_call" | custom-call | flops 1000 | tf_op jit(solution)/shard_map/pallas_call | solution.py:36
  2.6 0.0 copy-start.4
  2.6 6.1 %collective-permute-start = (bf16[4,152,128]{2,1,0:T(8,128)(2,1)S(1)}, bf16[4,152,128]{2,1,0:T(8,128)(2,1)S(1)}, u32[]{:S(2)}, u32[]{:S(2)}) collective-permute-start(bf16[4,152,128]{2,1,0:T(8,128)(2,1)S(1)} %get-tuple-element.34), channel_id=1, source_target_pairs={{0,32},{32,64},{64,96},{96,128},{128,160},{160,192},{192,224},{224... | collective-permute-start | bytes 466952 | tf_op jit(solution)/shard_map/ppermute | solution.py:494
  8.7 2.3 %collective-permute-start.1 = (bf16[4,152,128]{2,1,0:T(8,128)(2,1)S(1)}, bf16[4,152,128]{2,1,0:T(8,128)(2,1)S(1)}, u32[]{:S(2)}, u32[]{:S(2)}) collective-permute-start(bf16[4,152,128]{2,1,0:T(8,128)(2,1)S(1)} %get-tuple-element.35), channel_id=1, source_target_pairs={{32,0},{64,32},{96,64},{128,96},{160,128},{192,160},{224,192},{0,2... | collective-permute-start | bytes 466952 | tf_op jit(solution)/shard_map/ppermute | solution.py:494
  11.0 0.2 copy.15
  11.2 0.0 copy-start.5
  11.2 0.8 %shard_map.80 = (bf16[4,152,128]{2,1,0:T(8,128)(2,1)S(1)}, bf16[4,152,128]{2,1,0:T(8,128)(2,1)S(1)}, bf16[8,152,128]{2,1,0:T(8,128)(2,1)S(1)}, bf16[8,152,128]{2,1,0:T(8,128)(2,1)S(1)}) custom-call(bf16[32,175,128]{2,1,0:T(8,128)(2,1)S(1)} %bitcast.26, bf16[6,80,175]{2,1,0:T(8,128)(2,1)S(1)} %pad.4.bt_ref.refs_9_.refs_7_), custom_call_target="tpu_custom_call" | custom-call | flops 1000 | tf_op jit(solution)/shard_map/pallas_call | solution.py:36
  12.1 0.8 collective-permute-start.4
  12.9 3.6 %collective-permute-start.5 = (bf16[8,152,128]{2,1,0:T(8,128)(2,1)S(1)}, bf16[8,152,128]{2,1,0:T(8,128)(2,1)S(1)}, u32[]{:S(2)}, u32[]{:S(2)}) collective-permute-start(bf16[8,152,128]{2,1,0:T(8,128)(2,1)S(1)} %get-tuple-element.40), channel_id=1, source_target_pairs={{1,2},{2,1},{5,6},{6,5},{9,10},{10,9},{13,14},{14,13},{17,18},{18,... | collective-permute-start | bytes 933896 | tf_op jit(solution)/shard_map/ppermute | solution.py:499
  16.5 1.9 %collective-permute-start.2 = (bf16[4,152,128]{2,1,0:T(8,128)(2,1)S(1)}, bf16[4,152,128]{2,1,0:T(8,128)(2,1)S(1)}, u32[]{:S(2)}, u32[]{:S(2)}) collective-permute-start(bf16[4,152,128]{2,1,0:T(8,128)(2,1)S(1)} %get-tuple-element.37), channel_id=1, source_target_pairs={{0,4},{8,12},{16,20},{24,28},{4,0},{12,8},{20,16},{28,24},{1,5},{9... | collective-permute-start | bytes 466952 | tf_op jit(solution)/shard_map/ppermute | solution.py:499
  18.4 0.8 copy.13
  19.2 0.0 copy-start.3
  19.2 3.4 %shard_map.78 = (bf16[32,6,80,80]{3,2,1,0:T(8,128)(2,1)S(1)}, bf16[32,6,80,80]{3,2,1,0:T(8,128)(2,1)S(1)}, bf16[6,175,128]{2,1,0:T(8,128)(2,1)S(1)}, bf16[175,480]{1,0:T(8,128)(2,1)S(1)}) custom-call(bf16[32,6,75,75]{3,2,1,0:T(8,128)(2,1)S(1)} %bitcast.23, s32[32,6,15]{2,1,0:T(8,128)S(1)} %bitcast.30, bf16[6,80,175]{2,1,0:T(8,128)(2,1)S(1)} %pad.4.bt_ref.refs_9_.refs_7_), custom_call_target="tpu_custom_call" | custom-call | flops 1000 | tf_op jit(solution)/shard_map/pallas_call | solution.py:36
  22.7 0.2 copy.16
  22.9 0.0 collective-permute-done.low_ref.refs_0_
  22.9 0.1 collective-permute-start.3
  23.0 0.0 copy-start.2
  23.0 4.3 %shard_map.81.refs_5_ = f32[32,175,128]{2,1,0:T(8,128)S(1)} custom-call(bf16[32,175,128]{2,1,0:T(8,128)(2,1)S(1)} %bitcast.27, bf16[32,175,128]{2,1,0:T(8,128)(2,1)S(1)} %bitcast.24, bf16[32,6,80,80]{3,2,1,0:T(8,128)(2,1)S(1)} %get-tuple-element.36.j_ref.refs_7_.refs_5_.refs_4_.refs_8_, bf16[6,80,175]{2,1,0:T(8,128)(2,1)S(1)} %pad.4.bt_ref.refs_9_.refs_7_, ...), custom_call_target="tpu_custom_call" | custom-call | flops 1000 | tf_op jit(solution)/shard_map/pallas_call | solution.py:36
  27.3 0.4 copy.17
  27.8 0.0 collective-permute-done.1.high_ref
  27.8 0.3 shard_map.79.refs_0_
  28.1 0.0 collective-permute-done.2.refs_1_
  28.1 0.7 collective-permute-done.3.refs_2_
  28.9 0.8 collective-permute-done.4.refs_3_
  29.7 0.5 collective-permute-done.5.refs_4_
  30.2 1.7 %shard_map.82 = (bf16[32,175,128]{2,1,0:T(8,128)(2,1)S(1)}, bf16[4,152,128]{2,1,0:T(8,128)(2,1)S(1)}, bf16[4,152,128]{2,1,0:T(8,128)(2,1)S(1)}, bf16[4,152,128]{2,1,0:T(8,128)(2,1)S(1)}, bf16[4,152,128]{2,1,0:T(8,128)(2,1)S(1)}) custom-call(bf16[16,80,128]{2,1,0:T(8,128)(2,1)S(1)} %shard_map.79.refs_0_, ...), custom_call_target="tpu_custom_call" | custom-call | flops 1000 | tf_op jit(solution)/shard_map/pallas_call | solution.py:36
  31.9 0.2 collective-permute-start.8
  32.1 3.4 %collective-permute-start.9 = (bf16[4,152,128]{2,1,0:T(8,128)(2,1)S(1)}, bf16[4,152,128]{2,1,0:T(8,128)(2,1)S(1)}, u32[]{:S(2)}, u32[]{:S(2)}) collective-permute-start(bf16[4,152,128]{2,1,0:T(8,128)(2,1)S(1)} %get-tuple-element.48), channel_id=1, source_target_pairs={{1,2},{2,1},{5,6},{6,5},{9,10},{10,9},{13,14},{14,13},{17,18},{18,... | collective-permute-start | bytes 466952 | tf_op jit(solution)/shard_map/ppermute | solution.py:499
  35.5 1.5 %collective-permute-start.6 = (bf16[4,152,128]{2,1,0:T(8,128)(2,1)S(1)}, bf16[4,152,128]{2,1,0:T(8,128)(2,1)S(1)}, u32[]{:S(2)}, u32[]{:S(2)}) collective-permute-start(bf16[4,152,128]{2,1,0:T(8,128)(2,1)S(1)} %get-tuple-element.45), channel_id=1, source_target_pairs={{0,32},{32,64},{64,96},{96,128},{128,160},{160,192},{192,224},{224... | collective-permute-start | bytes 466952 | tf_op jit(solution)/shard_map/ppermute | solution.py:494
  37.0 6.1 %collective-permute-start.7 = (bf16[4,152,128]{2,1,0:T(8,128)(2,1)S(1)}, bf16[4,152,128]{2,1,0:T(8,128)(2,1)S(1)}, u32[]{:S(2)}, u32[]{:S(2)}) collective-permute-start(bf16[4,152,128]{2,1,0:T(8,128)(2,1)S(1)} %get-tuple-element.46), channel_id=1, source_target_pairs={{32,0},{64,32},{96,64},{128,96},{160,128},{192,160},{224,192},{0,2... | collective-permute-start | bytes 466952 | tf_op jit(solution)/shard_map/ppermute | solution.py:494
  43.1 1.6 %shard_map.83 = (bf16[32,175,128]{2,1,0:T(8,128)(2,1)S(1)}, bf16[4,152,128]{2,1,0:T(8,128)(2,1)S(1)}, bf16[4,152,128]{2,1,0:T(8,128)(2,1)S(1)}, bf16[4,152,128]{2,1,0:T(8,128)(2,1)S(1)}, bf16[4,152,128]{2,1,0:T(8,128)(2,1)S(1)}) custom-call(bf16[32,175,128]{2,1,0:T(8,128)(2,1)S(1)} %get-tuple-element.49.refs_0_, ...), custom_call_target="tpu_custom_call" | custom-call | flops 1000 | tf_op jit(solution)/shard_map/pallas_call | solution.py:36
  44.7 1.9 %collective-permute-start.10 = (bf16[4,152,128]{2,1,0:T(8,128)(2,1)S(1)}, bf16[4,152,128]{2,1,0:T(8,128)(2,1)S(1)}, u32[]{:S(2)}, u32[]{:S(2)}) collective-permute-start(bf16[4,152,128]{2,1,0:T(8,128)(2,1)S(1)} %get-tuple-element.51), channel_id=1, source_target_pairs={{0,4},{8,12},{16,20},{24,28},{4,0},{12,8},{20,16},{28,24},{1,5},{9... | collective-permute-start | bytes 466952 | tf_op jit(solution)/shard_map/ppermute | solution.py:499
  46.6 0.0 collective-permute-done.8.refs_0_.first_ref
  46.6 0.0 collective-permute-start.11
  46.6 4.3 %shard_map.84._.refs_3_.refs_5_ = f32[32,175,128]{2,1,0:T(8,128)S(1)} custom-call(bf16[32,175,128]{2,1,0:T(8,128)(2,1)S(1)} %get-tuple-element.50.a_ref, bf16[32,175,128]{2,1,0:T(8,128)(2,1)S(1)} %bitcast.25, bf16[32,6,80,80]{3,2,1,0:T(8,128)(2,1)S(1)} %get-tuple-element.36.j_ref.refs_7_.refs_5_.refs_4_.refs_8_, ...), custom_call_target="tpu_custom_call" | custom-call | flops 1000 | tf_op jit(solution)/shard_map/pallas_call | solution.py:36
  51.0 0.0 collective-permute-done.9.second_ref
  51.0 0.1 collective-permute-start.12
  51.1 0.3 shard_map.85.refs_0_
  51.4 2.1 %collective-permute-done.6.low_ref = bf16[4,152,128]{2,1,0:T(8,128)(2,1)S(1)} collective-permute-done((bf16[4,152,128]{2,1,0:T(8,128)(2,1)S(1)}, bf16[4,152,128]{2,1,0:T(8,128)(2,1)S(1)}, u32[]{:S(2)}, u32[]{:S(2)}) %collective-permute-start.6) | collective-permute-done | bytes 155680 | tf_op jit(solution)/shard_map/ppermute | solution.py:494
  53.5 2.2 %collective-permute-start.13 = (bf16[4,152,128]{2,1,0:T(8,128)(2,1)S(1)}, bf16[4,152,128]{2,1,0:T(8,128)(2,1)S(1)}, u32[]{:S(2)}, u32[]{:S(2)}) collective-permute-start(bf16[4,152,128]{2,1,0:T(8,128)(2,1)S(1)} %get-tuple-element.55), channel_id=1, source_target_pairs={{1,2},{2,1},{5,6},{6,5},{9,10},{10,9},{13,14},{14,13},{17,18},{18,... | collective-permute-start | bytes 466952 | tf_op jit(solution)/shard_map/ppermute | solution.py:499
  55.7 0.0 collective-permute-done.7.high_ref
  55.7 0.3 shard_map.86.refs_0_
  56.0 0.0 collective-permute-done.10.refs_1_
  56.0 0.0 collective-permute-done.11.refs_2_
  56.1 1.5 %shard_map.87 = (bf16[32,175,128]{2,1,0:T(8,128)(2,1)S(1)}, bf16[4,152,128]{2,1,0:T(8,128)(2,1)S(1)}, bf16[4,152,128]{2,1,0:T(8,128)(2,1)S(1)}) custom-call(bf16[32,80,128]{2,1,0:T(8,128)(2,1)S(1)} %shard_map.86.refs_0_, bf16[4,152,128]{2,1,0:T(8,128)(2,1)S(1)} %collective-permute-done.10.refs_1_, bf16[4,152,128]{2,1,0:T(8,128)(2,1)S(1)} %collective-permute-done.11.refs_2_, ...), custom_call_target="tpu_custom_call" | custom-call | flops 1000 | tf_op jit(solution)/shard_map/pallas_call | solution.py:36
  57.5 1.3 %collective-permute-start.14 = (bf16[4,152,128]{2,1,0:T(8,128)(2,1)S(1)}, bf16[4,152,128]{2,1,0:T(8,128)(2,1)S(1)}, u32[]{:S(2)}, u32[]{:S(2)}) collective-permute-start(bf16[4,152,128]{2,1,0:T(8,128)(2,1)S(1)} %get-tuple-element.58.refs_3_), channel_id=1, source_target_pairs={{0,32},{32,64},{64,96},{96,128},{128,160},{160,192},{192,224},{224... | collective-permute-start | bytes 466952 | tf_op jit(solution)/shard_map/ppermute | solution.py:494
  58.8 6.2 %collective-permute-start.19 = (bf16[4,152,128]{2,1,0:T(8,128)(2,1)S(1)}, bf16[4,152,128]{2,1,0:T(8,128)(2,1)S(1)}, u32[]{:S(2)}, u32[]{:S(2)}) collective-permute-start(bf16[4,152,128]{2,1,0:T(8,128)(2,1)S(1)} %get-tuple-element.64.refs_2_), channel_id=1, source_target_pairs={{32,0},{64,32},{96,64},{128,96},{160,128},{192,160},{224,192},{0,2... | collective-permute-start | bytes 466952 | tf_op jit(solution)/shard_map/ppermute | solution.py:494
  65.1 0.0 collective-permute-done.12.refs_3_
  65.1 0.0 collective-permute-done.13.refs_4_
  65.1 1.8 %shard_map.88 = (bf16[32,175,128]{2,1,0:T(8,128)(2,1)S(1)}, bf16[4,152,128]{2,1,0:T(8,128)(2,1)S(1)}, bf16[4,152,128]{2,1,0:T(8,128)(2,1)S(1)}, bf16[8,152,128]{2,1,0:T(8,128)(2,1)S(1)}, bf16[8,152,128]{2,1,0:T(8,128)(2,1)S(1)}) custom-call(bf16[32,175,128]{2,1,0:T(8,128)(2,1)S(1)} %get-tuple-element.53.refs_0_, ...), custom_call_target="tpu_custom_call" | custom-call | flops 1000 | tf_op jit(solution)/shard_map/pallas_call | solution.py:36
  66.9 0.1 collective-permute-start.15
  67.0 3.1 %collective-permute-start.16 = (bf16[8,152,128]{2,1,0:T(8,128)(2,1)S(1)}, bf16[8,152,128]{2,1,0:T(8,128)(2,1)S(1)}, u32[]{:S(2)}, u32[]{:S(2)}) collective-permute-start(bf16[8,152,128]{2,1,0:T(8,128)(2,1)S(1)} %get-tuple-element.61.refs_5_), channel_id=1, source_target_pairs={{1,2},{2,1},{5,6},{6,5},{9,10},{10,9},{13,14},{14,13},{17,18},{18,... | collective-permute-start | bytes 933896 | tf_op jit(solution)/shard_map/ppermute | solution.py:499
  70.1 4.5 %collective-permute-start.17 = (bf16[4,152,128]{2,1,0:T(8,128)(2,1)S(1)}, bf16[4,152,128]{2,1,0:T(8,128)(2,1)S(1)}, u32[]{:S(2)}, u32[]{:S(2)}) collective-permute-start(bf16[4,152,128]{2,1,0:T(8,128)(2,1)S(1)} %get-tuple-element.62.refs_6_), channel_id=1, source_target_pairs={{0,4},{8,12},{16,20},{24,28},{4,0},{12,8},{20,16},{28,24},{1,5},{9... | collective-permute-start | bytes 466952 | tf_op jit(solution)/shard_map/ppermute | solution.py:499
  74.6 1.1 %copy.20 = bf16[16,2,175,128]{3,1,2,0:T(2,128)(2,1)S(1)} copy(bf16[16,2,175,128]{3,2,1,0:T(8,128)(2,1)S(1)} %bitcast.28) | data formatting | bytes 2867200 | tf_op jit(solution)/shard_map/reshape | solution.py:415
  75.7 0.0 collective-permute-done.14._.refs_0_
  75.7 0.1 collective-permute-start.18
  75.8 4.0 %shard_map.89 = (f32[32,8,128]{2,1,0:T(8,128)S(1)}, bf16[16,175,2,128]{3,2,1,0:T(2,128)(2,1)}) custom-call(bf16[32,175,128]{2,1,0:T(8,128)(2,1)S(1)} %get-tuple-element.56.a_ref, bf16[16,175,2,128]{3,2,1,0:T(2,128)(2,1)S(1)} %bitcast.29, bf16[32,6,80,80]{3,2,1,0:T(8,128)(2,1)S(1)} %get-tuple-element.36.j_ref.refs_7_.refs_5_.refs_4_.refs_8_, ...), custom_call_target="tpu_custom_call" | custom-call | flops 1000 | tf_op jit(solution)/shard_map/pallas_call | solution.py:36
  79.8 0.0 collective-permute-done.19.refs_1_
  79.8 0.4 shard_map.90.refs_10_
  80.2 0.0 collective-permute-done.17.refs_2_
  80.2 1.5 %collective-permute-done.18.refs_3_ = bf16[4,152,128]{2,1,0:T(8,128)(2,1)S(1)} collective-permute-done((bf16[4,152,128]{2,1,0:T(8,128)(2,1)S(1)}, bf16[4,152,128]{2,1,0:T(8,128)(2,1)S(1)}, u32[]{:S(2)}, u32[]{:S(2)}) %collective-permute-start.18) | collective-permute-done | bytes 155680 | tf_op jit(solution)/shard_map/ppermute | solution.py:499
  81.7 0.0 collective-permute-done.15.refs_0_
  81.7 0.0 collective-permute-done.16.refs_1_
  81.7 1.7 %shard_map.91 = f32[16,6,2,128]{3,2,1,0:T(2,128)} custom-call(bf16[8,152,128]{2,1,0:T(8,128)(2,1)S(1)} %collective-permute-done.15.refs_0_, bf16[8,152,128]{2,1,0:T(8,128)(2,1)S(1)} %collective-permute-done.16.refs_1_, bf16[4,152,128]{2,1,0:T(8,128)(2,1)S(1)} %collective-permute-done.17.refs_2_, bf16[4,152,128]{2,1,0:T(8,128)(2,1)S(1)} %collective-permute-done.18.refs_3_, ...), custom_call_target="tpu_custom_call" | custom-call | flops 1000 | tf_op jit(solution)/shard_map/pallas_call | solution.py:36
  (10 shorter events, 0.1 us)
Async XLA Ops:
  0.6 10.3 %copy-start = (bf16[4,4,2,175,128]{4,2,3,1,0:T(2,128)(2,1)S(1)}, bf16[4,4,2,175,128]{4,2,3,1,0:T(2,128)(2,1)}, u32[]{:S(2)}) copy-start(bf16[4,4,2,175,128]{4,2,3,1,0:T(2,128)(2,1)} %param.7) | copy-start | bytes 4300804
  2.6 8.6 %copy-start.4 = (bf16[6,175,75]{1,2,0:T(8,128)(2,1)S(1)}, bf16[6,175,75]{1,2,0:T(8,128)(2,1)}, u32[]{:S(2)}) copy-start(bf16[6,175,75]{1,2,0:T(8,128)(2,1)} %param.10) | copy-start | bytes 472504
  2.6 20.3 %collective-permute-start = (bf16[4,152,128]{2,1,0:T(8,128)(2,1)S(1)}, bf16[4,152,128]{2,1,0:T(8,128)(2,1)S(1)}, u32[]{:S(2)}, u32[]{:S(2)}) collective-permute-start(bf16[4,152,128]{2,1,0:T(8,128)(2,1)S(1)} %get-tuple-element.34), channel_id=1, source_target_pairs={{0,32},{32,64},{64,96},{96,128},{128,160},{160,192},{192,224},{224... | collective-permute-start | bytes 466952 | tf_op jit(solution)/shard_map/ppermute | solution.py:494
  8.7 19.1 %collective-permute-start.1 = (bf16[4,152,128]{2,1,0:T(8,128)(2,1)S(1)}, bf16[4,152,128]{2,1,0:T(8,128)(2,1)S(1)}, u32[]{:S(2)}, u32[]{:S(2)}) collective-permute-start(bf16[4,152,128]{2,1,0:T(8,128)(2,1)S(1)} %get-tuple-element.35), channel_id=1, source_target_pairs={{32,0},{64,32},{96,64},{128,96},{160,128},{192,160},{224,192},{0,2... | collective-permute-start | bytes 466952 | tf_op jit(solution)/shard_map/ppermute | solution.py:494
  11.0 7.5 %copy-start.1 = (bf16[4,4,2,6,75,75]{5,2,4,3,1,0:T(2,128)(2,1)S(1)}, bf16[4,4,2,6,75,75]{5,2,4,3,1,0:T(2,128)(2,1)}, u32[]{:S(2)}) copy-start(bf16[4,4,2,6,75,75]{5,2,4,3,1,0:T(2,128)(2,1)} %param.9) | copy-start | bytes 6480004
  11.2 7.2 %copy-start.5 = (s32[4,4,2,6,15]{4,2,3,1,0:T(2,128)S(1)}, s32[4,4,2,6,15]{4,2,3,1,0:T(2,128)}, u32[]{:S(2)}) copy-start(s32[4,4,2,6,15]{4,2,3,1,0:T(2,128)} %param.11) | copy-start | bytes 34564
  12.1 17.6 %collective-permute-start.4 = (bf16[8,152,128]{2,1,0:T(8,128)(2,1)S(1)}, bf16[8,152,128]{2,1,0:T(8,128)(2,1)S(1)}, u32[]{:S(2)}, u32[]{:S(2)}) collective-permute-start(bf16[8,152,128]{2,1,0:T(8,128)(2,1)S(1)} %get-tuple-element.39), channel_id=1, source_target_pairs={{0,1},{2,3},{1,0},{3,2},{4,5},{6,7},{5,4},{7,6},{8,9},{10,11},{9,8... | collective-permute-start | bytes 933896 | tf_op jit(solution)/shard_map/ppermute | solution.py:499
  12.9 17.3 %collective-permute-start.5 = (bf16[8,152,128]{2,1,0:T(8,128)(2,1)S(1)}, bf16[8,152,128]{2,1,0:T(8,128)(2,1)S(1)}, u32[]{:S(2)}, u32[]{:S(2)}) collective-permute-start(bf16[8,152,128]{2,1,0:T(8,128)(2,1)S(1)} %get-tuple-element.40), channel_id=1, source_target_pairs={{1,2},{2,1},{5,6},{6,5},{9,10},{10,9},{13,14},{14,13},{17,18},{18,... | collective-permute-start | bytes 933896 | tf_op jit(solution)/shard_map/ppermute | solution.py:499
  16.5 11.6 %collective-permute-start.2 = (bf16[4,152,128]{2,1,0:T(8,128)(2,1)S(1)}, bf16[4,152,128]{2,1,0:T(8,128)(2,1)S(1)}, u32[]{:S(2)}, u32[]{:S(2)}) collective-permute-start(bf16[4,152,128]{2,1,0:T(8,128)(2,1)S(1)} %get-tuple-element.37), channel_id=1, source_target_pairs={{0,4},{8,12},{16,20},{24,28},{4,0},{12,8},{20,16},{28,24},{1,5},{9... | collective-permute-start | bytes 466952 | tf_op jit(solution)/shard_map/ppermute | solution.py:499
  19.2 3.5 %copy-start.3 = (bf16[4,4,2,175,128]{4,2,3,1,0:T(2,128)(2,1)S(1)}, bf16[4,4,2,175,128]{4,2,3,1,0:T(2,128)(2,1)}, u32[]{:S(2)}) copy-start(bf16[4,4,2,175,128]{4,2,3,1,0:T(2,128)(2,1)} %param.6) | copy-start | bytes 4300804
  22.9 6.0 %collective-permute-start.3 = (bf16[4,152,128]{2,1,0:T(8,128)(2,1)S(1)}, bf16[4,152,128]{2,1,0:T(8,128)(2,1)S(1)}, u32[]{:S(2)}, u32[]{:S(2)}) collective-permute-start(bf16[4,152,128]{2,1,0:T(8,128)(2,1)S(1)} %get-tuple-element.38), channel_id=1, source_target_pairs={{4,8},{12,16},{20,24},{28,0},{8,4},{16,12},{24,20},{0,28},{5,9},{1... | collective-permute-start | bytes 466952 | tf_op jit(solution)/shard_map/ppermute | solution.py:499
  23.0 4.3 %copy-start.2 = (bf16[4,4,2,175,175]{4,2,3,1,0:T(2,128)(2,1)S(1)}, bf16[4,4,2,175,175]{4,2,3,1,0:T(2,128)(2,1)}, u32[]{:S(2)}) copy-start(bf16[4,4,2,175,175]{4,2,3,1,0:T(2,128)(2,1)} %param.8) | copy-start | bytes 5880004
  31.9 14.7 %collective-permute-start.8 = (bf16[4,152,128]{2,1,0:T(8,128)(2,1)S(1)}, bf16[4,152,128]{2,1,0:T(8,128)(2,1)S(1)}, u32[]{:S(2)}, u32[]{:S(2)}) collective-permute-start(bf16[4,152,128]{2,1,0:T(8,128)(2,1)S(1)} %get-tuple-element.47), channel_id=1, source_target_pairs={{0,1},{2,3},{1,0},{3,2},{4,5},{6,7},{5,4},{7,6},{8,9},{10,11},{9,8... | collective-permute-start | bytes 466952 | tf_op jit(solution)/shard_map/ppermute | solution.py:499
  32.1 18.9 %collective-permute-start.9 = (bf16[4,152,128]{2,1,0:T(8,128)(2,1)S(1)}, bf16[4,152,128]{2,1,0:T(8,128)(2,1)S(1)}, u32[]{:S(2)}, u32[]{:S(2)}) collective-permute-start(bf16[4,152,128]{2,1,0:T(8,128)(2,1)S(1)} %get-tuple-element.48), channel_id=1, source_target_pairs={{1,2},{2,1},{5,6},{6,5},{9,10},{10,9},{13,14},{14,13},{17,18},{18,... | collective-permute-start | bytes 466952 | tf_op jit(solution)/shard_map/ppermute | solution.py:499
  35.5 18.0 %collective-permute-start.6 = (bf16[4,152,128]{2,1,0:T(8,128)(2,1)S(1)}, bf16[4,152,128]{2,1,0:T(8,128)(2,1)S(1)}, u32[]{:S(2)}, u32[]{:S(2)}) collective-permute-start(bf16[4,152,128]{2,1,0:T(8,128)(2,1)S(1)} %get-tuple-element.45), channel_id=1, source_target_pairs={{0,32},{32,64},{64,96},{96,128},{128,160},{160,192},{192,224},{224... | collective-permute-start | bytes 466952 | tf_op jit(solution)/shard_map/ppermute | solution.py:494
  37.0 18.7 %collective-permute-start.7 = (bf16[4,152,128]{2,1,0:T(8,128)(2,1)S(1)}, bf16[4,152,128]{2,1,0:T(8,128)(2,1)S(1)}, u32[]{:S(2)}, u32[]{:S(2)}) collective-permute-start(bf16[4,152,128]{2,1,0:T(8,128)(2,1)S(1)} %get-tuple-element.46), channel_id=1, source_target_pairs={{32,0},{64,32},{96,64},{128,96},{160,128},{192,160},{224,192},{0,2... | collective-permute-start | bytes 466952 | tf_op jit(solution)/shard_map/ppermute | solution.py:494
  44.7 11.3 %collective-permute-start.10 = (bf16[4,152,128]{2,1,0:T(8,128)(2,1)S(1)}, bf16[4,152,128]{2,1,0:T(8,128)(2,1)S(1)}, u32[]{:S(2)}, u32[]{:S(2)}) collective-permute-start(bf16[4,152,128]{2,1,0:T(8,128)(2,1)S(1)} %get-tuple-element.51), channel_id=1, source_target_pairs={{0,4},{8,12},{16,20},{24,28},{4,0},{12,8},{20,16},{28,24},{1,5},{9... | collective-permute-start | bytes 466952 | tf_op jit(solution)/shard_map/ppermute | solution.py:499
  46.6 9.4 %collective-permute-start.11 = (bf16[4,152,128]{2,1,0:T(8,128)(2,1)S(1)}, bf16[4,152,128]{2,1,0:T(8,128)(2,1)S(1)}, u32[]{:S(2)}, u32[]{:S(2)}) collective-permute-start(bf16[4,152,128]{2,1,0:T(8,128)(2,1)S(1)} %get-tuple-element.52), channel_id=1, source_target_pairs={{4,8},{12,16},{20,24},{28,0},{8,4},{16,12},{24,20},{0,28},{5,9},{1... | collective-permute-start | bytes 466952 | tf_op jit(solution)/shard_map/ppermute | solution.py:499
  51.0 14.1 %collective-permute-start.12 = (bf16[4,152,128]{2,1,0:T(8,128)(2,1)S(1)}, bf16[4,152,128]{2,1,0:T(8,128)(2,1)S(1)}, u32[]{:S(2)}, u32[]{:S(2)}) collective-permute-start(bf16[4,152,128]{2,1,0:T(8,128)(2,1)S(1)} %get-tuple-element.54), channel_id=1, source_target_pairs={{0,1},{2,3},{1,0},{3,2},{4,5},{6,7},{5,4},{7,6},{8,9},{10,11},{9,8... | collective-permute-start | bytes 466952 | tf_op jit(solution)/shard_map/ppermute | solution.py:499
  53.5 11.6 %collective-permute-start.13 = (bf16[4,152,128]{2,1,0:T(8,128)(2,1)S(1)}, bf16[4,152,128]{2,1,0:T(8,128)(2,1)S(1)}, u32[]{:S(2)}, u32[]{:S(2)}) collective-permute-start(bf16[4,152,128]{2,1,0:T(8,128)(2,1)S(1)} %get-tuple-element.55), channel_id=1, source_target_pairs={{1,2},{2,1},{5,6},{6,5},{9,10},{10,9},{13,14},{14,13},{17,18},{18,... | collective-permute-start | bytes 466952 | tf_op jit(solution)/shard_map/ppermute | solution.py:499
  57.5 18.2 %collective-permute-start.14 = (bf16[4,152,128]{2,1,0:T(8,128)(2,1)S(1)}, bf16[4,152,128]{2,1,0:T(8,128)(2,1)S(1)}, u32[]{:S(2)}, u32[]{:S(2)}) collective-permute-start(bf16[4,152,128]{2,1,0:T(8,128)(2,1)S(1)} %get-tuple-element.58.refs_3_), channel_id=1, source_target_pairs={{0,32},{32,64},{64,96},{96,128},{128,160},{160,192},{192,224},{224... | collective-permute-start | bytes 466952 | tf_op jit(solution)/shard_map/ppermute | solution.py:494
  58.8 21.0 %collective-permute-start.19 = (bf16[4,152,128]{2,1,0:T(8,128)(2,1)S(1)}, bf16[4,152,128]{2,1,0:T(8,128)(2,1)S(1)}, u32[]{:S(2)}, u32[]{:S(2)}) collective-permute-start(bf16[4,152,128]{2,1,0:T(8,128)(2,1)S(1)} %get-tuple-element.64.refs_2_), channel_id=1, source_target_pairs={{32,0},{64,32},{96,64},{128,96},{160,128},{192,160},{224,192},{0,2... | collective-permute-start | bytes 466952 | tf_op jit(solution)/shard_map/ppermute | solution.py:494
  66.9 14.8 %collective-permute-start.15 = (bf16[8,152,128]{2,1,0:T(8,128)(2,1)S(1)}, bf16[8,152,128]{2,1,0:T(8,128)(2,1)S(1)}, u32[]{:S(2)}, u32[]{:S(2)}) collective-permute-start(bf16[8,152,128]{2,1,0:T(8,128)(2,1)S(1)} %get-tuple-element.60.refs_4_), channel_id=1, source_target_pairs={{0,1},{2,3},{1,0},{3,2},{4,5},{6,7},{5,4},{7,6},{8,9},{10,11},{9,8... | collective-permute-start | bytes 933896 | tf_op jit(solution)/shard_map/ppermute | solution.py:499
  67.0 14.7 %collective-permute-start.16 = (bf16[8,152,128]{2,1,0:T(8,128)(2,1)S(1)}, bf16[8,152,128]{2,1,0:T(8,128)(2,1)S(1)}, u32[]{:S(2)}, u32[]{:S(2)}) collective-permute-start(bf16[8,152,128]{2,1,0:T(8,128)(2,1)S(1)} %get-tuple-element.61.refs_5_), channel_id=1, source_target_pairs={{1,2},{2,1},{5,6},{6,5},{9,10},{10,9},{13,14},{14,13},{17,18},{18,... | collective-permute-start | bytes 933896 | tf_op jit(solution)/shard_map/ppermute | solution.py:499
  70.1 10.1 %collective-permute-start.17 = (bf16[4,152,128]{2,1,0:T(8,128)(2,1)S(1)}, bf16[4,152,128]{2,1,0:T(8,128)(2,1)S(1)}, u32[]{:S(2)}, u32[]{:S(2)}) collective-permute-start(bf16[4,152,128]{2,1,0:T(8,128)(2,1)S(1)} %get-tuple-element.62.refs_6_), channel_id=1, source_target_pairs={{0,4},{8,12},{16,20},{24,28},{4,0},{12,8},{20,16},{28,24},{1,5},{9... | collective-permute-start | bytes 466952 | tf_op jit(solution)/shard_map/ppermute | solution.py:499
  75.7 6.0 %collective-permute-start.18 = (bf16[4,152,128]{2,1,0:T(8,128)(2,1)S(1)}, bf16[4,152,128]{2,1,0:T(8,128)(2,1)S(1)}, u32[]{:S(2)}, u32[]{:S(2)}) collective-permute-start(bf16[4,152,128]{2,1,0:T(8,128)(2,1)S(1)} %get-tuple-element.63.refs_7_), channel_id=1, source_target_pairs={{4,8},{12,16},{20,24},{28,0},{8,4},{16,12},{24,20},{0,28},{5,9},{1... | collective-permute-start | bytes 466952 | tf_op jit(solution)/shard_map/ppermute | solution.py:499
